TPU v7x, 512 devices: a whole 4x4x16 slice. The times are simulated.
512 devices in a mesh: ctx: 64 (over z, x), head: 8 (over y, core).
Axes of the slice: x: 4, y: 4, z: 16, core: 2. Of those that a mesh axis runs over, the one named last changes fastest.
Arguments:
- frames: bfloat16 [8192, 1024], P('ctx'), may hold values from -6 to 6
- w_query: bfloat16 [1024, 1024], P(None, 'head'), may hold values from -0.1875 to 0.1875
- w_keys: bfloat16 [1024, 2048], P(None, 'head'), may hold values from -0.1875 to 0.1875
- w_values: bfloat16 [1024, 2048], P(None, 'head'), may hold values from -0.1875 to 0.1875
- w_beta: bfloat16 [1024, 16], P(None, 'head'), may hold values from -0.1875 to 0.1875
- beta_bias: float32 [16], P('head'), may hold values from -1 to 7
- cotangent: bfloat16 [8192, 1024], P('ctx', 'head'), may hold values from -6 to 6
Outputs:
- outputs: bfloat16 [8192, 1024], P('ctx', 'head')
- grad_frames: bfloat16 [8192, 1024], P('ctx', 'head')
- grad_query: float32 [1024, 1024], P(None, 'head')
- grad_keys: float32 [1024, 2048], P(None, 'head')
- grad_values: float32 [1024, 2048], P(None, 'head')
- grad_beta: float32 [1024, 16], P(None, 'head')
- grad_bias: float32 [16], P('head')
All inputs are finite; a program needn't handle non-finite values.
Results may differ from a plain program's by a relative error of at most 0.007.
Values sent between devices are 32-bit elements; how exact they have to be, the bound alone decides.
No kernel may reach another device: no remote copies, remote signals or barrier semaphores. Data moves between devices by JAX's collectives and lax.ppermute only.
A program may use at most 64 MiB of HBM per device.

v0:
```python
import jax
import jax.numpy as jnp
from jax import lax
from jax.sharding import PartitionSpec as P

DH = 128
BLOCK_ROWS = 128


HIGH = lax.Precision.HIGHEST


def prefix(part, axis, combine, identity, reverse):
    count = lax.axis_size(axis)
    place = lax.axis_index(axis)
    ahead = count - 1 - place if reverse else place
    gathered = jax.tree.map(lambda a: lax.all_gather(a, axis), part)
    state = jax.tree.map(lambda a, e: jnp.zeros_like(a) + jnp.asarray(e, a.dtype), part, identity)

    def one(turn, state):
        source = count - 1 - turn if reverse else turn
        return combine(
            state, jax.tree.map(lambda a: lax.dynamic_index_in_dim(a, source, 0, False), gathered)
        )

    return lax.fori_loop(0, ahead, one, state)


def normalize(rows):
    return rows * lax.rsqrt(jnp.sum(rows * rows, axis=-1, keepdims=True) + 1e-06)


def block_solve(keys_block, values_block, beta_block):
    size = keys_block.shape[0]
    gram = jnp.dot(keys_block, keys_block.T, precision=HIGH)
    order = jnp.arange(size)
    below = order[:, None] > order[None, :]
    system = jnp.eye(size, dtype=gram.dtype) + jnp.where(below, beta_block[:, None] * gram, 0.0)
    right = jnp.concatenate(
        [beta_block[:, None] * keys_block, beta_block[:, None] * values_block], axis=1
    )
    solved = jax.scipy.linalg.solve_triangular(system, right, lower=True, unit_diagonal=True)
    width = keys_block.shape[1]
    return (solved[:, :width], solved[:, width:])


def prepare_head(query_raw, keys_raw, values_raw, logits_raw, bias):
    count = query_raw.shape[0]
    width = query_raw.shape[1]
    blocks = 2 * count // BLOCK_ROWS
    queries = normalize(query_raw).reshape(blocks, BLOCK_ROWS // 2, width)
    keys = normalize(keys_raw.reshape(count, 2, width)).reshape(blocks, BLOCK_ROWS, width)
    values = values_raw.reshape(blocks, BLOCK_ROWS, width)
    betas = (2.0 * jax.nn.sigmoid(logits_raw + bias[None, :])).reshape(blocks, BLOCK_ROWS)
    return (queries, keys, values, betas)


@jax.checkpoint
def block_step(state, pieces):
    query_block, keys_block, values_block, beta_block = pieces
    weight_keys, weight_values = block_solve(keys_block, values_block, beta_block)
    fresh = weight_values - jnp.dot(weight_keys, state, precision=HIGH)
    scores = jnp.dot(query_block, keys_block.T, precision=HIGH)
    rows = jnp.arange(query_block.shape[0])
    cols = jnp.arange(keys_block.shape[0])
    seen = cols[None, :] <= 2 * rows[:, None] + 1
    output = jnp.dot(query_block, state, precision=HIGH) + jnp.dot(
        jnp.where(seen, scores, 0.0), fresh, precision=HIGH
    )
    return (state + jnp.dot(keys_block.T, fresh, precision=HIGH), output)


def summary_step(carry, pieces):
    transition, offset = carry
    query_block, keys_block, values_block, beta_block = pieces
    weight_keys, weight_values = block_solve(keys_block, values_block, beta_block)
    mapping = jnp.eye(keys_block.shape[1], dtype=jnp.float32) - jnp.dot(
        keys_block.T, weight_keys, precision=HIGH
    )
    transition = jnp.dot(mapping, transition, precision=HIGH)
    offset = jnp.dot(mapping, offset, precision=HIGH) + jnp.dot(
        keys_block.T, weight_values, precision=HIGH
    )
    return ((transition, offset), None)


def core_head(query_raw, keys_raw, values_raw, logits_raw, bias, state):
    queries, keys, values, betas = prepare_head(query_raw, keys_raw, values_raw, logits_raw, bias)
    final, outs = lax.scan(block_step, state, (queries, keys, values, betas))
    return (outs.reshape(query_raw.shape), final)


def summary_head(query_raw, keys_raw, values_raw, logits_raw, bias):
    pieces = prepare_head(query_raw, keys_raw, values_raw, logits_raw, bias)
    width = query_raw.shape[1]
    start = (jnp.eye(width, dtype=jnp.float32), jnp.zeros((width, width), jnp.float32))
    final, unused = lax.scan(summary_step, start, pieces)
    return final


def split_heads(query_raw, keys_raw, values_raw, logits_raw, bias, heads):
    count = query_raw.shape[0]
    query_h = jnp.transpose(query_raw.reshape(count, heads, -1), (1, 0, 2))
    keys_h = jnp.transpose(keys_raw.reshape(count, heads, -1), (1, 0, 2))
    values_h = jnp.transpose(values_raw.reshape(count, heads, -1), (1, 0, 2))
    logits_h = jnp.transpose(logits_raw.reshape(count, heads, 2), (1, 0, 2))
    return (query_h, keys_h, values_h, logits_h, bias.reshape(heads, 2))


def core_heads(query_raw, keys_raw, values_raw, logits_raw, bias, states):
    heads = states.shape[0]
    count = query_raw.shape[0]
    parts = split_heads(query_raw, keys_raw, values_raw, logits_raw, bias, heads)
    outs, finals = jax.vmap(core_head)(*parts, states)
    return (jnp.transpose(outs, (1, 0, 2)).reshape(count, -1), finals)


def compose(earlier, later):
    first_map, first_shift = earlier
    second_map, second_shift = later
    joined = jnp.einsum("hij,hjk->hik", second_map, first_map, precision=HIGH)
    shifted = jnp.einsum("hij,hjk->hik", second_map, first_shift, precision=HIGH) + second_shift
    return (joined, shifted)


def local(frames, w_query, w_keys, w_values, w_beta, beta_bias, cotangent):
    query_raw = jnp.dot(frames, w_query, preferred_element_type=jnp.float32)
    keys_raw = jnp.dot(frames, w_keys, preferred_element_type=jnp.float32)
    values_raw = jnp.dot(frames, w_values, preferred_element_type=jnp.float32)
    logits_raw = jnp.dot(frames, w_beta, preferred_element_type=jnp.float32)
    heads = w_query.shape[1] // DH
    identity_map = jnp.broadcast_to(jnp.eye(DH, dtype=jnp.float32), (heads, DH, DH))
    empty_state = jnp.zeros((heads, DH, DH), jnp.float32)
    parts = split_heads(query_raw, keys_raw, values_raw, logits_raw, beta_bias, heads)
    transition, offset = jax.vmap(summary_head)(*parts)
    entering = prefix((transition, offset), "ctx", compose, (identity_map, empty_state), False)[1]
    (outputs, finals), pull = jax.vjp(
        core_heads, query_raw, keys_raw, values_raw, logits_raw, beta_bias, entering
    )
    upstream = cotangent.astype(jnp.float32)
    own_adjoint = pull((upstream, jnp.zeros_like(finals)))[5]
    leaving = prefix(
        (jnp.swapaxes(transition, 1, 2), own_adjoint),
        "ctx",
        compose,
        (identity_map, empty_state),
        True,
    )[1]
    grads = pull((upstream, leaving))
    g_query = grads[0].astype(jnp.bfloat16)
    g_keys = grads[1].astype(jnp.bfloat16)
    g_values = grads[2].astype(jnp.bfloat16)
    g_logits = grads[3].astype(jnp.bfloat16)
    local_query = jnp.dot(frames.T, g_query, preferred_element_type=jnp.float32)
    local_keys = jnp.dot(frames.T, g_keys, preferred_element_type=jnp.float32)
    local_values = jnp.dot(frames.T, g_values, preferred_element_type=jnp.float32)
    local_beta = jnp.dot(frames.T, g_logits, preferred_element_type=jnp.float32)
    summed = lax.psum((local_query, local_keys, local_values, local_beta, grads[4]), "ctx")
    partial_frames = jnp.dot(g_query, w_query.T, preferred_element_type=jnp.float32)
    partial_frames = partial_frames + jnp.dot(g_keys, w_keys.T, preferred_element_type=jnp.float32)
    partial_frames = partial_frames + jnp.dot(
        g_values, w_values.T, preferred_element_type=jnp.float32
    )
    partial_frames = partial_frames + jnp.dot(
        g_logits, w_beta.T, preferred_element_type=jnp.float32
    )
    grad_frames = lax.psum_scatter(partial_frames, "head", scatter_dimension=1, tiled=True).astype(
        jnp.bfloat16
    )
    return (
        outputs.astype(jnp.bfloat16),
        grad_frames,
        summed[0],
        summed[1],
        summed[2],
        summed[3],
        summed[4],
    )


def solution(mesh):
    in_specs = (
        P("ctx", None),
        P(None, "head"),
        P(None, "head"),
        P(None, "head"),
        P(None, "head"),
        P("head"),
        P("ctx", "head"),
    )
    out_specs = (
        P("ctx", "head"),
        P("ctx", "head"),
        P(None, "head"),
        P(None, "head"),
        P(None, "head"),
        P(None, "head"),
        P("head"),
    )
    return jax.shard_map(local, mesh=mesh, in_specs=in_specs, out_specs=out_specs, check_vma=False)
```

profile of v0, /device:TPU:24, one launch (start us, length us, event | category | flops | bytes accessed | tf_op | source)
XLA Modules:
  0.0 1073.8 jit_solution(7057044294413810868)
XLA Ops:
  8.2 1.2 fusion.173
  9.9 1.1 broadcast_multiply_fusion.5
  11.3 1.4 fusion.174
  12.9 23.2 %while.91 = (s32[]{:T(128)}, f32[1,128,128]{2,1,0:T(8,128)S(1)}, f32[1,128,128]{2,1,0:T(8,128)S(1)}, f32[2,1,128,128]{3,2,1,0:T(8,128)S(1)}, f32[2,1,128]{2,1,0:...) while((s32[]{:T(128)}, f32[1,128,128]{2,1,0:T(8,128)S(1)}, f32[1,128,128]{2,1,0:T(8,128)S(1)}, ...), condition=%wide.region_2.4_spmd, body=%wide.region_1.3_spmd.sunk | while | flops 176472192 | bytes 1707105 | solution.py:97
  13.3 9.8 custom-call.30
  24.9 9.8 custom-call.30
  38.0 23.9 %while.96 = (s32[]{:T(128)}, f32[1,128,128]{1,2,0:T(8,128)S(1)}, f32[2,1,64,128]{3,2,1,0:T(8,128)S(1)}, f32[2,1,128,128]{3,2,1,0:T(8,128)S(1)}, f32[2,1,128,128]...) while((s32[]{:T(128)}, f32[1,128,128]{1,2,0:T(8,128)S(1)}, ...), condition=%wide.region_9.11_spmd.clone, body=%wide.region_8.10_spmd.clone.sunk | while | flops 163922176 | bytes 2231935 | solution.py:89
  38.4 9.8 custom-call.34
  50.3 9.8 custom-call.34
  63.6 124.2 %all-gather.9.cloned.1.call-done = f32[64,128,128]{2,1,0:T(8,128)} async-done(((f32[1,128,128]{2,1,0:T(8,128)}), f32[64,128,128]{2,1,0:T(8,128)}) %all-gather.9.cloned.1.call-update) | async-done | bytes 4194320 | tf_op jit(solution)/shard_map/all_gather | solution.py:17
  187.8 144.7 %all-gather.11.cloned.1.call-done = f32[64,128,128]{2,1,0:T(8,128)} async-done(((f32[1,128,128]{2,1,0:T(8,128)}), f32[64,128,128]{2,1,0:T(8,128)}) %all-gather.11.cloned.1.call-update) | async-done | bytes 4194320 | tf_op jit(solution)/shard_map/all_gather | solution.py:17
  332.5 23.5 %while.95 = (s32[]{:T(128)}, f32[1,128,128]{2,1,0:T(8,128)S(1)}, bf16[2,1,64,128]{3,2,1,0:T(8,128)(2,1)S(1)}, f32[2,1,128,128]{3,2,1,0:T(8,128)S(1)}, f32[2,1,12...) while((s32[]{:T(128)}, f32[1,128,128]{2,1,0:T(8,128)S(1)}, ...), condition=%wide.region_7.9_spmd.clone, body=%wide.region_6.8_spmd.clone.sunk | while | flops 163881088 | bytes 1806977 | solution.py:89
  332.9 9.8 custom-call.33
  344.6 9.8 custom-call.33
  356.0 121.1 %all-gather.15.cloned.1.call-done = f32[64,128,128]{2,1,0:T(8,128)} async-done(((f32[1,128,128]{2,1,0:T(8,128)}), f32[64,128,128]{2,1,0:T(8,128)}) %all-gather.15.cloned.1.call-update) | async-done | bytes 4194320 | tf_op jit(solution)/shard_map/all_gather | solution.py:17
  477.0 144.6 %all-gather.13.cloned.1.call-done = f32[64,128,128]{2,1,0:T(8,128)} async-done(((f32[1,128,128]{2,1,0:T(8,128)}), f32[64,128,128]{2,1,0:T(8,128)}) %all-gather.13.cloned.1.call-update) | async-done | bytes 4194320 | tf_op jit(solution)/shard_map/all_gather | solution.py:17
  621.6 71.2 %while.93 = (s32[]{:T(128)}, f32[1,128,128]{2,1,0:T(8,128)S(1)}, s32[]{:T(128)}, f32[64,1,128,128]{3,2,1,0:T(8,128)}, f32[64,1,128,128]{3,2,1,0:T(8,128)}, /*index=5*/s32[]{:T(128)}, s32[]{:T(128)}, s32[]{:T(128)}, s32[]{:T(128)}) while((s32[]{:T(128)}, f32[1,128,128]{2,1,0:T(8,128)S(1)}, s32[]{:T(128)}, f32[64,1,128,128]{3,2,1,0:T(8,128)}, ...), condition=%wide.region_11.13_spmd, body=%wide.region_10.12_spmd.sunk | while | flops 25182212 | bytes 394379 | solution.py:26
  621.6 1.1 fusion.325
  622.7 1.1 fusion.325
  693.0 51.2 %while.94 = (s32[]{:T(128)}, f32[1,128,128]{1,2,0:T(8,128)S(1)}, f32[2,1,64,128]{3,2,1,0:T(8,128)S(1)}, f32[2,1,128,128]{3,2,0,1:T(8,128)S(1)}, bf16[2,1,128,128...) while((s32[]{:T(128)}, f32[1,128,128]{1,2,0:T(8,128)S(1)}, ...), condition=%wide.region_16.18_spmd, body=%wide.region_12.17_spmd.sunk | while | flops 466509952 | bytes 6073261 | solution.py:89
  693.7 9.8 custom-call.31
  704.9 9.8 custom-call.32
  719.3 9.8 custom-call.31
  730.5 9.8 custom-call.32
  746.5 1.1 fusion.157
  748.7 1.3 convolution_bitcast_fusion.18
  750.0 1.3 convolution_bitcast_fusion.17
  751.6 143.5 %all-reduce.2 = (f32[1024,2]{0,1:T(2,128)}, f32[2]{0:T(128)}) all-reduce(f32[1024,2]{0,1:T(2,128)S(1)} %convolution_bitcast_fusion.20, f32[2]{0:T(128)S(1)} %fusion.171), channel_id=1, replica_groups=mesh['ctx'=64,'head'=8] {'ctx'}, use_global_device_ids=true, to_apply=%region_23.25 | all-reduce | flops 2050 | bytes 16400 | tf_op jit(solution)/shard_map/psum | solution.py:158
  895.1 1.5 convert_element_type.71
  896.5 164.3 %all-reduce.6.cloned.1.call-done = (f32[1024,128]{0,1:T(8,128)}, f32[1024,256]{0,1:T(8,128)}, f32[1024,256]{0,1:T(8,128)}) async-done(((f32[1024,128]{0,1:T(8,128)}, f32[1024,256]{0,1:T(8,128)}, f32[1024,256]{0,1:T(8,128)}), (f32[1024,128]{0,1:T(8,128)}, f32[1024,256]{0,1:T(8,128)}, f32[1024,256]{0,1:T(8,128)})) %all-reduce.6.cloned.1.call-update) | async-done | bytes 2621456 | tf_op jit(solution)/shard_map/psum | solution.py:158
  1060.9 2.6 copy.110
  1063.5 2.5 copy.111
  (349 shorter events, 98.8 us)
Async XLA Ops:
  7.2 1.0 copy-start
  7.2 180.6 %all-gather.9.cloned.1.call-start = ((), (), s32[]{:S(2)}) async-start(), calls=%async_computation.2 | async-start | bytes 4259840 | tf_op jit(solution)/shard_map/all_gather | solution.py:17
  12.8 24.7 %copy-start.8 = (bf16[128,128]{1,0:T(8,128)(2,1)S(1)}, bf16[128,128]{1,0:T(8,128)(2,1)}, u32[]{:S(2)}) copy-start(bf16[128,128]{1,0:T(8,128)(2,1)} %param.27) | copy-start | bytes 98308
  12.8 24.7 %copy-start.1 = (bf16[128,1024]{1,0:T(8,128)(2,1)S(1)}, bf16[128,1024]{1,0:T(8,128)(2,1)}, u32[]{:S(2)}) copy-start(bf16[128,1024]{1,0:T(8,128)(2,1)} %param.21) | copy-start | bytes 786436
  12.9 24.7 %copy-start.6 = (bf16[1024,128]{1,0:T(8,128)(2,1)S(1)}, bf16[1024,128]{1,0:T(8,128)(2,1)}, u32[]{:S(2)}) copy-start(bf16[1024,128]{1,0:T(8,128)(2,1)} %param.22) | copy-start | bytes 786436
  36.1 0.6 copy-start.2
  36.1 0.7 copy-start.4
  36.7 295.8 %all-gather.11.cloned.1.call-start = ((), (), s32[]{:S(2)}) async-start(), calls=%async_computation.3 | async-start | bytes 4259840 | tf_op jit(solution)/shard_map/all_gather | solution.py:17
  37.5 439.6 %all-gather.15.cloned.1.call-start = ((), (), s32[]{:S(2)}) async-start(), calls=%async_computation.5 | async-start | bytes 4259840 | tf_op jit(solution)/shard_map/all_gather | solution.py:17
  38.0 24.7 %copy-start.3 = (f32[1,128,128]{2,1,0:T(8,128)S(1)}, f32[1,128,128]{2,1,0:T(8,128)}, u32[]{:S(2)}) copy-start(f32[1,128,128]{2,1,0:T(8,128)} %copy-done.2) | copy-start | bytes 196612
  62.7 559.0 %all-gather.13.cloned.1.call-start = ((), (), s32[]{:S(2)}) async-start(), calls=%async_computation.4 | async-start | bytes 4259840 | tf_op jit(solution)/shard_map/all_gather | solution.py:17
  63.5 831.6 %reduce-scatter.2.cloned.1.call-start = ((), (), s32[]{:S(2)}) async-start(), calls=%async_computation.1 | async-start | bytes 589824 | tf_op jit(solution)/shard_map/reduce_scatter | solution.py:167
  356.0 337.1 %copy-start.9 = (bf16[2,1,64,128]{3,2,1,0:T(8,128)(2,1)}, bf16[2,1,64,128]{3,2,1,0:T(8,128)(2,1)S(1)}, u32[]{:S(2)}) copy-start(bf16[2,1,64,128]{3,2,1,0:T(8,128)(2,1)S(1)} %get-tuple-element.665) | copy-start | bytes 98308
  744.2 2.0 copy-start.10
  744.2 2.2 copy-start.5
  747.6 313.3 %all-reduce.6.cloned.1.call-start = ((), (), s32[]{:S(2)}) async-start(), calls=%async_computation.6 | async-start | bytes 5242880 | tf_op jit(solution)/shard_map/psum | solution.py:158
  1060.9 5.1 copy-start.7
Sparse Core Ops, SparseCore 0:
  36.8 150.8 all-gather.8
  191.3 141.1 all-gather.10
  335.4 141.5 all-gather.14
  480.4 141.1 all-gather.12
  747.7 24.3 reduce-scatter.1
  776.6 284.2 all-reduce.5
where the time goes:
time: 1080 us; the launch traced here: 1070 us
  waiting for transfers between devices  700 us (65%)
  blocking collectives  143 us (13%)
  other arithmetic  102 us (9%)
  matrix products  98.4 us (9%)
  between operations  14.6 us (1%)
  local copies, waits for them, and re-layouts  11.9 us (1%)
    all_gather x4, waiting for transfers between devices, prefix(): gathered = jax.tree.map(lambda a: lax.all_gather(a, axis), part)  535 us
    psum x1, waiting for transfers between devices, local(): lax.psum((local_query, local_keys, local_values, local_beta, grads[4]), '...  164 us
    psum x1, blocking collectives, local(): lax.psum((local_query, local_keys, local_values, local_beta, grads[4]), '...  143 us
    another operation x22, other arithmetic, block_solve(): jax.scipy.linalg.solve_triangular(system, right, lower=True, unit_diagona...  98.5 us
    dot_general x63, matrix products, compose(): jnp.einsum('hij,hjk->hik', second_map, first_shift, precision=HIGH)  68.1 us
  transfers between devices with their start and end apart: 6, of which 5 were waited for; matrix products, arithmetic and copies ran while one was open for 5% of the time, Pallas kernels for 0%

commit v1 on v0

v1 whole, which is shorter than its diff:
```python
import jax
import jax.numpy as jnp
from jax import lax
from jax.experimental import pallas as pl
from jax.experimental.pallas import tpu as pltpu
from jax.sharding import Mesh, PartitionSpec as P

DH = 128
ROWS = 128
HALF = 64
REFL = 256
X_SIZE = 4
Y_SIZE = 4
EPS = 1e-06
VMEM_BYTES = 40 * 1024 * 1024


def halves(a):
    high = a.astype(jnp.bfloat16)
    return high, (a - high.astype(jnp.float32)).astype(jnp.bfloat16)


def dot(a, b, ca=1, cb=0):
    return lax.dot_general(a, b, (((ca,), (cb,)), ((), ())), preferred_element_type=jnp.float32)


def mm(a, b, ca=1, cb=0):
    return mm_halves(halves(a), halves(b), ca, cb)


def mm_halves(a, b, ca=1, cb=0):
    return dot(a[0], b[0], ca, cb) + (dot(a[0], b[1], ca, cb) + dot(a[1], b[0], ca, cb))


def mix(first, second):
    return jnp.concatenate([first[:HALF], second[:HALF], first[HALF:], second[HALF:]], axis=0)


def unmix(rows):
    first = jnp.concatenate([rows[:HALF], rows[ROWS : ROWS + HALF]], axis=0)
    second = jnp.concatenate([rows[HALF:ROWS], rows[ROWS + HALF :]], axis=0)
    return first, second


def place(shape, axis):
    row = lax.broadcasted_iota(jnp.int32, shape, axis)
    return (row & ROWS) + 2 * (row & (HALF - 1)) + ((row >> 6) & 1)


def seen_mask():
    frame = lax.broadcasted_iota(jnp.int32, (ROWS, REFL), 0)
    return (place((ROWS, REFL), 1) >> 1) <= frame


def prepare_kernel(
    frames_ref, wq_ref, wk_ref, wv_ref, wb_ref, bias_ref, cot_ref,
    send_ref, q_ref, k_ref, v_ref, w_ref, u_ref, z_ref, yg_ref, qt_ref, pu_ref, cols_ref, wide_ref,
):
    frames = frames_ref[...]
    wide_ref[...] = frames.astype(jnp.float32)
    q_raw = dot(frames, wq_ref[...])
    k_raw = dot(frames, wk_ref[...])
    v_raw = dot(frames, wv_ref[...])
    logits = dot(frames, wb_ref[...]) + bias_ref[...]
    rq = lax.rsqrt(jnp.sum(q_raw * q_raw, axis=1, keepdims=True) + EPS)
    q = q_raw * rq
    keys = mix(k_raw[:, :DH], k_raw[:, DH:])
    rk = lax.rsqrt(jnp.sum(keys * keys, axis=1, keepdims=True) + EPS)
    k = keys * rk
    v = mix(v_raw[:, :DH], v_raw[:, DH:])
    strength = 2.0 * jax.nn.sigmoid(logits)
    beta = mix(strength[:, 0:1], strength[:, 1:2])
    q_ref[...] = q
    k_ref[...] = k
    v_ref[...] = v
    lane = lax.broadcasted_iota(jnp.int32, (REFL, DH), 1)
    rq_long = jnp.concatenate([rq, rq], axis=0)
    cols_ref[...] = jnp.where(lane == 0, beta, jnp.where(lane == 1, rk, rq_long))

    gram = mm(k, k, 1, 1)
    system = beta * gram
    row, col = place((ROWS, ROWS), 0), place((ROWS, ROWS), 1)
    parts = [system[:ROWS, :ROWS], system[ROWS:, ROWS:]]
    pair = ((row >> 1) == (col >> 1)) & (row > col)
    eye = jnp.where(row == col, 1.0, 0.0)
    inverse = [eye - jnp.where(pair, part, 0.0) for part in parts]
    for level in range(1, 7):
        lower = ((row >> (level + 1)) == (col >> (level + 1))) & ((row >> level) > (col >> level))
        inner = [mm(jnp.where(lower, part, 0.0), inv) for part, inv in zip(parts, inverse)]
        inverse = [inv - mm(inv, mid) for inv, mid in zip(inverse, inner)]
    corner = -mm(inverse[1], mm(system[ROWS:, :ROWS], inverse[0]))
    zero = jnp.zeros((ROWS, ROWS), jnp.float32)
    inverse = jnp.concatenate(
        [
            jnp.concatenate([inverse[0], zero], axis=1),
            jnp.concatenate([corner, inverse[1]], axis=1),
        ],
        axis=0,
    )
    wu = mm(inverse, jnp.concatenate([beta * k, beta * v], axis=1))
    w, u = wu[:, :DH], wu[:, DH:]
    w_ref[...] = w
    u_ref[...] = u
    kwu = mm(k, wu, 0, 0)
    scores = jnp.where(seen_mask(), mm(q, k, 1, 1), 0.0)
    pwu = mm(scores, wu)
    qt = q - pwu[:, :DH]
    qt_ref[...] = qt
    pu_ref[...] = pwu[:, DH:]
    cot = cot_ref[...].astype(jnp.float32)
    send_ref[0] = eye_like() - kwu[:, :DH]
    send_ref[1] = kwu[:, DH:]
    send_ref[2] = mm(cot, qt, 0, 0)
    pg = mm(scores, cot, 0, 0)
    zy = mm(inverse, jnp.concatenate([k, pg], axis=1), 0, 0)
    z_ref[...] = zy[:, :DH]
    yg_ref[...] = zy[:, DH:]


def eye_like():
    row = lax.broadcasted_iota(jnp.int32, (DH, DH), 0)
    col = lax.broadcasted_iota(jnp.int32, (DH, DH), 1)
    return jnp.where(row == col, 1.0, 0.0)


def group_kernel(place_ref, parts_ref, total_ref, before_ref, after_ref):
    me = place_ref[0]
    count = parts_ref.shape[0]
    maps = [halves(parts_ref[i, 0]) for i in range(count)]
    ahead = [jnp.concatenate([parts_ref[0, 0], parts_ref[0, 1]], axis=1)]
    for i in range(1, count):
        moved = mm_halves(maps[i], halves(ahead[-1]))
        ahead.append(jnp.concatenate([moved[:, :DH], moved[:, DH:] + parts_ref[i, 1]], axis=1))
    last = count - 1
    behind = [jnp.concatenate([parts_ref[last, 0], parts_ref[last, 2]], axis=0)]
    for i in range(last - 1, -1, -1):
        moved = mm_halves(halves(behind[-1]), maps[i])
        behind.append(jnp.concatenate([moved[:DH], moved[DH:] + parts_ref[i, 2]], axis=0))
    total_ref[0] = ahead[last][:, :DH]
    total_ref[1] = ahead[last][:, DH:]
    total_ref[2] = behind[last][DH:]
    eye, zero = eye_like(), jnp.zeros((DH, DH), jnp.float32)
    before = jnp.concatenate([eye, zero], axis=1)
    after = jnp.concatenate([eye, zero], axis=0)
    for i in range(last):
        before = jnp.where(me == i + 1, ahead[i], before)
        after = jnp.where(me == last - 1 - i, behind[i], after)
    before_ref[0] = before[:, :DH]
    before_ref[1] = before[:, DH:]
    after_ref[0] = after[:DH]
    after_ref[1] = after[DH:]


def group_scan(parts, place):
    return pl.pallas_call(
        group_kernel,
        out_shape=(f32(3, DH, DH), f32(2, DH, DH), f32(2, DH, DH)),
        in_specs=[
            pl.BlockSpec(memory_space=pltpu.SMEM),
            pl.BlockSpec(memory_space=pltpu.VMEM),
        ],
        compiler_params=pltpu.CompilerParams(vmem_limit_bytes=VMEM_BYTES),
        name="group_scan",
    )(place, parts)


def finish_kernel(
    place_ref, far_ref, near_before_ref, near_after_ref, own_before_ref, own_after_ref,
    frames_ref, wq_ref, wk_ref, wv_ref, wb_ref, cot_ref,
    q_ref, k_ref, v_ref, w_ref, u_ref, z_ref, yg_ref, qt_ref, pu_ref, cols_ref,
    out_ref, pieces_ref, part_ref,
):
    me = place_ref[0]
    count = far_ref.shape[1]

    def far(group, which):
        return jnp.concatenate([far_ref[i, group, which] for i in range(far_ref.shape[0])], axis=0)

    entering = jnp.where(me > 0, far(0, 1), 0.0)
    for i in range(1, count - 1):
        entering = jnp.where(me > i, mm(far(i, 0), entering) + far(i, 1), entering)
    leaving = jnp.where(me < count - 1, far(count - 1, 2), 0.0)
    for i in range(count - 2, 0, -1):
        leaving = jnp.where(me < i, mm(leaving, far(i, 0)) + far(i, 2), leaving)
    for before_ref, after_ref in ((near_before_ref, near_after_ref), (own_before_ref, own_after_ref)):
        entering = mm(before_ref[0], entering) + before_ref[1]
        leaving = mm(leaving, after_ref[0]) + after_ref[1]
    q, k, v = q_ref[...], k_ref[...], v_ref[...]
    cot = cot_ref[...].astype(jnp.float32)
    beta, rk, rq = cols_ref[:, 0:1], cols_ref[:, 1:2], cols_ref[:ROWS, 2:3]
    out_ref[...] = (mm(qt_ref[...], entering) + pu_ref[...]).astype(jnp.bfloat16)
    fresh = u_ref[...] - mm(w_ref[...], entering)
    y = yg_ref[...] + mm(z_ref[...], leaving, 1, 1)
    gram = mm(k, k, 1, 1)
    row, col = place((REFL, REFL), 0), place((REFL, REFL), 1)
    d_system = jnp.where(row > col, -mm(y, fresh, 1, 1), 0.0)
    d_scores = jnp.where(seen_mask(), mm(cot, fresh, 1, 1), 0.0)
    d_query = mm(cot, entering, 1, 1) + mm(d_scores, k)
    error = v - mm(k, entering)
    d_beta = jnp.sum(y * error, axis=1, keepdims=True) + jnp.sum(
        d_system * gram, axis=1, keepdims=True
    )
    by = beta * y
    d_gram = beta * d_system
    d_keys = (
        mm(d_scores, q, 0, 0)
        + mm(fresh, leaving)
        - mm(by, entering, 1, 1)
        + mm(d_gram, k)
        + mm(d_gram, k, 0, 0)
    )
    d_query = rq * (d_query - q * jnp.sum(d_query * q, axis=1, keepdims=True))
    d_keys = rk * (d_keys - k * jnp.sum(d_keys * k, axis=1, keepdims=True))
    d_logits = d_beta * beta * (1.0 - 0.5 * beta)
    l_first, l_second = unmix(d_logits)
    lane2 = lax.broadcasted_iota(jnp.int32, (ROWS, 2), 1)
    g_logits_f32 = jnp.where(lane2 == 0, l_first, l_second)
    g_query = d_query.astype(jnp.bfloat16)
    k_first, k_second = unmix(d_keys)
    v_first, v_second = unmix(by)
    g_keys = jnp.concatenate([k_first, k_second], axis=1).astype(jnp.bfloat16)
    g_values = jnp.concatenate([v_first, v_second], axis=1).astype(jnp.bfloat16)
    g_logits = g_logits_f32.astype(jnp.bfloat16)
    frames = frames_ref[...]
    wide = jnp.float32
    tiles = [
        g_query.astype(wide),
        g_keys[:, :DH].astype(wide),
        g_keys[:, DH:].astype(wide),
        g_values[:, :DH].astype(wide),
    ]
    shared = g_values[:, DH:].astype(wide)
    beta_rows = dot(g_logits, frames, 0, 0)
    bias_row = jnp.sum(g_logits_f32, axis=0, keepdims=True)
    bias_lanes = jnp.where(
        lax.broadcasted_iota(jnp.int32, (1, DH), 1) == 0, bias_row[:, 0:1], bias_row[:, 1:2]
    )
    for i in range(4):
        pieces_ref[i, :ROWS] = tiles[i]
        pieces_ref[i, ROWS : 2 * ROWS] = shared
        span = beta_rows[:, 256 * i : 256 * i + 256]
        pieces_ref[i, 2 * ROWS :] = jnp.concatenate(
            [span[:, :DH], span[:, DH:], bias_lanes, jnp.zeros((3, DH), wide)], axis=0
        )
    part_ref[...] = (
        dot(g_query, wq_ref[...], 1, 1)
        + dot(g_keys, wk_ref[...], 1, 1)
        + dot(g_values, wv_ref[...], 1, 1)
        + dot(g_logits, wb_ref[...], 1, 1)
    )


def f32(*shape):
    return jax.ShapeDtypeStruct(shape, jnp.float32)


def prepare(*args):
    wide = f32(REFL, DH)
    narrow = f32(ROWS, DH)
    return pl.pallas_call(
        prepare_kernel,
        out_shape=(
            f32(3, DH, DH), narrow, wide, wide, wide, wide, wide, wide, narrow, narrow, wide,
            f32(ROWS, 1024),
        ),
        compiler_params=pltpu.CompilerParams(vmem_limit_bytes=VMEM_BYTES),
        name="prepare",
    )(*args)


def finish(*args):
    return pl.pallas_call(
        finish_kernel,
        out_shape=(
            jax.ShapeDtypeStruct((ROWS, DH), jnp.bfloat16),
            f32(4, 264, DH),
            f32(ROWS, 1024),
        ),
        in_specs=[pl.BlockSpec(memory_space=pltpu.SMEM)]
        + [pl.BlockSpec(memory_space=pltpu.VMEM)] * (len(args) - 1),
        compiler_params=pltpu.CompilerParams(vmem_limit_bytes=VMEM_BYTES),
        name="finish",
    )(*args)


def weigh_kernel(place_ref, frames_ref, pieces_ref, sums_ref):
    me = place_ref[0]
    total = jnp.zeros((1024, DH), jnp.float32)
    corner = jnp.zeros((256, DH), jnp.float32)
    extra = jnp.zeros((8, DH), jnp.float32)
    for i in range(4):
        piece = pieces_ref[i, : 2 * ROWS].astype(jnp.bfloat16)
        frames = frames_ref[i].astype(jnp.bfloat16)
        total = total + dot(frames, piece[:ROWS], 0, 0)
        quarter = frames_ref[i, :, pl.ds(pl.multiple_of(me * 256, 256), 256)].astype(jnp.bfloat16)
        corner = corner + dot(quarter, piece[ROWS:], 0, 0)
        extra = extra + pieces_ref[i, 2 * ROWS :]
    for j in range(4):
        if j < 3:
            sums_ref[j, :320] = total[320 * j : 320 * j + 320]
        else:
            sums_ref[j, :64] = total[960:]
            sums_ref[j, 64:320] = corner
        sums_ref[j, 320:] = extra


def weigh(place, frames, pieces):
    return pl.pallas_call(
        weigh_kernel,
        out_shape=f32(4, 328, DH),
        in_specs=[pl.BlockSpec(memory_space=pltpu.SMEM)]
        + [pl.BlockSpec(memory_space=pltpu.VMEM)] * 2,
        compiler_params=pltpu.CompilerParams(vmem_limit_bytes=VMEM_BYTES),
        name="weigh",
    )(place, frames, pieces)


def spread(a, axis):
    return lax.all_to_all(jnp.broadcast_to(a[None], (4, *a.shape)), axis, 0, 0, tiled=True)


def trade(a, axis):
    return lax.all_to_all(a, axis, 0, 0, tiled=True)


def local(frames, w_query, w_keys, w_values, w_beta, beta_bias, cotangent):
    at_x = lax.axis_index("x")[None]
    at_low = lax.axis_index("zl")[None]
    at_high = lax.axis_index("zh")[None]
    weights = (w_query, w_keys, w_values, w_beta)
    own, *kept, wide_frames = prepare(frames, *weights, beta_bias[None], cotangent)
    total, own_before, own_after = group_scan(spread(own, "x"), at_x)
    total, near_before, near_after = group_scan(spread(total, "zl"), at_low)
    quarter = lax.dynamic_slice_in_dim(total, lax.axis_index("x") * 32, 32, axis=1)
    far = spread(spread(quarter, "zh"), "x")
    group_frames = lax.all_gather(wide_frames, "x")
    outputs, pieces, partial = finish(
        at_high, far, near_before, near_after, own_before, own_after,
        frames, *weights, cotangent, *kept,
    )
    grad_frames = lax.psum_scatter(partial, ("y", "core"), scatter_dimension=1, tiled=True).astype(
        jnp.bfloat16
    )
    sums = weigh(at_x, group_frames, trade(pieces, "x"))
    part = jnp.sum(trade(sums, "zl"), axis=0)
    extra = part[320:]
    part = jnp.concatenate(
        [part[:320].reshape(4, 80, DH), jnp.broadcast_to(extra[None], (4, 8, DH))], axis=1
    )
    part = jnp.sum(trade(part, "zh"), axis=0)
    extra = part[80:]
    part = spread(part[:80], "zh")
    part = spread(part.reshape(320, DH), "zl").reshape(1280, DH)
    whole = spread(jnp.concatenate([part, extra], axis=0), "x")
    grad_query = whole[0, :1024]
    grad_keys = jnp.concatenate([whole[1, :1024], whole[2, :1024]], axis=1)
    grad_values = jnp.concatenate(
        [whole[3, :1024], whole[:, 1024:1280].reshape(1024, DH)], axis=1
    )
    beta_rows = whole[:, 1280:1284].reshape(4, 2, 2, DH)
    grad_beta = jnp.transpose(beta_rows, (0, 1, 3, 2)).reshape(1024, 2)
    grad_bias = whole[0, 1284, :2]
    return (outputs, grad_frames, grad_query, grad_keys, grad_values, grad_beta, grad_bias)


def solution(mesh):
    fine = Mesh(mesh.devices.reshape(4, 4, 4, 4, 2), ("zh", "zl", "x", "y", "core"))
    ctx, head = ("zh", "zl", "x"), ("y", "core")
    in_specs = (
        P(ctx, None),
        P(None, head),
        P(None, head),
        P(None, head),
        P(None, head),
        P(head),
        P(ctx, head),
    )
    out_specs = (
        P(ctx, head),
        P(ctx, head),
        P(None, head),
        P(None, head),
        P(None, head),
        P(None, head),
        P(head),
    )
    return jax.shard_map(local, mesh=fine, in_specs=in_specs, out_specs=out_specs, check_vma=False)
```

time: 1080 us -> 263 us (0.24)
  waiting for transfers between devices: 700 us -> 96.3 us
  other arithmetic: 102 us -> 3.01 us
  matrix products: 98.4 us -> 0 us
  blocking collectives: 143 us -> 83.4 us
  starting transfers between devices: 0.24 us -> 24.4 us
  local copies, waits for them, and re-layouts: 11.9 us -> 25.5 us
    all_gather x4 -> x1, waiting for transfers between devices: 535 us -> 0.02 us  [local(): group_frames = lax.all_gather(wide_frames, 'x')]
    psum x1 -> x0, waiting for transfers between devices: 164 us -> none  [local(): lax.psum((local_query, local_keys, local_values, local_beta, grads[4]), '...]
    psum x1 -> x0, blocking collectives: 143 us -> none  [local(): lax.psum((local_query, local_keys, local_values, local_beta, grads[4]), '...]
    another operation x25 -> x0, other arithmetic: 98.5 us -> none  [the longest x22 98.5 us: block_solve(): jax.scipy.linalg.solve_triangular(system, right, lower=True, unit_diagona...]
    dot_general x141 -> x0, matrix products: 94.7 us -> none  [the longest x63 68.1 us: compose(): jnp.einsum('hij,hjk->hik', second_map, first_shift, precision=HIGH)]
    all_to_all x0 -> x4, blocking collectives: none -> 83.4 us  [the longest x2 45.8 us: spread(): lax.all_to_all(jnp.broadcast_to(a[None], (4, *a.shape)), axis, 0, 0, tile...]
    all_to_all x0 -> x6, waiting for transfers between devices: none -> 62 us  [the longest x5 53.9 us: spread(): lax.all_to_all(jnp.broadcast_to(a[None], (4, *a.shape)), axis, 0, 0, tile...]
    reduce_scatter x1, waiting for transfers between devices: 0.01 us -> 33.1 us  [local(): lax.psum_scatter(partial, ('y', 'core'), scatter_dimension=1, tiled=True)]
  transfers between devices with their start and end apart: 6 -> 8, of which waited for: 5 -> 6; matrix products, arithmetic and copies ran while one was open for 5% -> 1% of each run, Pallas kernels for 0% -> 2%
where the time goes in v1:
time: 263 us; the launch traced here: 259 us
  waiting for transfers between devices  96.3 us (37%)
  blocking collectives  83.4 us (32%)
  local copies, waits for them, and re-layouts  25.5 us (10%)
  starting transfers between devices  24.4 us (9%)
  between operations  15.7 us (6%)
  Pallas kernels  10.6 us (4%)
  other arithmetic  3.01 us (1%)
    all_to_all x5, waiting for transfers between devices, spread(): lax.all_to_all(jnp.broadcast_to(a[None], (4, *a.shape)), axis, 0, 0, tile...  53.9 us
    all_to_all x2, blocking collectives, spread(): lax.all_to_all(jnp.broadcast_to(a[None], (4, *a.shape)), axis, 0, 0, tile...  45.8 us
    all_to_all x2, blocking collectives, trade(): return lax.all_to_all(a, axis, 0, 0, tiled=True)  37.6 us
    reduce_scatter x1, waiting for transfers between devices, local(): lax.psum_scatter(partial, ('y', 'core'), scatter_dimension=1, tiled=True)  33.1 us
    all_to_all x5, starting transfers between devices, spread(): lax.all_to_all(jnp.broadcast_to(a[None], (4, *a.shape)), axis, 0, 0, tile...  20.8 us
    unnamed x53, local copies, waits for them, and re-layouts  17.9 us
    all_to_all x1, waiting for transfers between devices, trade(): return lax.all_to_all(a, axis, 0, 0, tiled=True)  8.11 us
    broadcast_in_dim x7, local copies, waits for them, and re-layouts, spread(): jnp.broadcast_to(a[None], (4, *a.shape))  5.43 us
  transfers between devices with their start and end apart: 8, of which 6 were waited for; matrix products, arithmetic and copies ran while one was open for 1% of the time, Pallas kernels for 2%

profile of v1, /device:TPU:24, one launch (start us, length us, event | category | flops | bytes accessed | tf_op | source)
XLA Modules:
  0.0 258.9 jit_solution(913111950972582677)
XLA Ops:
  8.9 1.0 copy-done.1
  9.9 1.0 copy-done.3
  11.0 0.9 copy-done.5
  11.9 0.9 copy-done.7
  14.3 4.9 %prepare.1 = (f32[3,128,128]{2,1,0:T(8,128)S(1)}, f32[128,128]{1,0:T(8,128)S(1)}, f32[256,128]{1,0:T(8,128)S(1)}, f32[256,128]{1,0:T(8,128)S(1)}, f32[256,128]{1...) custom-call(bf16[128,1024]{1,0:T(8,128)(2,1)S(1)} %copy-done.5, ...), custom_call_target="tpu_custom_call" | custom-call | tf_op jit(solution)/shard_map/prepare/pallas_call | solution.py:260
  21.1 0.9 broadcast_in_dim.30
  22.0 4.3 %all-to-all-start = ((f32[4,3,128,128]{3,2,1,0:T(8,128)}), f32[4,3,128,128]{3,2,1,0:T(8,128)S(1)}, u32[]{:S(2)}, u32[]{:S(2)}) async-start(f32[4,3,128,128]{3,2,1,0:T(8,128)} %broadcast_in_dim.30), calls=%async_computation | async-start | bytes 1572864 | tf_op jit(solution)/shard_map/all_to_all | solution.py:319
  26.3 12.3 %all-to-all-done.parts_ref = f32[4,3,128,128]{3,2,1,0:T(8,128)S(1)} async-done(((f32[4,3,128,128]{3,2,1,0:T(8,128)}), f32[4,3,128,128]{3,2,1,0:T(8,128)S(1)}, u32[]{:S(2)}, u32[]{:S(2)}) %all-to-all-start) | async-done | bytes 786464 | tf_op jit(solution)/shard_map/all_to_all | solution.py:319
  38.6 1.0 group_scan.2
  40.2 0.9 broadcast_in_dim.31
  41.2 5.9 %all-to-all-start.1 = ((f32[4,3,128,128]{3,2,1,0:T(8,128)}), f32[4,3,128,128]{3,2,1,0:T(8,128)S(1)}, u32[]{:S(2)}, u32[]{:S(2)}) async-start(f32[4,3,128,128]{3,2,1,0:T(8,128)} %broadcast_in_dim.31), calls=%async_computation.1 | async-start | bytes 1572864 | tf_op jit(solution)/shard_map/all_to_all | solution.py:319
  47.8 18.1 %all-to-all-done.1.parts_ref = f32[4,3,128,128]{3,2,1,0:T(8,128)S(1)} async-done(((f32[4,3,128,128]{3,2,1,0:T(8,128)}), f32[4,3,128,128]{3,2,1,0:T(8,128)S(1)}, u32[]{:S(2)}, u32[]{:S(2)}) %all-to-all-start.1) | async-done | bytes 786464 | tf_op jit(solution)/shard_map/all_to_all | solution.py:319
  66.0 1.0 group_scan.3
  68.3 27.8 %all_to_all.50 = f32[4,3,32,128]{3,2,1,0:T(8,128)S(1)} all-to-all(f32[4,3,32,128]{3,2,1,0:T(8,128)S(1)} %broadcast_in_dim.32), channel_id=1, replica_groups=mesh['zh'=4,'zl'=4,'x'=4,'y'=4,'core'=2] {'zh'}, dimensions={0} | all-to-all | bytes 393216 | tf_op jit(solution)/shard_map/all_to_all | solution.py:319
  96.1 1.0 broadcast_in_dim.33
  97.1 3.5 %all-to-all-start.3 = ((f32[4,4,3,32,128]{4,3,2,1,0:T(8,128)}), f32[4,4,3,32,128]{4,3,2,1,0:T(8,128)S(1)}, u32[]{:S(2)}, u32[]{:S(2)}) async-start(f32[4,4,3,32,128]{4,3,2,1,0:T(8,128)} %broadcast_in_dim.33), calls=%async_computation.3 | async-start | bytes 1572864 | tf_op jit(solution)/shard_map/all_to_all | solution.py:319
  100.6 10.4 %all-to-all-done.3.far_ref = f32[4,4,3,32,128]{4,3,2,1,0:T(8,128)S(1)} async-done(((f32[4,4,3,32,128]{4,3,2,1,0:T(8,128)}), f32[4,4,3,32,128]{4,3,2,1,0:T(8,128)S(1)}, u32[]{:S(2)}, u32[]{:S(2)}) %all-to-all-start.3) | async-done | bytes 786464 | tf_op jit(solution)/shard_map/all_to_all | solution.py:319
  117.2 3.3 %finish.1 = (bf16[128,128]{1,0:T(8,128)(2,1)}, f32[4,264,128]{2,1,0:T(8,128)}, f32[128,1024]{1,0:T(8,128)}) custom-call(s32[1]{0:T(128)} %bitcast.place_ref, f32[4,4,3,32,128]{4,3,2,1,0:T(8,128)S(1)} %all-to-all-done.3.far_ref, f32[2,128,128]{2,1,0:T(8,128)S(1)} %copy-done.18, f32[2,128,128]{2,1,0:T(8,128)S(1)} %copy-done.20, f32[2,128,128]{2,1,0:T(8,128)S(1)} %copy-done.14, ...), custom_call_target="tpu_custom_call" | custom-call | tf_op jit(solution)/shard_map/finish/pallas_call | solution.py:272
  120.5 3.5 %all-to-all-start.4 = ((f32[4,264,128]{2,1,0:T(8,128)}), f32[4,264,128]{2,1,0:T(8,128)S(1)}, u32[]{:S(2)}, u32[]{:S(2)}) async-start(f32[4,264,128]{2,1,0:T(8,128)} %get-tuple-element.48), calls=%async_computation.5 | async-start | bytes 1081344 | tf_op jit(solution)/shard_map/all_to_all | solution.py:323
  124.0 8.1 %all-to-all-done.4.pieces_ref = f32[4,264,128]{2,1,0:T(8,128)S(1)} async-done(((f32[4,264,128]{2,1,0:T(8,128)}), f32[4,264,128]{2,1,0:T(8,128)S(1)}, u32[]{:S(2)}, u32[]{:S(2)}) %all-to-all-start.4) | async-done | bytes 540704 | tf_op jit(solution)/shard_map/all_to_all | solution.py:323
  132.1 1.6 copy-done
  134.3 16.5 %all_to_all.51 = f32[4,328,128]{2,1,0:T(8,128)S(1)} all-to-all(f32[4,328,128]{2,1,0:T(8,128)S(1)} %weigh.1), channel_id=1, replica_groups=mesh['zh'=4,'zl'=4,'x'=4,'y'=4,'core'=2] {'zl'}, dimensions={0} | all-to-all | bytes 1343488 | tf_op jit(solution)/shard_map/all_to_all | solution.py:323
  150.8 21.2 %all_to_all.52 = f32[4,88,128]{2,1,0:T(8,128)S(1)} all-to-all(f32[4,88,128]{2,1,0:T(8,128)S(1)} %pad_maximum_fusion.3), channel_id=1, replica_groups=mesh['zh'=4,'zl'=4,'x'=4,'y'=4,'core'=2] {'zh'}, dimensions={0} | all-to-all | bytes 360448 | tf_op jit(solution)/shard_map/all_to_all | solution.py:323
  172.0 18.0 %all_to_all.53 = f32[4,80,128]{2,1,0:T(8,128)S(1)} all-to-all(f32[4,80,128]{2,1,0:T(8,128)S(1)} %broadcast_in_dim.70), channel_id=1, replica_groups=mesh['zh'=4,'zl'=4,'x'=4,'y'=4,'core'=2] {'zh'}, dimensions={0} | all-to-all | bytes 327680 | tf_op jit(solution)/shard_map/all_to_all | solution.py:319
  190.9 3.5 %all-to-all-start.8 = ((f32[4,320,128]{2,1,0:T(8,128)}), f32[4,320,128]{2,1,0:T(8,128)S(1)}, u32[]{:S(2)}, u32[]{:S(2)}) async-start(f32[4,320,128]{2,1,0:T(8,128)} %broadcast_in_dim.72), calls=%async_computation.9 | async-start | bytes 1310720 | tf_op jit(solution)/shard_map/all_to_all | solution.py:319
  194.4 13.1 %all-to-all-done.8 = f32[4,320,128]{2,1,0:T(8,128)S(1)} async-done(((f32[4,320,128]{2,1,0:T(8,128)}), f32[4,320,128]{2,1,0:T(8,128)S(1)}, u32[]{:S(2)}, u32[]{:S(2)}) %all-to-all-start.8) | async-done | bytes 655392 | tf_op jit(solution)/shard_map/all_to_all | solution.py:319
  207.5 1.6 broadcast_in_dim.73
  209.1 3.7 %all-to-all-start.9 = ((f32[4,1288,128]{2,1,0:T(8,128)}), f32[4,1288,128]{2,1,0:T(8,128)S(1)}, u32[]{:S(2)}, u32[]{:S(2)}) async-start(f32[4,1288,128]{2,1,0:T(8,128)} %broadcast_in_dim.73), calls=%async_computation.10 | async-start | bytes 5275648 | tf_op jit(solution)/shard_map/all_to_all | solution.py:319
  213.4 33.1 %reduce-scatter.2.cloned.1.call-done = f32[128,128]{1,0:T(8,128)} async-done(((f32[128,1024]{1,0:T(8,128)}), f32[128,128]{1,0:T(8,128)}) %reduce-scatter.2.cloned.1.call-update) | async-done | bytes 65552 | tf_op jit(solution)/shard_map/reduce_scatter | solution.py:341
  246.5 1.5 convert_element_type.3
  248.6 0.9 slice_bitcast_fusion
  249.5 1.4 pad_maximum_fusion
  (73 shorter events, 16.4 us)
Async XLA Ops:
  8.9 1.0 copy-start.1
  9.9 1.0 copy-start.3
  11.0 0.9 copy-start.5
  11.9 0.9 copy-start.7
  12.9 0.8 copy-start.9
  13.6 0.7 copy-start.25
  19.2 0.7 copy-start.11
  22.0 16.6 %all-to-all-start = ((f32[4,3,128,128]{3,2,1,0:T(8,128)}), f32[4,3,128,128]{3,2,1,0:T(8,128)S(1)}, u32[]{:S(2)}, u32[]{:S(2)}) async-start(f32[4,3,128,128]{3,2,1,0:T(8,128)} %broadcast_in_dim.30), calls=%async_computation | async-start | bytes 1572864 | tf_op jit(solution)/shard_map/all_to_all | solution.py:319
  39.6 0.7 copy-start.13
  40.2 1.0 copy-start.15
  41.2 24.8 %all-to-all-start.1 = ((f32[4,3,128,128]{3,2,1,0:T(8,128)}), f32[4,3,128,128]{3,2,1,0:T(8,128)S(1)}, u32[]{:S(2)}, u32[]{:S(2)}) async-start(f32[4,3,128,128]{3,2,1,0:T(8,128)} %broadcast_in_dim.31), calls=%async_computation.1 | async-start | bytes 1572864 | tf_op jit(solution)/shard_map/all_to_all | solution.py:319
  47.1 63.9 %copy-start.2 = (bf16[1024,256]{1,0:T(8,128)(2,1)S(1)}, bf16[1024,256]{1,0:T(8,128)(2,1)}, u32[]{:S(2)}) copy-start(bf16[1024,256]{1,0:T(8,128)(2,1)} %wk_ref.3) | copy-start | bytes 1572868
  47.1 63.9 %copy-start.4 = (bf16[1024,256]{1,0:T(8,128)(2,1)S(1)}, bf16[1024,256]{1,0:T(8,128)(2,1)}, u32[]{:S(2)}) copy-start(bf16[1024,256]{1,0:T(8,128)(2,1)} %wv_ref.3) | copy-start | bytes 1572868
  47.1 63.9 %copy-start.6 = (bf16[128,1024]{1,0:T(8,128)(2,1)S(1)}, bf16[128,1024]{1,0:T(8,128)(2,1)}, u32[]{:S(2)}) copy-start(bf16[128,1024]{1,0:T(8,128)(2,1)} %frames_ref.3) | copy-start | bytes 786436
  47.1 63.9 %copy-start.8 = (bf16[1024,128]{1,0:T(8,128)(2,1)S(1)}, bf16[1024,128]{1,0:T(8,128)(2,1)}, u32[]{:S(2)}) copy-start(bf16[1024,128]{1,0:T(8,128)(2,1)} %wq_ref.3) | copy-start | bytes 786436
  47.1 63.9 %copy-start.10 = (bf16[128,128]{1,0:T(8,128)(2,1)S(1)}, bf16[128,128]{1,0:T(8,128)(2,1)}, u32[]{:S(2)}) copy-start(bf16[128,128]{1,0:T(8,128)(2,1)} %cot_ref.3) | copy-start | bytes 98308
  47.1 76.9 %all-gather.3.cloned.1.call-start = ((), (), s32[]{:S(2)}) async-start(), calls=%async_computation.12 | async-start | bytes 2621440 | tf_op jit(solution)/shard_map/all_gather | solution.py:336
  66.9 0.7 copy-start.17
  67.6 0.6 copy-start.19
  97.1 13.9 %all-to-all-start.3 = ((f32[4,4,3,32,128]{4,3,2,1,0:T(8,128)}), f32[4,4,3,32,128]{4,3,2,1,0:T(8,128)S(1)}, u32[]{:S(2)}, u32[]{:S(2)}) async-start(f32[4,4,3,32,128]{4,3,2,1,0:T(8,128)} %broadcast_in_dim.33), calls=%async_computation.3 | async-start | bytes 1572864 | tf_op jit(solution)/shard_map/all_to_all | solution.py:319
  111.0 0.9 copy-start.12
  111.9 0.9 copy-start.14
  112.8 0.9 copy-start.16
  113.7 0.9 copy-start.18
  114.6 0.9 copy-start.20
  115.5 0.8 copy-start.22
  116.4 0.8 copy-start.24
  120.5 11.6 %all-to-all-start.4 = ((f32[4,264,128]{2,1,0:T(8,128)}), f32[4,264,128]{2,1,0:T(8,128)S(1)}, u32[]{:S(2)}, u32[]{:S(2)}) async-start(f32[4,264,128]{2,1,0:T(8,128)} %get-tuple-element.48), calls=%async_computation.5 | async-start | bytes 1081344 | tf_op jit(solution)/shard_map/all_to_all | solution.py:323
  132.1 1.6 copy-start
  190.9 16.6 %all-to-all-start.8 = ((f32[4,320,128]{2,1,0:T(8,128)}), f32[4,320,128]{2,1,0:T(8,128)S(1)}, u32[]{:S(2)}, u32[]{:S(2)}) async-start(f32[4,320,128]{2,1,0:T(8,128)} %broadcast_in_dim.72), calls=%async_computation.9 | async-start | bytes 1310720 | tf_op jit(solution)/shard_map/all_to_all | solution.py:319
  209.1 38.8 %all-to-all-start.9 = ((f32[4,1288,128]{2,1,0:T(8,128)}), f32[4,1288,128]{2,1,0:T(8,128)S(1)}, u32[]{:S(2)}, u32[]{:S(2)}) async-start(f32[4,1288,128]{2,1,0:T(8,128)} %broadcast_in_dim.73), calls=%async_computation.10 | async-start | bytes 5275648 | tf_op jit(solution)/shard_map/all_to_all | solution.py:319
  212.8 33.7 %reduce-scatter.2.cloned.1.call-start = ((), (), s32[]{:S(2)}) async-start(), calls=%async_computation.11 | async-start | bytes 589824 | tf_op jit(solution)/shard_map/reduce_scatter | solution.py:341
  (2 other events, 1.2 us)
Sparse Core Ops, SparseCore 0:
  50.8 38.9 all-gather.2
Sparse Core Ops, SparseCore 1:
  216.6 29.8 reduce-scatter.1

commit v2 on v1

v2 whole, which is shorter than its diff:
```python
import functools

import jax
import jax.numpy as jnp
from jax import lax
from jax.experimental import pallas as pl
from jax.experimental.pallas import tpu as pltpu
from jax.sharding import Mesh, PartitionSpec as P

DH = 128
ROWS = 128
HALF = 64
REFL = 256
PARTS = 4
KEPT_ROWS = (
    ("q", ROWS), ("k", REFL), ("v", REFL), ("w", REFL), ("u", REFL), ("z", REFL), ("yg", REFL),
    ("qt", ROWS), ("pu", ROWS), ("cols", REFL),
)
KEPT, KEPT_SIZE = {}, 0
for _name, _rows in KEPT_ROWS:
    KEPT[_name] = slice(KEPT_SIZE, KEPT_SIZE + _rows)
    KEPT_SIZE += _rows
EPS = 1e-06
EXTRA = 24
VMEM_BYTES = 63 * 1024 * 1024
SMALL_BYTES = 16 * 1024 * 1024


def halves(a):
    high = a.astype(jnp.bfloat16)
    return high, (a - high.astype(jnp.float32)).astype(jnp.bfloat16)


def dot(a, b, ca=1, cb=0):
    return lax.dot_general(a, b, (((ca,), (cb,)), ((), ())), preferred_element_type=jnp.float32)


def mm(a, b, ca=1, cb=0):
    return mm_halves(halves(a), halves(b), ca, cb)


def mm_halves(a, b, ca=1, cb=0):
    return dot(a[0], b[0], ca, cb) + (dot(a[0], b[1], ca, cb) + dot(a[1], b[0], ca, cb))


def mix(first, second):
    return jnp.concatenate([first[:HALF], second[:HALF], first[HALF:], second[HALF:]], axis=0)


def unmix(rows):
    first = jnp.concatenate([rows[:HALF], rows[ROWS : ROWS + HALF]], axis=0)
    second = jnp.concatenate([rows[HALF:ROWS], rows[ROWS + HALF :]], axis=0)
    return first, second


def place(shape, axis):
    row = lax.broadcasted_iota(jnp.int32, shape, axis)
    return (row & ROWS) + 2 * (row & (HALF - 1)) + ((row >> 6) & 1)


def seen_mask():
    frame = lax.broadcasted_iota(jnp.int32, (ROWS, REFL), 0)
    return (place((ROWS, REFL), 1) >> 1) <= frame


def fetch(pairs, sems):
    copies = [pltpu.make_async_copy(a, b, sems.at[i]) for i, (a, b) in enumerate(pairs)]
    for copy in copies:
        copy.start()
    return copies


def prepare_kernel(
    bias_ref, wb_ref, frames_any, wk_any, wq_any, wv_any, cot_any,
    send_ref, kept_any, wide_any,
    frames_ref, wk_ref, wq_ref, wv_ref, cot_ref, kept_ref, wide_ref, in_sems, out_sems,
):
    arrive = fetch(
        (
            (frames_any, frames_ref), (wk_any, wk_ref), (wq_any, wq_ref), (wv_any, wv_ref),
            (cot_any, cot_ref),
        ),
        in_sems,
    )

    def keep(name, value):
        kept_ref[KEPT[name], :] = value

    arrive[0].wait()
    frames = frames_ref[...]
    wide_ref[...] = frames.astype(jnp.float32)
    wide_copy = pltpu.make_async_copy(wide_ref, wide_any, out_sems.at[0])
    wide_copy.start()
    logits = dot(frames, wb_ref[...], 1, 1)
    arrive[1].wait()
    k_raw = dot(frames, wk_ref[...])
    for copy in arrive[2:]:
        copy.wait()
    q_raw = dot(frames, wq_ref[...])
    v_raw = dot(frames, wv_ref[...])
    rq = lax.rsqrt(jnp.sum(q_raw * q_raw, axis=1, keepdims=True) + EPS)
    q = q_raw * rq
    keys = mix(k_raw[:, :DH], k_raw[:, DH:])
    rk = lax.rsqrt(jnp.sum(keys * keys, axis=1, keepdims=True) + EPS)
    k = keys * rk
    v = mix(v_raw[:, :DH], v_raw[:, DH:])
    beta = 2.0 * jax.nn.sigmoid(mix(logits[:, 0:1] + bias_ref[0], logits[:, 1:2] + bias_ref[1]))
    keep("q", q)
    keep("k", k)
    keep("v", v)
    lane = lax.broadcasted_iota(jnp.int32, (REFL, DH), 1)
    rq_long = jnp.concatenate([rq, rq], axis=0)
    keep("cols", jnp.where(lane == 0, beta, jnp.where(lane == 1, rk, rq_long)))

    gram = mm(k, k, 1, 1)
    system = beta * gram
    row, col = place((ROWS, ROWS), 0), place((ROWS, ROWS), 1)
    parts = [system[:ROWS, :ROWS], system[ROWS:, ROWS:]]
    pair = ((row >> 1) == (col >> 1)) & (row > col)
    eye = jnp.where(row == col, 1.0, 0.0)
    inverse = [eye - jnp.where(pair, part, 0.0) for part in parts]
    for level in range(1, 7):
        lower = ((row >> (level + 1)) == (col >> (level + 1))) & ((row >> level) > (col >> level))
        inner = [mm(jnp.where(lower, part, 0.0), inv) for part, inv in zip(parts, inverse)]
        inverse = [inv - mm(inv, mid) for inv, mid in zip(inverse, inner)]
    corner = -mm(inverse[1], mm(system[ROWS:, :ROWS], inverse[0]))
    zero = jnp.zeros((ROWS, ROWS), jnp.float32)
    inverse = jnp.concatenate(
        [
            jnp.concatenate([inverse[0], zero], axis=1),
            jnp.concatenate([corner, inverse[1]], axis=1),
        ],
        axis=0,
    )
    wu = mm(inverse, jnp.concatenate([beta * k, beta * v], axis=1))
    w, u = wu[:, :DH], wu[:, DH:]
    keep("w", w)
    keep("u", u)
    kwu = mm(k, wu, 0, 0)
    scores = jnp.where(seen_mask(), mm(q, k, 1, 1), 0.0)
    pwu = mm(scores, wu)
    qt = q - pwu[:, :DH]
    keep("qt", qt)
    keep("pu", pwu[:, DH:])
    cot = cot_ref[...].astype(jnp.float32)
    send_ref[0] = eye_like() - kwu[:, :DH]
    send_ref[1] = kwu[:, DH:]
    send_ref[2] = mm(cot, qt, 0, 0)
    pg = mm(scores, cot, 0, 0)
    zy = mm(inverse, jnp.concatenate([k, pg], axis=1), 0, 0)
    keep("z", zy[:, :DH])
    keep("yg", zy[:, DH:])
    kept_copy = pltpu.make_async_copy(kept_ref, kept_any, out_sems.at[1])
    kept_copy.start()
    wide_copy.wait()
    kept_copy.wait()


def eye_like():
    row = lax.broadcasted_iota(jnp.int32, (DH, DH), 0)
    col = lax.broadcasted_iota(jnp.int32, (DH, DH), 1)
    return jnp.where(row == col, 1.0, 0.0)


def compose_group(me, parts):
    last = len(parts) - 1
    maps = [halves(part[0]) for part in parts]
    ahead = [jnp.concatenate([parts[0][0], parts[0][1]], axis=1)]
    behind = [jnp.concatenate([parts[last][0], parts[last][2]], axis=0)]
    for i in range(1, last + 1):
        moved = mm_halves(maps[i], halves(ahead[-1]))
        ahead.append(jnp.concatenate([moved[:, :DH], moved[:, DH:] + parts[i][1]], axis=1))
        j = last - i
        moved = mm_halves(halves(behind[-1]), maps[j])
        behind.append(jnp.concatenate([moved[:DH], moved[DH:] + parts[j][2]], axis=0))
    whole = (ahead[last][:, :DH], ahead[last][:, DH:], behind[last][DH:])
    eye, zero = eye_like(), jnp.zeros((DH, DH), jnp.float32)
    before = jnp.concatenate([eye, zero], axis=1)
    after = jnp.concatenate([eye, zero], axis=0)
    for i in range(last):
        before = jnp.where(me == i + 1, ahead[i], before)
        after = jnp.where(me == last - 1 - i, behind[i], after)
    return whole, (before[:, :DH], before[:, DH:], after[:DH], after[DH:])


def group_kernel(place_ref, parts_ref, total_ref, around_any, whole_ref, around_ref, sem, *, axis):
    parts = [tuple(parts_ref[i, j] for j in range(3)) for i in range(PARTS)]
    whole, around = compose_group(place_ref[axis], parts)
    for i, value in enumerate(around):
        around_ref[i] = value
    copy = pltpu.make_async_copy(around_ref, around_any, sem)
    copy.start()
    if total_ref.shape[1] == DH:
        for i, value in enumerate(whole):
            total_ref[i] = value
    else:
        for i, value in enumerate(whole):
            whole_ref[i] = value
        rows = DH // PARTS
        mine = pl.ds(pl.multiple_of(place_ref[0] * rows, rows), rows)
        for i in range(3):
            total_ref[i] = whole_ref[i, mine, :]
    copy.wait()


def group_scan(parts, place, axis, rows):
    return pl.pallas_call(
        functools.partial(group_kernel, axis=axis),
        out_shape=(f32(3, rows, DH), f32(4, DH, DH)),
        in_specs=[SMEM, VMEM],
        out_specs=(VMEM, ANY),
        scratch_shapes=[
            pltpu.VMEM((3, DH, DH), jnp.float32),
            pltpu.VMEM((4, DH, DH), jnp.float32),
            pltpu.SemaphoreType.DMA,
        ],
        compiler_params=pltpu.CompilerParams(vmem_limit_bytes=SMALL_BYTES),
        name="group_scan",
    )(place, parts)


def finish_kernel(
    place_ref, far_ref, wb_ref, near_any, own_any, kept_any, cot_any, frames_any, wq_any, wk_any, wv_any,
    out_ref, pieces_any, part_any,
    near_ref, own_ref, kept_ref, cot_ref, frames_ref, wq_ref, wk_ref, wv_ref, pieces_ref, part_ref,
    in_sems, out_sems,
):
    arrive = fetch(
        (
            (near_any, near_ref), (own_any, own_ref), (kept_any, kept_ref), (cot_any, cot_ref),
            (frames_any, frames_ref), (wq_any, wq_ref), (wk_any, wk_ref), (wv_any, wv_ref),
        ),
        in_sems,
    )
    me = place_ref[2]
    count = PARTS

    def far(group, which):
        return jnp.concatenate([far_ref[i, group, which] for i in range(PARTS)], axis=0)

    entering = jnp.where(me > 0, far(0, 1), 0.0)
    for i in range(1, count - 1):
        entering = jnp.where(me > i, mm(far(i, 0), entering) + far(i, 1), entering)
    leaving = jnp.where(me < count - 1, far(count - 1, 2), 0.0)
    for i in range(count - 2, 0, -1):
        leaving = jnp.where(me < i, mm(leaving, far(i, 0)) + far(i, 2), leaving)
    for copy in arrive[:4]:
        copy.wait()
    for around_ref in (near_ref, own_ref):
        entering = mm(around_ref[0], entering) + around_ref[1]
        leaving = mm(leaving, around_ref[2]) + around_ref[3]
    q, k, v = kept_ref[KEPT["q"], :], kept_ref[KEPT["k"], :], kept_ref[KEPT["v"], :]
    cot = cot_ref[...].astype(jnp.float32)
    cols = kept_ref[KEPT["cols"], :]
    beta, rk, rq = cols[:, 0:1], cols[:, 1:2], cols[:ROWS, 2:3]
    out_ref[...] = (mm(kept_ref[KEPT["qt"], :], entering) + kept_ref[KEPT["pu"], :]).astype(jnp.bfloat16)
    fresh = kept_ref[KEPT["u"], :] - mm(kept_ref[KEPT["w"], :], entering)
    y = kept_ref[KEPT["yg"], :] + mm(kept_ref[KEPT["z"], :], leaving, 1, 1)
    gram = mm(k, k, 1, 1)
    row, col = place((REFL, REFL), 0), place((REFL, REFL), 1)
    d_system = jnp.where(row > col, -mm(y, fresh, 1, 1), 0.0)
    d_scores = jnp.where(seen_mask(), mm(cot, fresh, 1, 1), 0.0)
    d_query = mm(cot, entering, 1, 1) + mm(d_scores, k)
    error = v - mm(k, entering)
    d_beta = jnp.sum(y * error, axis=1, keepdims=True) + jnp.sum(
        d_system * gram, axis=1, keepdims=True
    )
    by = beta * y
    d_gram = beta * d_system
    d_keys = (
        mm(d_scores, q, 0, 0)
        + mm(fresh, leaving)
        - mm(by, entering, 1, 1)
        + mm(d_gram, k)
        + mm(d_gram, k, 0, 0)
    )
    d_query = rq * (d_query - q * jnp.sum(d_query * q, axis=1, keepdims=True))
    d_keys = rk * (d_keys - k * jnp.sum(d_keys * k, axis=1, keepdims=True))
    d_logits = d_beta * beta * (1.0 - 0.5 * beta)
    l_first, l_second = unmix(d_logits)
    lane2 = lax.broadcasted_iota(jnp.int32, (ROWS, 2), 1)
    g_logits_f32 = jnp.where(lane2 == 0, l_first, l_second)
    g_query = d_query.astype(jnp.bfloat16)
    k_first, k_second = unmix(d_keys)
    v_first, v_second = unmix(by)
    g_keys = jnp.concatenate([k_first, k_second], axis=1).astype(jnp.bfloat16)
    g_values = jnp.concatenate([v_first, v_second], axis=1).astype(jnp.bfloat16)
    g_logits = g_logits_f32.astype(jnp.bfloat16)
    for copy in arrive[4:]:
        copy.wait()
    part_ref[...] = (
        dot(g_query, wq_ref[...], 1, 1)
        + dot(g_keys, wk_ref[...], 1, 1)
        + dot(g_values, wv_ref[...], 1, 1)
        + dot(g_logits, wb_ref[...])
    )
    part_copy = pltpu.make_async_copy(part_ref, part_any, out_sems.at[0])
    part_copy.start()
    wide = jnp.float32
    tiles = (g_query, g_keys[:, :DH], g_keys[:, DH:], g_values[:, :DH])
    shared = g_values[:, DH:].astype(wide)
    beta_rows = dot(g_logits, frames_ref[...], 0, 0)
    bias_row = jnp.sum(g_logits_f32, axis=0, keepdims=True)
    bias_lanes = jnp.where(
        lax.broadcasted_iota(jnp.int32, (1, DH), 1) == 0, bias_row[:, 0:1], bias_row[:, 1:2]
    )
    extra = [beta_rows[j : j + 1, DH * i : DH * i + DH] for j in range(2) for i in range(8)]
    extra = jnp.concatenate(extra + [bias_lanes, jnp.zeros((7, DH), wide)], axis=0)
    for i in range(PARTS):
        pieces_ref[i, :ROWS] = tiles[i].astype(wide)
        pieces_ref[i, ROWS : 2 * ROWS] = shared
        pieces_ref[i, 2 * ROWS :] = extra
    pieces_copy = pltpu.make_async_copy(pieces_ref, pieces_any, out_sems.at[1])
    pieces_copy.start()
    part_copy.wait()
    pieces_copy.wait()


def f32(*shape):
    return jax.ShapeDtypeStruct(shape, jnp.float32)


SMEM = pl.BlockSpec(memory_space=pltpu.SMEM)
VMEM = pl.BlockSpec(memory_space=pltpu.VMEM)
ANY = pl.BlockSpec(memory_space=pl.ANY)
HBM = pl.BlockSpec(memory_space=pltpu.HBM)


def held(a):
    return pltpu.VMEM(a.shape, a.dtype)


def prepare(bias, w_beta, *large):
    kept, wide = f32(KEPT_SIZE, DH), f32(ROWS, 1024)
    return pl.pallas_call(
        prepare_kernel,
        out_shape=(f32(3, DH, DH), kept, wide),
        in_specs=[SMEM, VMEM] + [HBM] * 5,
        out_specs=(VMEM, ANY, HBM),
        scratch_shapes=[held(a) for a in (*large, kept, wide)]
        + [pltpu.SemaphoreType.DMA((5,)), pltpu.SemaphoreType.DMA((2,))],
        compiler_params=pltpu.CompilerParams(vmem_limit_bytes=VMEM_BYTES),
        name="prepare",
    )(bias, w_beta, *large)


def finish(place, far, w_beta, *large):
    pieces, part = f32(PARTS, 2 * ROWS + EXTRA, DH), f32(ROWS, 1024)
    return pl.pallas_call(
        finish_kernel,
        out_shape=(
            jax.ShapeDtypeStruct((ROWS, DH), jnp.bfloat16),
            pieces,
            part,
        ),
        in_specs=[SMEM, VMEM, VMEM] + [ANY] * 3 + [HBM] * 5,
        out_specs=(VMEM, HBM, HBM),
        scratch_shapes=[held(a) for a in (*large, pieces, part)]
        + [pltpu.SemaphoreType.DMA((8,)), pltpu.SemaphoreType.DMA((2,))],
        compiler_params=pltpu.CompilerParams(vmem_limit_bytes=VMEM_BYTES),
        name="finish",
    )(place, far, w_beta, *large)


def weigh_kernel(place_ref, pieces_ref, frames_any, sums_ref, frames_ref, sems):
    arrive = fetch([(frames_any.at[i], frames_ref.at[i]) for i in range(PARTS)], sems)
    quarter = pl.ds(pl.multiple_of(place_ref[0] * 256, 256), 256)
    total = jnp.zeros((1024, DH), jnp.float32)
    corner = jnp.zeros((256, DH), jnp.float32)
    extra = jnp.zeros((EXTRA, DH), jnp.float32)
    for i in range(PARTS):
        piece = pieces_ref[i, : 2 * ROWS].astype(jnp.bfloat16)
        extra = extra + pieces_ref[i, 2 * ROWS :]
        arrive[i].wait()
        total = total + dot(frames_ref[i].astype(jnp.bfloat16), piece[:ROWS], 0, 0)
        corner = corner + dot(frames_ref[i, :, quarter].astype(jnp.bfloat16), piece[ROWS:], 0, 0)
    total = jnp.concatenate([total, corner], axis=0)
    rows = total.shape[0] // (PARTS * PARTS)
    for i in range(PARTS):
        for j in range(PARTS):
            block = PARTS * j + i
            sums_ref[i, rows * j : rows * j + rows] = total[rows * block : rows * block + rows]
        sums_ref[i, rows * PARTS :] = extra


def weigh(place, pieces, frames):
    return pl.pallas_call(
        weigh_kernel,
        out_shape=f32(PARTS, 1280 // PARTS + EXTRA, DH),
        in_specs=[SMEM, VMEM, HBM],
        scratch_shapes=[held(frames), pltpu.SemaphoreType.DMA((PARTS,))],
        compiler_params=pltpu.CompilerParams(vmem_limit_bytes=VMEM_BYTES),
        name="weigh",
    )(place, pieces, frames)


def lay_kernel(whole_any, query_any, keys_any, values_any, sems):
    left, right = pl.ds(0, DH), pl.ds(DH, DH)
    full = pl.ds(0, 1024)
    pairs = [
        (whole_any.at[0, full], query_any),
        (whole_any.at[1, full], keys_any.at[:, left]),
        (whole_any.at[2, full], keys_any.at[:, right]),
        (whole_any.at[3, full], values_any.at[:, left]),
    ]
    for i in range(PARTS):
        pairs.append(
            (whole_any.at[i, pl.ds(1024, 256)], values_any.at[pl.ds(256 * i, 256), right])
        )
    for copy in fetch(pairs, sems):
        copy.wait()


def lay(whole):
    return pl.pallas_call(
        lay_kernel,
        out_shape=(f32(1024, DH), f32(1024, 2 * DH), f32(1024, 2 * DH)),
        in_specs=[ANY],
        out_specs=(ANY, ANY, ANY),
        scratch_shapes=[pltpu.SemaphoreType.DMA((8,))],
        compiler_params=pltpu.CompilerParams(vmem_limit_bytes=VMEM_BYTES),
        name="lay",
    )(whole)


def spread(a, axis):
    return lax.all_to_all(jnp.broadcast_to(a[None], (PARTS, *a.shape)), axis, 0, 0, tiled=True)


def trade(a, axis):
    return lax.all_to_all(a, axis, 0, 0, tiled=True)


def local(frames, w_query, w_keys, w_values, w_beta, beta_bias, cotangent):
    place = jnp.stack([lax.axis_index("x"), lax.axis_index("zl"), lax.axis_index("zh")])
    beta_turned = w_beta.T
    own, kept, wide_frames = prepare(
        beta_bias, beta_turned, frames, w_keys, w_query, w_values, cotangent
    )
    row, wide_frames = lax.optimization_barrier((lax.all_gather(own, "x"), wide_frames))
    group_frames = lax.all_gather(wide_frames, "x")
    total, own_around = group_scan(row, place, 0, DH)
    total, near_around = group_scan(lax.all_gather(total, "zl"), place, 1, DH // PARTS)
    far = lax.all_gather(lax.all_gather(total, "zh"), "x")
    outputs, pieces, partial = finish(
        place, far, beta_turned, near_around, own_around, kept, cotangent,
        frames, w_query, w_keys, w_values,
    )
    summed = lax.psum_scatter(partial, ("y", "core"), scatter_dimension=1, tiled=True)
    sums = weigh(place, trade(pieces, "x"), group_frames)
    part = jnp.sum(trade(sums, "zl"), axis=0)
    part, extra = part[:320], part[320:]
    part = jnp.concatenate(
        [part.reshape(PARTS, 80, DH), jnp.broadcast_to(extra[None], (PARTS, EXTRA, DH))], axis=1
    )
    part = jnp.sum(trade(part, "zh"), axis=0)
    part, extra = part[:80], part[80:]
    part, summed = lax.optimization_barrier((part, summed))
    grad_frames = summed.astype(jnp.bfloat16)
    part = lax.all_gather(part, ("zh", "zl")).reshape(1280, DH)
    grad_query, grad_keys, grad_values = lay(spread(part, "x"))
    grad_beta = extra[:16].reshape(2, 1024).T
    grad_bias = extra[16, :2]
    return (outputs, grad_frames, grad_query, grad_keys, grad_values, grad_beta, grad_bias)


def solution(mesh):
    fine = Mesh(mesh.devices.reshape(4, 4, 4, 4, 2), ("zh", "zl", "x", "y", "core"))
    ctx, head = ("zh", "zl", "x"), ("y", "core")
    in_specs = (
        P(ctx, None),
        P(None, head),
        P(None, head),
        P(None, head),
        P(None, head),
        P(head),
        P(ctx, head),
    )
    out_specs = (
        P(ctx, head),
        P(ctx, head),
        P(None, head),
        P(None, head),
        P(None, head),
        P(None, head),
        P(head),
    )
    return jax.shard_map(local, mesh=fine, in_specs=in_specs, out_specs=out_specs, check_vma=False)
```

time: 263 us -> 311 us (1.18); the launches traced: 259 us -> 310 us
  Pallas kernels: 10.6 us -> 102 us
  waiting for transfers between devices: 96.3 us -> 40.3 us
  blocking collectives: 83.4 us -> 139 us
  local copies, waits for them, and re-layouts: 25.5 us -> 4.22 us
  starting transfers between devices: 24.4 us -> 8.27 us
    all_gather x0 -> x5, blocking collectives: none -> 107 us  [the longest x2 38.7 us: local(): far = lax.all_gather(lax.all_gather(total, 'zh'), 'x')]
    pallas_call x4 -> x5, Pallas kernels: 7.32 us -> 95.4 us  [the longest x1 80.6 us: lay(): pl.pallas_call(lay_kernel, out_shape=(f32(1024, DH), f32(1024, 2 * DH), f...]
    all_to_all x2 -> x0, blocking collectives: 45.8 us -> none  [spread(): lax.all_to_all(jnp.broadcast_to(a[None], (4, *a.shape)), axis, 0, 0, tile...]
    reduce_scatter x1, waiting for transfers between devices: 33.1 us -> 1.17 us  [local(): lax.psum_scatter(partial, ('y', 'core'), scatter_dimension=1, tiled=True)]
    all_to_all x5 -> x1, waiting for transfers between devices: 53.9 us -> 25.3 us  [spread(): lax.all_to_all(jnp.broadcast_to(a[None], (PARTS, *a.shape)), axis, 0, 0,...]
    unnamed x53 -> x8, local copies, waits for them, and re-layouts: 17.9 us -> 1.4 us
    all_to_all x5 -> x1, starting transfers between devices: 20.8 us -> 4.68 us  [spread(): lax.all_to_all(jnp.broadcast_to(a[None], (PARTS, *a.shape)), axis, 0, 0,...]
    all_to_all x2, blocking collectives: 37.6 us -> 32.1 us  [trade(): return lax.all_to_all(a, axis, 0, 0, tiled=True)]
  transfers between devices with their start and end apart: 8 -> 4, of which waited for: 6 -> 3; matrix products, arithmetic and copies ran while one was open for 1% -> 1% of each run, Pallas kernels for 2% -> 3%
where the time goes in v2:
time: 311 us; the launch traced here: 310 us
  blocking collectives  139 us (45%)
  Pallas kernels  102 us (33%)
  waiting for transfers between devices  40.3 us (13%)
  between operations  15.6 us (5%)
  starting transfers between devices  8.27 us (3%)
  local copies, waits for them, and re-layouts  4.22 us (1%)
    pallas_call x1, Pallas kernels, lay(): pl.pallas_call(lay_kernel, out_shape=(f32(1024, DH), f32(1024, 2 * DH), f...  80.6 us
    all_gather x2, blocking collectives, local(): far = lax.all_gather(lax.all_gather(total, 'zh'), 'x')  38.7 us
    all_gather x1, blocking collectives, local(): part = lax.all_gather(part, ('zh', 'zl')).reshape(1280, DH)  34 us
    all_to_all x2, blocking collectives, trade(): return lax.all_to_all(a, axis, 0, 0, tiled=True)  32.1 us
    all_to_all x1, waiting for transfers between devices, spread(): lax.all_to_all(jnp.broadcast_to(a[None], (PARTS, *a.shape)), axis, 0, 0,...  25.3 us
    all_gather x1, blocking collectives, local(): lax.all_gather(total, 'zl')  20.3 us
    all_gather x1, blocking collectives, local(): lax.all_gather(own, 'x')  13.9 us
    all_to_all x1, waiting for transfers between devices, trade(): return lax.all_to_all(a, axis, 0, 0, tiled=True)  13.3 us
  transfers between devices with their start and end apart: 4, of which 3 were waited for; matrix products, arithmetic and copies ran while one was open for 1% of the time, Pallas kernels for 3%

profile of v2, /device:TPU:24, one launch (start us, length us, event | category | flops | bytes accessed | tf_op | source)
XLA Modules:
  0.0 310.1 jit_solution(13914722701272617601)
XLA Ops:
  8.0 0.0 all-gather.8.cloned.1.call-start
  8.0 8.1 %prepare.1 = (f32[3,128,128]{2,1,0:T(8,128)}, f32[2176,128]{1,0:T(8,128)}, f32[128,1024]{1,0:T(8,128)}) custom-call(f32[2]{0:T(128)} %bias_ref.1, bf16[2,1024]{1,0:T(2,128)(2,1)} %bitcast.19, bf16[128,1024]{1,0:T(8,128)(2,1)} %frames_any.3, bf16[1024,256]{1,0:T(8,128)(2,1)} %wk_any.3, bf16[1024,128]{1,0:T(8,128)(2,1)} %wq_any.3, bf16[1024,256]{1,0:T(8,128)(2,1)} %wv_any.3, ...), custom_call_target="tpu_custom_call" | custom-call | tf_op jit(solution)/shard_map/prepare/pallas_call | solution.py:335
  16.2 13.9 %all-gather = f32[12,128,128]{2,1,0:T(8,128)S(1)} all-gather(f32[3,128,128]{2,1,0:T(8,128)} %get-tuple-element.24), channel_id=2, replica_groups=mesh['zh'=4,'zl'=4,'x'=4,'y'=4,'core'=2] {'x'}, dimensions={0}, use_global_device_ids=true | all-gather | bytes 983040 | tf_op jit(solution)/shard_map/all_gather | solution.py:440
  30.1 0.0 all-gather.8.cloned.1.call-update
  30.1 0.1 pad_add_fusion.place_ref
  30.2 1.3 group_scan.2
  31.5 0.0 copy-start
  31.5 0.7 copy-done
  32.2 20.3 %all-gather.1 = f32[12,128,128]{2,1,0:T(8,128)S(1)} all-gather(f32[3,128,128]{2,1,0:T(8,128)S(1)} %get-tuple-element.27), channel_id=3, replica_groups=mesh['zh'=4,'zl'=4,'x'=4,'y'=4,'core'=2] {'zl'}, dimensions={0}, use_global_device_ids=true | all-gather | bytes 983040 | tf_op jit(solution)/shard_map/all_gather | solution.py:443
  52.5 1.3 group_scan.3
  53.8 0.0 copy-start.1
  53.8 0.7 copy-done.1
  54.5 24.6 %all-gather.2 = f32[12,32,128]{2,1,0:T(8,128)S(1)} all-gather(f32[3,32,128]{2,1,0:T(8,128)S(1)} %get-tuple-element.28), channel_id=4, replica_groups=mesh['zh'=4,'zl'=4,'x'=4,'y'=4,'core'=2] {'zh'}, dimensions={0}, use_global_device_ids=true | all-gather | bytes 245760 | tf_op jit(solution)/shard_map/all_gather | solution.py:444
  79.1 14.0 %all-gather.3 = f32[16,3,32,128]{3,2,1,0:T(8,128)} all-gather(f32[4,3,32,128]{3,2,1,0:T(8,128)S(1)} %bitcast.17), channel_id=5, replica_groups=mesh['zh'=4,'zl'=4,'x'=4,'y'=4,'core'=2] {'x'}, dimensions={0}, use_global_device_ids=true | all-gather | bytes 983040 | tf_op jit(solution)/shard_map/all_gather | solution.py:444
  93.2 0.0 copy-done.2
  93.2 6.6 %finish.1 = (bf16[128,128]{1,0:T(8,128)(2,1)}, f32[4,280,128]{2,1,0:T(8,128)}, f32[128,1024]{1,0:T(8,128)}) custom-call(s32[3]{0:T(128)} %copy-done.2, f32[4,4,3,32,128]{4,3,2,1,0:T(8,128)} %bitcast.15, bf16[2,1024]{1,0:T(2,128)(2,1)} %bitcast.20, f32[4,128,128]{2,1,0:T(8,128)} %copy-done.1, f32[4,128,128]{2,1,0:T(8,128)} %copy-done, ...), custom_call_target="tpu_custom_call" | custom-call | tf_op jit(solution)/shard_map/finish/pallas_call | solution.py:349
  99.7 12.8 %all_to_all.20.pieces_ref = f32[4,280,128]{2,1,0:T(8,128)} all-to-all(f32[4,280,128]{2,1,0:T(8,128)} %get-tuple-element.33), channel_id=1, replica_groups=mesh['zh'=4,'zl'=4,'x'=4,'y'=4,'core'=2] {'x'}, dimensions={0} | all-to-all | bytes 1146880 | tf_op jit(solution)/shard_map/all_to_all | solution.py:431
  112.6 4.1 %weigh.1 = f32[4,344,128]{2,1,0:T(8,128)} custom-call(s32[3]{0:T(128)} %copy-done.2, f32[4,280,128]{2,1,0:T(8,128)} %all_to_all.20.pieces_ref, f32[4,128,1024]{2,1,0:T(8,128)} %bitcast.16), custom_call_target="tpu_custom_call" | custom-call | tf_op jit(solution)/shard_map/weigh/pallas_call | solution.py:387
  116.7 3.5 %all-to-all-start.1 = ((f32[4,344,128]{2,1,0:T(8,128)}), f32[4,344,128]{2,1,0:T(8,128)S(1)}, u32[]{:S(2)}, u32[]{:S(2)}) async-start(f32[4,344,128]{2,1,0:T(8,128)} %weigh.1), calls=%async_computation.1 | async-start | bytes 1409024 | tf_op jit(solution)/shard_map/all_to_all | solution.py:431
  120.2 0.0 reduce-scatter.2.cloned.1.call-start
  120.2 0.5 reduce-scatter.2.cloned.1.call-update
  120.7 13.3 %all-to-all-done.1 = f32[4,344,128]{2,1,0:T(8,128)S(1)} async-done(((f32[4,344,128]{2,1,0:T(8,128)}), f32[4,344,128]{2,1,0:T(8,128)S(1)}, u32[]{:S(2)}, u32[]{:S(2)}) %all-to-all-start.1) | async-done | bytes 704544 | tf_op jit(solution)/shard_map/all_to_all | solution.py:431
  134.2 19.2 %all_to_all.21 = f32[4,104,128]{2,1,0:T(8,128)S(1)} all-to-all(f32[4,104,128]{2,1,0:T(8,128)S(1)} %pad_maximum_fusion), channel_id=1, replica_groups=mesh['zh'=4,'zl'=4,'x'=4,'y'=4,'core'=2] {'zh'}, dimensions={0} | all-to-all | bytes 425984 | tf_op jit(solution)/shard_map/all_to_all | solution.py:431
  153.4 1.2 reduce-scatter.2.cloned.1.call-done
  154.6 34.0 %all-gather.5 = f32[1280,128]{1,0:T(8,128)S(1)} all-gather(f32[80,128]{1,0:T(8,128)S(1)} %slice.25), channel_id=7, replica_groups=mesh['zh'=4,'zl'=4,'x'=4,'y'=4,'core'=2] {'zh','zl'}, dimensions={0}, use_global_device_ids=true | all-gather | bytes 696320 | tf_op jit(solution)/shard_map/all_gather | solution.py:460
  188.6 1.7 broadcast_in_dim.15
  190.3 4.7 %all-to-all-start.3 = ((f32[4,1280,128]{2,1,0:T(8,128)}), f32[4,1280,128]{2,1,0:T(8,128)}, u32[]{:S(2)}, u32[]{:S(2)}) async-start(f32[4,1280,128]{2,1,0:T(8,128)} %broadcast_in_dim.15), calls=%async_computation.4 | async-start | bytes 5242880 | tf_op jit(solution)/shard_map/all_to_all | solution.py:427
  195.0 0.6 convert_element_type.3
  195.6 0.6 reshape.23
  196.2 0.5 slice_bitcast_fusion
  196.8 25.3 %all-to-all-done.3.whole_any = f32[4,1280,128]{2,1,0:T(8,128)} async-done(((f32[4,1280,128]{2,1,0:T(8,128)}), f32[4,1280,128]{2,1,0:T(8,128)}, u32[]{:S(2)}, u32[]{:S(2)}) %all-to-all-start.3) | async-done | bytes 2621472 | tf_op jit(solution)/shard_map/all_to_all | solution.py:427
  222.0 80.6 %lay.1 = (f32[1024,128]{1,0:T(8,128)}, f32[1024,256]{1,0:T(8,128)}, f32[1024,256]{1,0:T(8,128)}) custom-call(f32[4,1280,128]{2,1,0:T(8,128)} %all-to-all-done.3.whole_any), custom_call_target="tpu_custom_call" | custom-call | tf_op jit(solution)/shard_map/lay/pallas_call | solution.py:415
  (12 shorter events, 0.1 us)
Async XLA Ops:
  8.0 104.6 %all-gather.8.cloned.1.call-start = ((), (), s32[]{:S(2)}) async-start(), calls=%async_computation.6 | async-start | bytes 2621440 | tf_op jit(solution)/shard_map/all_gather | solution.py:441
  30.2 63.0 %copy-start.2 = (s32[3]{0:T(128)}, s32[3]{0:T(128)S(1)}, u32[]{:S(2)}) copy-start(s32[3]{0:T(128)S(1)} %pad_add_fusion.place_ref) | copy-start | bytes 40
  31.5 0.7 copy-start
  53.8 0.7 copy-start.1
  116.7 17.4 %all-to-all-start.1 = ((f32[4,344,128]{2,1,0:T(8,128)}), f32[4,344,128]{2,1,0:T(8,128)S(1)}, u32[]{:S(2)}, u32[]{:S(2)}) async-start(f32[4,344,128]{2,1,0:T(8,128)} %weigh.1), calls=%async_computation.1 | async-start | bytes 1409024 | tf_op jit(solution)/shard_map/all_to_all | solution.py:431
  120.2 34.5 %reduce-scatter.2.cloned.1.call-start = ((), (), s32[]{:S(2)}) async-start(), calls=%async_computation.5 | async-start | bytes 589824 | tf_op jit(solution)/shard_map/reduce_scatter | solution.py:449
  190.3 4.7 %copy-start.3 = (f32[128,128]{1,0:T(8,128)S(1)}, f32[128,128]{1,0:T(8,128)}, u32[]{:S(2)}) copy-start(f32[128,128]{1,0:T(8,128)} %reduce-scatter.2.cloned.1.call-done) | copy-start | bytes 196612
  190.3 31.7 %all-to-all-start.3 = ((f32[4,1280,128]{2,1,0:T(8,128)}), f32[4,1280,128]{2,1,0:T(8,128)}, u32[]{:S(2)}, u32[]{:S(2)}) async-start(f32[4,1280,128]{2,1,0:T(8,128)} %broadcast_in_dim.15), calls=%async_computation.4 | async-start | bytes 5242880 | tf_op jit(solution)/shard_map/all_to_all | solution.py:427
Sparse Core Ops, SparseCore 0:
  30.2 42.8 all-gather.7
Sparse Core Ops, SparseCore 1:
  124.0 30.5 reduce-scatter.1

commit v3 on v2

--- a/solution.py
+++ b/solution.py
@@ -13,8 +13,8 @@
 REFL = 256
 PARTS = 4
 KEPT_ROWS = (
-    ("q", ROWS), ("k", REFL), ("v", REFL), ("w", REFL), ("u", REFL), ("z", REFL), ("yg", REFL),
-    ("qt", ROWS), ("pu", ROWS), ("cols", REFL),
+    ("q", ROWS), ("k", REFL), ("v", REFL), ("w", REFL), ("u", REFL), ("qt", ROWS), ("pu", ROWS),
+    ("cols", REFL), ("z", REFL), ("yg", REFL),
 )
 KEPT, KEPT_SIZE = {}, 0
 for _name, _rows in KEPT_ROWS:
@@ -89,8 +89,7 @@
     arrive[0].wait()
     frames = frames_ref[...]
     wide_ref[...] = frames.astype(jnp.float32)
-    wide_copy = pltpu.make_async_copy(wide_ref, wide_any, out_sems.at[0])
-    wide_copy.start()
+    out_copies = fetch([(wide_ref, wide_any.at[i]) for i in range(PARTS)], out_sems)
     logits = dot(frames, wb_ref[...], 1, 1)
     arrive[1].wait()
     k_raw = dot(frames, wk_ref[...])
@@ -146,14 +145,26 @@
     send_ref[0] = eye_like() - kwu[:, :DH]
     send_ref[1] = kwu[:, DH:]
     send_ref[2] = mm(cot, qt, 0, 0)
+    late = KEPT["z"].start
+    out_copies.append(
+        pltpu.make_async_copy(
+            kept_ref.at[pl.ds(0, late)], kept_any.at[pl.ds(0, late)], out_sems.at[PARTS]
+        )
+    )
+    out_copies[-1].start()
     pg = mm(scores, cot, 0, 0)
     zy = mm(inverse, jnp.concatenate([k, pg], axis=1), 0, 0)
     keep("z", zy[:, :DH])
     keep("yg", zy[:, DH:])
-    kept_copy = pltpu.make_async_copy(kept_ref, kept_any, out_sems.at[1])
-    kept_copy.start()
-    wide_copy.wait()
-    kept_copy.wait()
+    late_rows = pl.ds(late, KEPT_SIZE - late)
+    out_copies.append(
+        pltpu.make_async_copy(
+            kept_ref.at[late_rows], kept_any.at[late_rows], out_sems.at[PARTS + 1]
+        )
+    )
+    out_copies[-1].start()
+    for copy in out_copies:
+        copy.wait()
 
 
 def eye_like():
@@ -208,31 +219,32 @@
         functools.partial(group_kernel, axis=axis),
         out_shape=(f32(3, rows, DH), f32(4, DH, DH)),
         in_specs=[SMEM, VMEM],
-        out_specs=(VMEM, ANY),
+        out_specs=(VMEM, HBM),
         scratch_shapes=[
             pltpu.VMEM((3, DH, DH), jnp.float32),
             pltpu.VMEM((4, DH, DH), jnp.float32),
             pltpu.SemaphoreType.DMA,
         ],
-        compiler_params=pltpu.CompilerParams(vmem_limit_bytes=SMALL_BYTES),
+        compiler_params=pltpu.CompilerParams(vmem_limit_bytes=VMEM_BYTES),
         name="group_scan",
     )(place, parts)
 
 
 def finish_kernel(
-    place_ref, far_ref, wb_ref, near_any, own_any, kept_any, cot_any, frames_any, wq_any, wk_any, wv_any,
+    place_ref, wb_ref, far_any, near_any, own_any, kept_any, cot_any, frames_any, wq_any, wk_any, wv_any,
     out_ref, pieces_any, part_any,
-    near_ref, own_ref, kept_ref, cot_ref, frames_ref, wq_ref, wk_ref, wv_ref, pieces_ref, part_ref,
+    far_ref, near_ref, own_ref, kept_ref, cot_ref, frames_ref, wq_ref, wk_ref, wv_ref, pieces_ref, part_ref,
     in_sems, out_sems,
 ):
     arrive = fetch(
         (
-            (near_any, near_ref), (own_any, own_ref), (kept_any, kept_ref), (cot_any, cot_ref),
+            (far_any, far_ref), (near_any, near_ref), (own_any, own_ref), (kept_any, kept_ref), (cot_any, cot_ref),
             (frames_any, frames_ref), (wq_any, wq_ref), (wk_any, wk_ref), (wv_any, wv_ref),
         ),
         in_sems,
     )
     me = place_ref[2]
+    arrive[0].wait()
     count = PARTS
 
     def far(group, which):
@@ -244,7 +256,7 @@
     leaving = jnp.where(me < count - 1, far(count - 1, 2), 0.0)
     for i in range(count - 2, 0, -1):
         leaving = jnp.where(me < i, mm(leaving, far(i, 0)) + far(i, 2), leaving)
-    for copy in arrive[:4]:
+    for copy in arrive[1:5]:
         copy.wait()
     for around_ref in (near_ref, own_ref):
         entering = mm(around_ref[0], entering) + around_ref[1]
@@ -286,14 +298,16 @@
     g_keys = jnp.concatenate([k_first, k_second], axis=1).astype(jnp.bfloat16)
     g_values = jnp.concatenate([v_first, v_second], axis=1).astype(jnp.bfloat16)
     g_logits = g_logits_f32.astype(jnp.bfloat16)
-    for copy in arrive[4:]:
+    for copy in arrive[5:]:
         copy.wait()
-    part_ref[...] = (
+    part = (
         dot(g_query, wq_ref[...], 1, 1)
         + dot(g_keys, wk_ref[...], 1, 1)
         + dot(g_values, wv_ref[...], 1, 1)
         + dot(g_logits, wb_ref[...])
     )
+    for i in range(8):
+        part_ref[i] = part[:, DH * i : DH * i + DH]
     part_copy = pltpu.make_async_copy(part_ref, part_any, out_sems.at[0])
     part_copy.start()
     wide = jnp.float32
@@ -331,21 +345,21 @@
 
 
 def prepare(bias, w_beta, *large):
-    kept, wide = f32(KEPT_SIZE, DH), f32(ROWS, 1024)
+    kept, wide = f32(KEPT_SIZE, DH), f32(PARTS, ROWS, 1024)
     return pl.pallas_call(
         prepare_kernel,
         out_shape=(f32(3, DH, DH), kept, wide),
         in_specs=[SMEM, VMEM] + [HBM] * 5,
-        out_specs=(VMEM, ANY, HBM),
-        scratch_shapes=[held(a) for a in (*large, kept, wide)]
-        + [pltpu.SemaphoreType.DMA((5,)), pltpu.SemaphoreType.DMA((2,))],
+        out_specs=(VMEM, HBM, HBM),
+        scratch_shapes=[held(a) for a in (*large, kept, f32(ROWS, 1024))]
+        + [pltpu.SemaphoreType.DMA((5,)), pltpu.SemaphoreType.DMA((PARTS + 2,))],
         compiler_params=pltpu.CompilerParams(vmem_limit_bytes=VMEM_BYTES),
         name="prepare",
     )(bias, w_beta, *large)
 
 
-def finish(place, far, w_beta, *large):
-    pieces, part = f32(PARTS, 2 * ROWS + EXTRA, DH), f32(ROWS, 1024)
+def finish(place, w_beta, *large):
+    pieces, part = f32(PARTS, 2 * ROWS + EXTRA, DH), f32(8, ROWS, DH)
     return pl.pallas_call(
         finish_kernel,
         out_shape=(
@@ -353,25 +367,27 @@
             pieces,
             part,
         ),
-        in_specs=[SMEM, VMEM, VMEM] + [ANY] * 3 + [HBM] * 5,
+        in_specs=[SMEM, VMEM] + [HBM] * 9,
         out_specs=(VMEM, HBM, HBM),
         scratch_shapes=[held(a) for a in (*large, pieces, part)]
-        + [pltpu.SemaphoreType.DMA((8,)), pltpu.SemaphoreType.DMA((2,))],
+        + [pltpu.SemaphoreType.DMA((9,)), pltpu.SemaphoreType.DMA((2,))],
         compiler_params=pltpu.CompilerParams(vmem_limit_bytes=VMEM_BYTES),
         name="finish",
-    )(place, far, w_beta, *large)
-
-
-def weigh_kernel(place_ref, pieces_ref, frames_any, sums_ref, frames_ref, sems):
-    arrive = fetch([(frames_any.at[i], frames_ref.at[i]) for i in range(PARTS)], sems)
+    )(place, w_beta, *large)
+
+
+def weigh_kernel(place_ref, pieces_any, frames_any, sums_ref, pieces_ref, frames_ref, sems):
+    pairs = [(pieces_any, pieces_ref)] + [(frames_any.at[i], frames_ref.at[i]) for i in range(PARTS)]
+    arrive = fetch(pairs, sems)
     quarter = pl.ds(pl.multiple_of(place_ref[0] * 256, 256), 256)
     total = jnp.zeros((1024, DH), jnp.float32)
     corner = jnp.zeros((256, DH), jnp.float32)
     extra = jnp.zeros((EXTRA, DH), jnp.float32)
+    arrive[0].wait()
     for i in range(PARTS):
         piece = pieces_ref[i, : 2 * ROWS].astype(jnp.bfloat16)
         extra = extra + pieces_ref[i, 2 * ROWS :]
-        arrive[i].wait()
+        arrive[i + 1].wait()
         total = total + dot(frames_ref[i].astype(jnp.bfloat16), piece[:ROWS], 0, 0)
         corner = corner + dot(frames_ref[i, :, quarter].astype(jnp.bfloat16), piece[ROWS:], 0, 0)
     total = jnp.concatenate([total, corner], axis=0)
@@ -387,25 +403,25 @@
     return pl.pallas_call(
         weigh_kernel,
         out_shape=f32(PARTS, 1280 // PARTS + EXTRA, DH),
-        in_specs=[SMEM, VMEM, HBM],
-        scratch_shapes=[held(frames), pltpu.SemaphoreType.DMA((PARTS,))],
+        in_specs=[SMEM, HBM, HBM],
+        scratch_shapes=[held(pieces), held(frames), pltpu.SemaphoreType.DMA((PARTS + 1,))],
         compiler_params=pltpu.CompilerParams(vmem_limit_bytes=VMEM_BYTES),
         name="weigh",
     )(place, pieces, frames)
 
 
-def lay_kernel(whole_any, query_any, keys_any, values_any, sems):
+def lay_kernel(whole_ref, query_any, keys_any, values_any, sems):
     left, right = pl.ds(0, DH), pl.ds(DH, DH)
     full = pl.ds(0, 1024)
     pairs = [
-        (whole_any.at[0, full], query_any),
-        (whole_any.at[1, full], keys_any.at[:, left]),
-        (whole_any.at[2, full], keys_any.at[:, right]),
-        (whole_any.at[3, full], values_any.at[:, left]),
+        (whole_ref.at[0, full], query_any),
+        (whole_ref.at[1, full], keys_any.at[:, left]),
+        (whole_ref.at[2, full], keys_any.at[:, right]),
+        (whole_ref.at[3, full], values_any.at[:, left]),
     ]
     for i in range(PARTS):
         pairs.append(
-            (whole_any.at[i, pl.ds(1024, 256)], values_any.at[pl.ds(256 * i, 256), right])
+            (whole_ref.at[i, pl.ds(1024, 256)], values_any.at[pl.ds(256 * i, 256), right])
         )
     for copy in fetch(pairs, sems):
         copy.wait()
@@ -415,10 +431,10 @@
     return pl.pallas_call(
         lay_kernel,
         out_shape=(f32(1024, DH), f32(1024, 2 * DH), f32(1024, 2 * DH)),
-        in_specs=[ANY],
-        out_specs=(ANY, ANY, ANY),
+        in_specs=[VMEM],
+        out_specs=(HBM, HBM, HBM),
         scratch_shapes=[pltpu.SemaphoreType.DMA((8,))],
-        compiler_params=pltpu.CompilerParams(vmem_limit_bytes=VMEM_BYTES),
+        compiler_params=pltpu.CompilerParams(vmem_limit_bytes=SMALL_BYTES),
         name="lay",
     )(whole)
 
@@ -438,15 +454,15 @@
         beta_bias, beta_turned, frames, w_keys, w_query, w_values, cotangent
     )
     row, wide_frames = lax.optimization_barrier((lax.all_gather(own, "x"), wide_frames))
-    group_frames = lax.all_gather(wide_frames, "x")
+    group_frames = trade(wide_frames, "x")
     total, own_around = group_scan(row, place, 0, DH)
     total, near_around = group_scan(lax.all_gather(total, "zl"), place, 1, DH // PARTS)
     far = lax.all_gather(lax.all_gather(total, "zh"), "x")
+    far, group_frames = lax.optimization_barrier((far, group_frames))
     outputs, pieces, partial = finish(
-        place, far, beta_turned, near_around, own_around, kept, cotangent,
+        place, beta_turned, far, near_around, own_around, kept, cotangent,
         frames, w_query, w_keys, w_values,
     )
-    summed = lax.psum_scatter(partial, ("y", "core"), scatter_dimension=1, tiled=True)
     sums = weigh(place, trade(pieces, "x"), group_frames)
     part = jnp.sum(trade(sums, "zl"), axis=0)
     part, extra = part[:320], part[320:]
@@ -455,9 +471,11 @@
     )
     part = jnp.sum(trade(part, "zh"), axis=0)
     part, extra = part[:80], part[80:]
-    part, summed = lax.optimization_barrier((part, summed))
-    grad_frames = summed.astype(jnp.bfloat16)
+    part, partial = lax.optimization_barrier((part, partial))
+    partial = trade(partial, ("y", "core"))
     part = lax.all_gather(part, ("zh", "zl")).reshape(1280, DH)
+    part, partial = lax.optimization_barrier((part, partial))
+    grad_frames = jnp.sum(partial, axis=0).astype(jnp.bfloat16)
     grad_query, grad_keys, grad_values = lay(spread(part, "x"))
     grad_beta = extra[:16].reshape(2, 1024).T
     grad_bias = extra[16, :2]

time: 311 us -> 233 us (0.75)
  Pallas kernels: 102 us -> 25.6 us
  blocking collectives: 139 us -> 164 us
  waiting for transfers between devices: 40.3 us -> 23.9 us
  between operations: 15.6 us -> 0.76 us
  starting transfers between devices: 8.27 us -> 12.8 us
    pallas_call x1, Pallas kernels: 80.6 us -> 1.54 us  [lay(): pl.pallas_call(lay_kernel, out_shape=(f32(1024, DH), f32(1024, 2 * DH), f...]
    all_to_all x2 -> x3, blocking collectives: 32.1 us -> 54.3 us  [trade(): return lax.all_to_all(a, axis, 0, 0, tiled=True)]
    all_to_all x1 -> x2, waiting for transfers between devices: 13.3 us -> 0.01 us  [trade(): return lax.all_to_all(a, axis, 0, 0, tiled=True)]
    all_to_all x1 -> x2, starting transfers between devices: 3.5 us -> 9.15 us  [trade(): return lax.all_to_all(a, axis, 0, 0, tiled=True)]
    pallas_call x2, Pallas kernels: 2.59 us -> 5.98 us  [group_scan(): pl.pallas_call(functools.partial(group_kernel, axis=axis), out_shape=(f32...]
    all_gather x1, blocking collectives: 13.9 us -> 17.2 us  [local(): lax.all_gather(own, 'x')]
  transfers between devices with their start and end apart: 4 -> 3, of which waited for: 3 -> 1; matrix products, arithmetic and copies ran while one was open for 1% -> 1% of each run, Pallas kernels for 3% -> 3%
where the time goes in v3:
time: 233 us; the launch traced here: 232 us
  blocking collectives  164 us (70%)
  Pallas kernels  25.6 us (11%)
  waiting for transfers between devices  23.9 us (10%)
  starting transfers between devices  12.8 us (5%)
  local copies, waits for them, and re-layouts  2.83 us (1%)
    all_to_all x3, blocking collectives, trade(): return lax.all_to_all(a, axis, 0, 0, tiled=True)  54.3 us
    all_gather x2, blocking collectives, local(): far = lax.all_gather(lax.all_gather(total, 'zh'), 'x')  39.8 us
    all_gather x1, blocking collectives, local(): part = lax.all_gather(part, ('zh', 'zl')).reshape(1280, DH)  31.9 us
    all_to_all x1, waiting for transfers between devices, spread(): lax.all_to_all(jnp.broadcast_to(a[None], (PARTS, *a.shape)), axis, 0, 0,...  23.9 us
    all_gather x1, blocking collectives, local(): lax.all_gather(total, 'zl')  21.2 us
    all_gather x1, blocking collectives, local(): lax.all_gather(own, 'x')  17.2 us
    all_to_all x2, starting transfers between devices, trade(): return lax.all_to_all(a, axis, 0, 0, tiled=True)  9.15 us
    pallas_call x1, Pallas kernels, prepare(): pl.pallas_call(prepare_kernel, out_shape=(f32(3, DH, DH), kept, wide), in...  7.9 us
  transfers between devices with their start and end apart: 3, of which 1 were waited for; matrix products, arithmetic and copies ran while one was open for 1% of the time, Pallas kernels for 3%

profile of v3, /device:TPU:24, one launch (start us, length us, event | category | flops | bytes accessed | tf_op | source)
XLA Modules:
  0.0 231.6 jit_solution(1324098646199987170)
XLA Ops:
  0.6 7.9 %prepare.1 = (f32[3,128,128]{2,1,0:T(8,128)}, f32[2176,128]{1,0:T(8,128)}, f32[4,128,1024]{2,1,0:T(8,128)}) custom-call(f32[2]{0:T(128)} %bias_ref.1, bf16[2,1024]{1,0:T(2,128)(2,1)} %bitcast.17, bf16[128,1024]{1,0:T(8,128)(2,1)} %frames_any.3, bf16[1024,256]{1,0:T(8,128)(2,1)} %wk_any.3, bf16[1024,128]{1,0:T(8,128)(2,1)} %wq_any.3, ...), custom_call_target="tpu_custom_call" | custom-call | tf_op jit(solution)/shard_map/prepare/pallas_call | solution.py:349
  8.5 17.2 %all-gather = f32[12,128,128]{2,1,0:T(8,128)} all-gather(f32[3,128,128]{2,1,0:T(8,128)} %get-tuple-element.28), channel_id=2, replica_groups=mesh['zh'=4,'zl'=4,'x'=4,'y'=4,'core'=2] {'x'}, dimensions={0}, use_global_device_ids=true | all-gather | bytes 983040 | tf_op jit(solution)/shard_map/all_gather | solution.py:456
  25.7 4.4 %all-to-all-start = ((f32[4,128,1024]{2,1,0:T(8,128)}), f32[4,128,1024]{2,1,0:T(8,128)}, u32[]{:S(2)}, u32[]{:S(2)}) async-start(f32[4,128,1024]{2,1,0:T(8,128)} %get-tuple-element.33), calls=%async_computation | async-start | bytes 4194304 | tf_op jit(solution)/shard_map/all_to_all | solution.py:447
  30.2 0.6 pad_add_fusion.place_ref
  30.8 3.0 %group_scan.2 = (f32[3,128,128]{2,1,0:T(8,128)}, f32[4,128,128]{2,1,0:T(8,128)}) custom-call(s32[3]{0:T(128)} %pad_add_fusion.place_ref, f32[4,3,128,128]{3,2,1,0:T(8,128)} %bitcast.13), custom_call_target="tpu_custom_call" | custom-call | tf_op jit(solution)/shard_map/group_scan/pallas_call | solution.py:218
  33.8 21.2 %all-gather.1 = f32[12,128,128]{2,1,0:T(8,128)} all-gather(f32[3,128,128]{2,1,0:T(8,128)} %get-tuple-element.31), channel_id=3, replica_groups=mesh['zh'=4,'zl'=4,'x'=4,'y'=4,'core'=2] {'zl'}, dimensions={0}, use_global_device_ids=true | all-gather | bytes 983040 | tf_op jit(solution)/shard_map/all_gather | solution.py:459
  55.0 3.0 %group_scan.3 = (f32[3,32,128]{2,1,0:T(8,128)}, f32[4,128,128]{2,1,0:T(8,128)}) custom-call(s32[3]{0:T(128)} %pad_add_fusion.place_ref, f32[4,3,128,128]{3,2,1,0:T(8,128)} %bitcast.14), custom_call_target="tpu_custom_call" | custom-call | tf_op jit(solution)/shard_map/group_scan/pallas_call | solution.py:218
  57.9 24.7 %all-gather.2 = f32[12,32,128]{2,1,0:T(8,128)S(1)} all-gather(f32[3,32,128]{2,1,0:T(8,128)} %get-tuple-element.32), channel_id=4, replica_groups=mesh['zh'=4,'zl'=4,'x'=4,'y'=4,'core'=2] {'zh'}, dimensions={0}, use_global_device_ids=true | all-gather | bytes 245760 | tf_op jit(solution)/shard_map/all_gather | solution.py:460
  82.6 15.1 %all-gather.3 = f32[16,3,32,128]{3,2,1,0:T(8,128)} all-gather(f32[4,3,32,128]{3,2,1,0:T(8,128)S(1)} %bitcast.15), channel_id=5, replica_groups=mesh['zh'=4,'zl'=4,'x'=4,'y'=4,'core'=2] {'x'}, dimensions={0}, use_global_device_ids=true | all-gather | bytes 983040 | tf_op jit(solution)/shard_map/all_gather | solution.py:460
  97.7 0.0 all-to-all-done.frames_any
  97.7 6.4 %finish.1 = (bf16[128,128]{1,0:T(8,128)(2,1)}, f32[4,280,128]{2,1,0:T(8,128)}, f32[8,128,128]{2,1,0:T(8,128)}) custom-call(s32[3]{0:T(128)} %pad_add_fusion.place_ref, bf16[2,1024]{1,0:T(2,128)(2,1)} %bitcast.18, f32[4,4,3,32,128]{4,3,2,1,0:T(8,128)} %bitcast.12, f32[4,128,128]{2,1,0:T(8,128)} %get-tuple-element.35.near_any, ...), custom_call_target="tpu_custom_call" | custom-call | tf_op jit(solution)/shard_map/finish/pallas_call | solution.py:363
  104.1 12.6 %all_to_all.30.pieces_any = f32[4,280,128]{2,1,0:T(8,128)} all-to-all(f32[4,280,128]{2,1,0:T(8,128)} %get-tuple-element.39), channel_id=1, replica_groups=mesh['zh'=4,'zl'=4,'x'=4,'y'=4,'core'=2] {'x'}, dimensions={0} | all-to-all | bytes 1146880 | tf_op jit(solution)/shard_map/all_to_all | solution.py:447
  116.7 3.8 %weigh.1 = f32[4,344,128]{2,1,0:T(8,128)} custom-call(s32[3]{0:T(128)} %pad_add_fusion.place_ref, f32[4,280,128]{2,1,0:T(8,128)} %all_to_all.30.pieces_any, f32[4,128,1024]{2,1,0:T(8,128)} %all-to-all-done.frames_any), custom_call_target="tpu_custom_call" | custom-call | tf_op jit(solution)/shard_map/weigh/pallas_call | solution.py:403
  120.5 20.0 %all_to_all.31 = f32[4,344,128]{2,1,0:T(8,128)S(1)} all-to-all(f32[4,344,128]{2,1,0:T(8,128)} %weigh.1), channel_id=1, replica_groups=mesh['zh'=4,'zl'=4,'x'=4,'y'=4,'core'=2] {'zl'}, dimensions={0} | all-to-all | bytes 1409024 | tf_op jit(solution)/shard_map/all_to_all | solution.py:447
  140.6 21.8 %all_to_all.32 = f32[4,104,128]{2,1,0:T(8,128)S(1)} all-to-all(f32[4,104,128]{2,1,0:T(8,128)S(1)} %pad_maximum_fusion), channel_id=1, replica_groups=mesh['zh'=4,'zl'=4,'x'=4,'y'=4,'core'=2] {'zh'}, dimensions={0} | all-to-all | bytes 425984 | tf_op jit(solution)/shard_map/all_to_all | solution.py:447
  162.4 4.7 %all-to-all-start.4 = ((f32[8,128,128]{2,1,0:T(8,128)}), f32[8,128,128]{2,1,0:T(8,128)S(1)}, u32[]{:S(2)}, u32[]{:S(2)}) async-start(f32[8,128,128]{2,1,0:T(8,128)} %get-tuple-element.43), calls=%async_computation.4 | async-start | bytes 1048576 | tf_op jit(solution)/shard_map/all_to_all | solution.py:447
  167.1 31.9 %all-gather.4 = f32[1280,128]{1,0:T(8,128)S(1)} all-gather(f32[80,128]{1,0:T(8,128)S(1)} %slice.25), channel_id=6, replica_groups=mesh['zh'=4,'zl'=4,'x'=4,'y'=4,'core'=2] {'zh','zl'}, dimensions={0}, use_global_device_ids=true | all-gather | bytes 696320 | tf_op jit(solution)/shard_map/all_gather | solution.py:476
  199.0 0.0 all-to-all-done.4
  199.0 1.7 broadcast_in_dim.5
  200.7 3.7 %all-to-all-start.5 = ((f32[4,1280,128]{2,1,0:T(8,128)}), f32[4,1280,128]{2,1,0:T(8,128)S(1)}, u32[]{:S(2)}, u32[]{:S(2)}) async-start(f32[4,1280,128]{2,1,0:T(8,128)} %broadcast_in_dim.5), calls=%async_computation.5 | async-start | bytes 5242880 | tf_op jit(solution)/shard_map/all_to_all | solution.py:443
  204.4 0.6 reshape.27
  205.0 0.5 slice_bitcast_fusion
  205.5 0.6 reduce_sum.29
  206.1 23.9 %all-to-all-done.5.whole_ref = f32[4,1280,128]{2,1,0:T(8,128)S(1)} async-done(((f32[4,1280,128]{2,1,0:T(8,128)}), f32[4,1280,128]{2,1,0:T(8,128)S(1)}, u32[]{:S(2)}, u32[]{:S(2)}) %all-to-all-start.5) | async-done | bytes 2621472 | tf_op jit(solution)/shard_map/all_to_all | solution.py:443
  230.0 1.5 lay.1
  (8 shorter events, 0.1 us)
Async XLA Ops:
  25.7 72.0 %all-to-all-start = ((f32[4,128,1024]{2,1,0:T(8,128)}), f32[4,128,1024]{2,1,0:T(8,128)}, u32[]{:S(2)}, u32[]{:S(2)}) async-start(f32[4,128,1024]{2,1,0:T(8,128)} %get-tuple-element.33), calls=%async_computation | async-start | bytes 4194304 | tf_op jit(solution)/shard_map/all_to_all | solution.py:447
  162.4 36.6 %all-to-all-start.4 = ((f32[8,128,128]{2,1,0:T(8,128)}), f32[8,128,128]{2,1,0:T(8,128)S(1)}, u32[]{:S(2)}, u32[]{:S(2)}) async-start(f32[8,128,128]{2,1,0:T(8,128)} %get-tuple-element.43), calls=%async_computation.4 | async-start | bytes 1048576 | tf_op jit(solution)/shard_map/all_to_all | solution.py:447
  200.7 29.3 %all-to-all-start.5 = ((f32[4,1280,128]{2,1,0:T(8,128)}), f32[4,1280,128]{2,1,0:T(8,128)S(1)}, u32[]{:S(2)}, u32[]{:S(2)}) async-start(f32[4,1280,128]{2,1,0:T(8,128)} %broadcast_in_dim.5), calls=%async_computation.5 | async-start | bytes 5242880 | tf_op jit(solution)/shard_map/all_to_all | solution.py:443

commit v4 on v3

--- a/solution.py
+++ b/solution.py
@@ -21,9 +21,12 @@
     KEPT[_name] = slice(KEPT_SIZE, KEPT_SIZE + _rows)
     KEPT_SIZE += _rows
 EPS = 1e-06
-EXTRA = 24
-VMEM_BYTES = 63 * 1024 * 1024
+EXTRA = 8
+LARGE_BYTES = 63 * 1024 * 1024
 SMALL_BYTES = 16 * 1024 * 1024
+FINISH_BYTES = LARGE_BYTES
+
+SIDE_BYTES = LARGE_BYTES
 
 
 def halves(a):
@@ -225,21 +228,21 @@
             pltpu.VMEM((4, DH, DH), jnp.float32),
             pltpu.SemaphoreType.DMA,
         ],
-        compiler_params=pltpu.CompilerParams(vmem_limit_bytes=VMEM_BYTES),
+        compiler_params=pltpu.CompilerParams(vmem_limit_bytes=SMALL_BYTES),
         name="group_scan",
     )(place, parts)
 
 
 def finish_kernel(
-    place_ref, wb_ref, far_any, near_any, own_any, kept_any, cot_any, frames_any, wq_any, wk_any, wv_any,
-    out_ref, pieces_any, part_any,
-    far_ref, near_ref, own_ref, kept_ref, cot_ref, frames_ref, wq_ref, wk_ref, wv_ref, pieces_ref, part_ref,
+    place_ref, far_any, near_any, own_any, kept_any, cot_any, frames_any,
+    out_ref, pieces_any, tiles_any,
+    far_ref, near_ref, own_ref, kept_ref, cot_ref, frames_ref, pieces_ref, tiles_ref,
     in_sems, out_sems,
 ):
     arrive = fetch(
         (
-            (far_any, far_ref), (near_any, near_ref), (own_any, own_ref), (kept_any, kept_ref), (cot_any, cot_ref),
-            (frames_any, frames_ref), (wq_any, wq_ref), (wk_any, wk_ref), (wv_any, wv_ref),
+            (far_any, far_ref), (near_any, near_ref), (own_any, own_ref), (kept_any, kept_ref),
+            (cot_any, cot_ref), (frames_any, frames_ref),
         ),
         in_sems,
     )
@@ -298,18 +301,15 @@
     g_keys = jnp.concatenate([k_first, k_second], axis=1).astype(jnp.bfloat16)
     g_values = jnp.concatenate([v_first, v_second], axis=1).astype(jnp.bfloat16)
     g_logits = g_logits_f32.astype(jnp.bfloat16)
-    for copy in arrive[5:]:
-        copy.wait()
-    part = (
-        dot(g_query, wq_ref[...], 1, 1)
-        + dot(g_keys, wk_ref[...], 1, 1)
-        + dot(g_values, wv_ref[...], 1, 1)
-        + dot(g_logits, wb_ref[...])
-    )
-    for i in range(8):
-        part_ref[i] = part[:, DH * i : DH * i + DH]
-    part_copy = pltpu.make_async_copy(part_ref, part_any, out_sems.at[0])
-    part_copy.start()
+    tiles_ref[:, :DH] = g_query
+    tiles_ref[:, DH : 3 * DH] = g_keys
+    tiles_ref[:, 3 * DH : 5 * DH] = g_values
+    lane = lax.broadcasted_iota(jnp.int32, (ROWS, DH), 1)
+    padded = jnp.where(lane == 0, l_first, jnp.where(lane == 1, l_second, 0.0))
+    tiles_ref[:, 5 * DH :] = padded.astype(jnp.bfloat16)
+    tiles_copy = pltpu.make_async_copy(tiles_ref, tiles_any, out_sems.at[0])
+    tiles_copy.start()
+    arrive[5].wait()
     wide = jnp.float32
     tiles = (g_query, g_keys[:, :DH], g_keys[:, DH:], g_values[:, :DH])
     shared = g_values[:, DH:].astype(wide)
@@ -318,15 +318,16 @@
     bias_lanes = jnp.where(
         lax.broadcasted_iota(jnp.int32, (1, DH), 1) == 0, bias_row[:, 0:1], bias_row[:, 1:2]
     )
-    extra = [beta_rows[j : j + 1, DH * i : DH * i + DH] for j in range(2) for i in range(8)]
-    extra = jnp.concatenate(extra + [bias_lanes, jnp.zeros((7, DH), wide)], axis=0)
     for i in range(PARTS):
         pieces_ref[i, :ROWS] = tiles[i].astype(wide)
         pieces_ref[i, ROWS : 2 * ROWS] = shared
-        pieces_ref[i, 2 * ROWS :] = extra
+        span = beta_rows[:, 256 * i : 256 * i + 256]
+        pieces_ref[i, 2 * ROWS :] = jnp.concatenate(
+            [span[:, :DH], span[:, DH:], bias_lanes, jnp.zeros((EXTRA - 5, DH), wide)], axis=0
+        )
     pieces_copy = pltpu.make_async_copy(pieces_ref, pieces_any, out_sems.at[1])
     pieces_copy.start()
-    part_copy.wait()
+    tiles_copy.wait()
     pieces_copy.wait()
 
 
@@ -353,43 +354,82 @@
         out_specs=(VMEM, HBM, HBM),
         scratch_shapes=[held(a) for a in (*large, kept, f32(ROWS, 1024))]
         + [pltpu.SemaphoreType.DMA((5,)), pltpu.SemaphoreType.DMA((PARTS + 2,))],
-        compiler_params=pltpu.CompilerParams(vmem_limit_bytes=VMEM_BYTES),
+        compiler_params=pltpu.CompilerParams(vmem_limit_bytes=LARGE_BYTES),
         name="prepare",
     )(bias, w_beta, *large)
 
 
-def finish(place, w_beta, *large):
-    pieces, part = f32(PARTS, 2 * ROWS + EXTRA, DH), f32(8, ROWS, DH)
+def finish(place, *large):
+    pieces = f32(PARTS, 2 * ROWS + EXTRA, DH)
+    tiles = jax.ShapeDtypeStruct((ROWS, 6 * DH), jnp.bfloat16)
     return pl.pallas_call(
         finish_kernel,
-        out_shape=(
-            jax.ShapeDtypeStruct((ROWS, DH), jnp.bfloat16),
-            pieces,
-            part,
+        out_shape=(jax.ShapeDtypeStruct((ROWS, DH), jnp.bfloat16), pieces, tiles),
+        in_specs=[SMEM] + [HBM] * 6,
+        out_specs=(VMEM, HBM, HBM),
+        scratch_shapes=[held(a) for a in (*large, pieces, tiles)]
+        + [pltpu.SemaphoreType.DMA((6,)), pltpu.SemaphoreType.DMA((2,))],
+        compiler_params=pltpu.CompilerParams(vmem_limit_bytes=FINISH_BYTES),
+        name="finish",
+    )(place, *large)
+
+
+def side_kernel(
+    tiles_any, wb_ref, wq_any, wk_any, wv_any, frames_any, part_any, narrow_any,
+    tiles_ref, wq_ref, wk_ref, wv_ref, frames_ref, part_ref, narrow_ref, in_sems, out_sems,
+):
+    arrive = fetch(
+        (
+            (frames_any, frames_ref), (tiles_any, tiles_ref), (wq_any, wq_ref), (wk_any, wk_ref),
+            (wv_any, wv_ref),
         ),
-        in_specs=[SMEM, VMEM] + [HBM] * 9,
-        out_specs=(VMEM, HBM, HBM),
-        scratch_shapes=[held(a) for a in (*large, pieces, part)]
-        + [pltpu.SemaphoreType.DMA((9,)), pltpu.SemaphoreType.DMA((2,))],
-        compiler_params=pltpu.CompilerParams(vmem_limit_bytes=VMEM_BYTES),
-        name="finish",
-    )(place, w_beta, *large)
-
-
-def weigh_kernel(place_ref, pieces_any, frames_any, sums_ref, pieces_ref, frames_ref, sems):
-    pairs = [(pieces_any, pieces_ref)] + [(frames_any.at[i], frames_ref.at[i]) for i in range(PARTS)]
-    arrive = fetch(pairs, sems)
+        in_sems,
+    )
+    arrive[0].wait()
+    narrow_ref[...] = frames_ref[...].astype(jnp.bfloat16)
+    out_copies = fetch([(narrow_ref, narrow_any)], out_sems)
+    for copy in arrive[1:]:
+        copy.wait()
+    part = (
+        dot(tiles_ref[:, :DH], wq_ref[...], 1, 1)
+        + dot(tiles_ref[:, DH : 3 * DH], wk_ref[...], 1, 1)
+        + dot(tiles_ref[:, 3 * DH : 5 * DH], wv_ref[...], 1, 1)
+        + dot(tiles_ref[:, 5 * DH : 5 * DH + 2], wb_ref[...])
+    )
+    for i in range(8):
+        part_ref[i] = part[:, DH * i : DH * i + DH]
+    out_copies.append(pltpu.make_async_copy(part_ref, part_any, out_sems.at[1]))
+    out_copies[1].start()
+    for copy in out_copies:
+        copy.wait()
+
+
+def side(tiles, w_beta, *large):
+    part = f32(8, ROWS, DH)
+    narrow = jax.ShapeDtypeStruct((PARTS, ROWS, 1024), jnp.bfloat16)
+    return pl.pallas_call(
+        side_kernel,
+        out_shape=(part, narrow),
+        in_specs=[HBM, VMEM] + [HBM] * 4,
+        out_specs=(HBM, HBM),
+        scratch_shapes=[held(a) for a in (tiles, *large, part, narrow)]
+        + [pltpu.SemaphoreType.DMA((5,)), pltpu.SemaphoreType.DMA((2,))],
+        compiler_params=pltpu.CompilerParams(vmem_limit_bytes=SIDE_BYTES),
+        cost_estimate=pl.CostEstimate(flops=170_000_000, bytes_accessed=6_000_000, transcendentals=0),
+        name="side",
+    )(tiles, w_beta, *large)
+
+
+def weigh_kernel(place_ref, pieces_ref, frames_ref, sums_ref):
     quarter = pl.ds(pl.multiple_of(place_ref[0] * 256, 256), 256)
     total = jnp.zeros((1024, DH), jnp.float32)
     corner = jnp.zeros((256, DH), jnp.float32)
     extra = jnp.zeros((EXTRA, DH), jnp.float32)
-    arrive[0].wait()
     for i in range(PARTS):
         piece = pieces_ref[i, : 2 * ROWS].astype(jnp.bfloat16)
         extra = extra + pieces_ref[i, 2 * ROWS :]
-        arrive[i + 1].wait()
-        total = total + dot(frames_ref[i].astype(jnp.bfloat16), piece[:ROWS], 0, 0)
-        corner = corner + dot(frames_ref[i, :, quarter].astype(jnp.bfloat16), piece[ROWS:], 0, 0)
+        total = total + dot(frames_ref[i], piece[:ROWS], 0, 0)
+        corner = corner + dot(frames_ref[i, :, quarter], piece[ROWS:], 0, 0)
     total = jnp.concatenate([total, corner], axis=0)
     rows = total.shape[0] // (PARTS * PARTS)
     for i in range(PARTS):
@@ -403,14 +443,13 @@
     return pl.pallas_call(
         weigh_kernel,
         out_shape=f32(PARTS, 1280 // PARTS + EXTRA, DH),
-        in_specs=[SMEM, HBM, HBM],
-        scratch_shapes=[held(pieces), held(frames), pltpu.SemaphoreType.DMA((PARTS + 1,))],
-        compiler_params=pltpu.CompilerParams(vmem_limit_bytes=VMEM_BYTES),
+        in_specs=[SMEM, VMEM, VMEM],
+        compiler_params=pltpu.CompilerParams(vmem_limit_bytes=SMALL_BYTES),
         name="weigh",
     )(place, pieces, frames)
 
 
-def lay_kernel(whole_ref, query_any, keys_any, values_any, sems):
+def lay_kernel(whole_ref, query_any, keys_any, values_any, beta_ref, bias_ref, sems):
     left, right = pl.ds(0, DH), pl.ds(DH, DH)
     full = pl.ds(0, 1024)
     pairs = [
@@ -423,16 +462,24 @@
         pairs.append(
             (whole_ref.at[i, pl.ds(1024, 256)], values_any.at[pl.ds(256 * i, 256), right])
         )
-    for copy in fetch(pairs, sems):
+    copies = fetch(pairs, sems)
+    rows = [whole_ref[i, 1280:] for i in range(PARTS)]
+    beta_ref[...] = jnp.concatenate(
+        [row[2 * half : 2 * half + 2] for row in rows for half in range(2)], axis=1
+    )
+    bias_ref[...] = rows[0][4:5, :2]
+    for copy in copies:
         copy.wait()
 
 
 def lay(whole):
     return pl.pallas_call(
         lay_kernel,
-        out_shape=(f32(1024, DH), f32(1024, 2 * DH), f32(1024, 2 * DH)),
+        out_shape=(
+            f32(1024, DH), f32(1024, 2 * DH), f32(1024, 2 * DH), f32(2, 1024), f32(1, 2),
+        ),
         in_specs=[VMEM],
-        out_specs=(HBM, HBM, HBM),
+        out_specs=(HBM, HBM, HBM, VMEM, VMEM),
         scratch_shapes=[pltpu.SemaphoreType.DMA((8,))],
         compiler_params=pltpu.CompilerParams(vmem_limit_bytes=SMALL_BYTES),
         name="lay",
@@ -459,10 +506,8 @@
     total, near_around = group_scan(lax.all_gather(total, "zl"), place, 1, DH // PARTS)
     far = lax.all_gather(lax.all_gather(total, "zh"), "x")
     far, group_frames = lax.optimization_barrier((far, group_frames))
-    outputs, pieces, partial = finish(
-        place, beta_turned, far, near_around, own_around, kept, cotangent,
-        frames, w_query, w_keys, w_values,
-    )
+    outputs, pieces, tiles = finish(place, far, near_around, own_around, kept, cotangent, frames)
+    partial, group_frames = side(tiles, beta_turned, w_query, w_keys, w_values, group_frames)
     sums = weigh(place, trade(pieces, "x"), group_frames)
     part = jnp.sum(trade(sums, "zl"), axis=0)
     part, extra = part[:320], part[320:]
@@ -474,11 +519,12 @@
     part, partial = lax.optimization_barrier((part, partial))
     partial = trade(partial, ("y", "core"))
     part = lax.all_gather(part, ("zh", "zl")).reshape(1280, DH)
-    part, partial = lax.optimization_barrier((part, partial))
     grad_frames = jnp.sum(partial, axis=0).astype(jnp.bfloat16)
-    grad_query, grad_keys, grad_values = lay(spread(part, "x"))
-    grad_beta = extra[:16].reshape(2, 1024).T
-    grad_bias = extra[16, :2]
+    part, grad_frames = lax.optimization_barrier((part, grad_frames))
+    whole = jnp.concatenate([part, extra], axis=0)
+    grad_query, grad_keys, grad_values, beta_rows, bias_row = lay(spread(whole, "x"))
+    grad_beta = beta_rows.T
+    grad_bias = bias_row.reshape(2)
     return (outputs, grad_frames, grad_query, grad_keys, grad_values, grad_beta, grad_bias)
 
 

time: 233 us -> 216 us (0.927)
  waiting for transfers between devices: 23.9 us -> 4.05 us
  blocking collectives: 164 us -> 170 us
    all_to_all x0 -> x1, blocking collectives: none -> 28.4 us  [spread(): lax.all_to_all(jnp.broadcast_to(a[None], (PARTS, *a.shape)), axis, 0, 0,...]
    all_to_all x1 -> x0, waiting for transfers between devices: 23.9 us -> none  [spread(): lax.all_to_all(jnp.broadcast_to(a[None], (PARTS, *a.shape)), axis, 0, 0,...]
    all_to_all x3 -> x2, blocking collectives: 54.3 us -> 36 us  [trade(): return lax.all_to_all(a, axis, 0, 0, tiled=True)]
    pallas_call x0 -> x1, Pallas kernels: none -> 4.12 us  [side(): pl.pallas_call(side_kernel, out_shape=(part, narrow), in_specs=[HBM, VMEM...]
    all_to_all x2 -> x3, waiting for transfers between devices: 0.01 us -> 4.05 us  [trade(): return lax.all_to_all(a, axis, 0, 0, tiled=True)]
    all_to_all x2 -> x3, starting transfers between devices: 9.15 us -> 13 us  [trade(): return lax.all_to_all(a, axis, 0, 0, tiled=True)]
    all_to_all x1 -> x0, starting transfers between devices: 3.65 us -> none  [spread(): lax.all_to_all(jnp.broadcast_to(a[None], (PARTS, *a.shape)), axis, 0, 0,...]
    pallas_call x2, Pallas kernels: 5.98 us -> 2.6 us  [group_scan(): pl.pallas_call(functools.partial(group_kernel, axis=axis), out_shape=(f32...]
  transfers between devices with their start and end apart: 3 -> 3, of which waited for: 1 -> 1; matrix products, arithmetic and copies ran while one was open for 1% -> 0% of each run, Pallas kernels for 3% -> 3%
where the time goes in v4:
time: 216 us; the launch traced here: 215 us
  blocking collectives  170 us (79%)
  Pallas kernels  23.5 us (11%)
  starting transfers between devices  13 us (6%)
  waiting for transfers between devices  4.05 us (2%)
  local copies, waits for them, and re-layouts  2.83 us (1%)
    all_gather x2, blocking collectives, local(): far = lax.all_gather(lax.all_gather(total, 'zh'), 'x')  39.5 us
    all_to_all x2, blocking collectives, trade(): return lax.all_to_all(a, axis, 0, 0, tiled=True)  36 us
    all_gather x1, blocking collectives, local(): part = lax.all_gather(part, ('zh', 'zl')).reshape(1280, DH)  31.9 us
    all_to_all x1, blocking collectives, spread(): lax.all_to_all(jnp.broadcast_to(a[None], (PARTS, *a.shape)), axis, 0, 0,...  28.4 us
    all_gather x1, blocking collectives, local(): lax.all_gather(total, 'zl')  20.3 us
    all_gather x1, blocking collectives, local(): lax.all_gather(own, 'x')  13.9 us
    all_to_all x3, starting transfers between devices, trade(): return lax.all_to_all(a, axis, 0, 0, tiled=True)  13 us
    pallas_call x1, Pallas kernels, prepare(): pl.pallas_call(prepare_kernel, out_shape=(f32(3, DH, DH), kept, wide), in...  7.88 us
  transfers between devices with their start and end apart: 3, of which 1 were waited for; matrix products, arithmetic and copies ran while one was open for 0% of the time, Pallas kernels for 3%

profile of v4, /device:TPU:24, one launch (start us, length us, event | category | flops | bytes accessed | tf_op | source)
XLA Modules:
  0.0 215.0 jit_solution(15171657386456267957)
XLA Ops:
  0.6 7.9 %prepare.1 = (f32[3,128,128]{2,1,0:T(8,128)}, f32[2176,128]{1,0:T(8,128)}, f32[4,128,1024]{2,1,0:T(8,128)}) custom-call(f32[2]{0:T(128)} %bias_ref.1, bf16[2,1024]{1,0:T(2,128)(2,1)} %bitcast.16, bf16[128,1024]{1,0:T(8,128)(2,1)} %frames_any.3, bf16[1024,256]{1,0:T(8,128)(2,1)} %wk_any.3, bf16[1024,128]{1,0:T(8,128)(2,1)} %wq_any.3, ...), custom_call_target="tpu_custom_call" | custom-call | tf_op jit(solution)/shard_map/prepare/pallas_call | solution.py:350
  8.5 13.9 %all-gather = f32[12,128,128]{2,1,0:T(8,128)S(1)} all-gather(f32[3,128,128]{2,1,0:T(8,128)} %get-tuple-element.32), channel_id=2, replica_groups=mesh['zh'=4,'zl'=4,'x'=4,'y'=4,'core'=2] {'x'}, dimensions={0}, use_global_device_ids=true | all-gather | bytes 983040 | tf_op jit(solution)/shard_map/all_gather | solution.py:503
  22.4 4.5 %all-to-all-start = ((f32[4,128,1024]{2,1,0:T(8,128)}), f32[4,128,1024]{2,1,0:T(8,128)}, u32[]{:S(2)}, u32[]{:S(2)}) async-start(f32[4,128,1024]{2,1,0:T(8,128)} %get-tuple-element.37), calls=%async_computation | async-start | bytes 4194304 | tf_op jit(solution)/shard_map/all_to_all | solution.py:494
  26.9 0.1 pad_add_fusion.place_ref
  26.9 1.3 group_scan.2
  28.2 0.0 copy-start.1
  28.3 0.7 copy-done.1
  29.0 20.3 %all-gather.1 = f32[12,128,128]{2,1,0:T(8,128)S(1)} all-gather(f32[3,128,128]{2,1,0:T(8,128)S(1)} %get-tuple-element.35), channel_id=3, replica_groups=mesh['zh'=4,'zl'=4,'x'=4,'y'=4,'core'=2] {'zl'}, dimensions={0}, use_global_device_ids=true | all-gather | bytes 983040 | tf_op jit(solution)/shard_map/all_gather | solution.py:506
  49.3 1.3 group_scan.3
  50.6 0.0 copy-start.2
  50.6 0.7 copy-done.2
  51.3 25.0 %all-gather.2 = f32[12,32,128]{2,1,0:T(8,128)S(1)} all-gather(f32[3,32,128]{2,1,0:T(8,128)S(1)} %get-tuple-element.36), channel_id=4, replica_groups=mesh['zh'=4,'zl'=4,'x'=4,'y'=4,'core'=2] {'zh'}, dimensions={0}, use_global_device_ids=true | all-gather | bytes 245760 | tf_op jit(solution)/shard_map/all_gather | solution.py:507
  76.3 14.5 %all-gather.3 = f32[16,3,32,128]{3,2,1,0:T(8,128)} all-gather(f32[4,3,32,128]{3,2,1,0:T(8,128)S(1)} %bitcast.14), channel_id=5, replica_groups=mesh['zh'=4,'zl'=4,'x'=4,'y'=4,'core'=2] {'x'}, dimensions={0}, use_global_device_ids=true | all-gather | bytes 983040 | tf_op jit(solution)/shard_map/all_gather | solution.py:507
  90.8 0.0 all-to-all-done.frames_any
  90.8 0.0 copy-done.3
  90.8 5.7 %finish.1 = (bf16[128,128]{1,0:T(8,128)(2,1)}, f32[4,264,128]{2,1,0:T(8,128)}, bf16[128,768]{1,0:T(8,128)(2,1)}) custom-call(s32[3]{0:T(128)} %copy-done.3, f32[4,4,3,32,128]{4,3,2,1,0:T(8,128)} %bitcast.13, f32[4,128,128]{2,1,0:T(8,128)} %copy-done.2, f32[4,128,128]{2,1,0:T(8,128)} %copy-done.1, f32[2176,128]{1,0:T(8,128)} %get-tuple-element.41.kept_any, ...), custom_call_target="tpu_custom_call" | custom-call | tf_op jit(solution)/shard_map/finish/pallas_call | solution.py:365
  96.5 0.0 copy-start.4
  96.5 3.8 %all-to-all-start.1 = ((f32[4,264,128]{2,1,0:T(8,128)}), f32[4,264,128]{2,1,0:T(8,128)S(1)}, u32[]{:S(2)}, u32[]{:S(2)}) async-start(f32[4,264,128]{2,1,0:T(8,128)} %get-tuple-element.43), calls=%async_computation.1 | async-start | bytes 1081344 | tf_op jit(solution)/shard_map/all_to_all | solution.py:494
  100.3 4.1 %side.1 = (f32[8,128,128]{2,1,0:T(8,128)}, bf16[4,128,1024]{2,1,0:T(8,128)(2,1)}) custom-call(bf16[128,768]{1,0:T(8,128)(2,1)} %get-tuple-element.44.tiles_any, bf16[2,1024]{1,0:T(2,128)(2,1)} %bitcast.17, bf16[1024,128]{1,0:T(8,128)(2,1)} %wq_any.3, bf16[1024,256]{1,0:T(8,128)(2,1)} %wk_any.3, bf16[1024,256]{1,0:T(8,128)(2,1)} %wv_any.3, ...), custom_call_target="tpu_custom_call" | custom-call | flops 170000000 | bytes 6000000 | tf_op jit(solution)/shard_map/side/pallas_call | solution.py:410
  104.4 4.0 %all-to-all-done.1.pieces_ref = f32[4,264,128]{2,1,0:T(8,128)S(1)} async-done(((f32[4,264,128]{2,1,0:T(8,128)}), f32[4,264,128]{2,1,0:T(8,128)S(1)}, u32[]{:S(2)}, u32[]{:S(2)}) %all-to-all-start.1) | async-done | bytes 540704 | tf_op jit(solution)/shard_map/all_to_all | solution.py:494
  108.5 0.0 copy-done.4
  108.5 1.2 copy-done
  109.7 1.1 weigh.1
  110.8 16.4 %all_to_all.30 = f32[4,328,128]{2,1,0:T(8,128)S(1)} all-to-all(f32[4,328,128]{2,1,0:T(8,128)S(1)} %weigh.1), channel_id=1, replica_groups=mesh['zh'=4,'zl'=4,'x'=4,'y'=4,'core'=2] {'zl'}, dimensions={0} | all-to-all | bytes 1343488 | tf_op jit(solution)/shard_map/all_to_all | solution.py:494
  127.3 19.6 %all_to_all.31 = f32[4,88,128]{2,1,0:T(8,128)S(1)} all-to-all(f32[4,88,128]{2,1,0:T(8,128)S(1)} %pad_maximum_fusion.1), channel_id=1, replica_groups=mesh['zh'=4,'zl'=4,'x'=4,'y'=4,'core'=2] {'zh'}, dimensions={0} | all-to-all | bytes 360448 | tf_op jit(solution)/shard_map/all_to_all | solution.py:494
  147.0 4.7 %all-to-all-start.4 = ((f32[8,128,128]{2,1,0:T(8,128)}), f32[8,128,128]{2,1,0:T(8,128)S(1)}, u32[]{:S(2)}, u32[]{:S(2)}) async-start(f32[8,128,128]{2,1,0:T(8,128)} %get-tuple-element.49), calls=%async_computation.4 | async-start | bytes 1048576 | tf_op jit(solution)/shard_map/all_to_all | solution.py:494
  151.7 31.9 %all-gather.4 = f32[1280,128]{1,0:T(8,128)S(1)} all-gather(f32[80,128]{1,0:T(8,128)S(1)} %slice.18), channel_id=6, replica_groups=mesh['zh'=4,'zl'=4,'x'=4,'y'=4,'core'=2] {'zh','zl'}, dimensions={0}, use_global_device_ids=true | all-gather | bytes 696320 | tf_op jit(solution)/shard_map/all_gather | solution.py:521
  183.6 0.0 all-to-all-done.4
  183.6 0.6 reduce_sum.29
  184.3 0.2 broadcast_in_dim.5
  184.5 28.4 %all_to_all.32.whole_ref = f32[4,1288,128]{2,1,0:T(8,128)S(1)} all-to-all(f32[4,1288,128]{2,1,0:T(8,128)S(1)} %broadcast_in_dim.5), channel_id=1, replica_groups=mesh['zh'=4,'zl'=4,'x'=4,'y'=4,'core'=2] {'x'}, dimensions={0} | all-to-all | bytes 5275648 | tf_op jit(solution)/shard_map/all_to_all | solution.py:490
  212.8 2.1 lay.1
  (11 shorter events, 0.1 us)
Async XLA Ops:
  22.4 68.4 %all-to-all-start = ((f32[4,128,1024]{2,1,0:T(8,128)}), f32[4,128,1024]{2,1,0:T(8,128)}, u32[]{:S(2)}, u32[]{:S(2)}) async-start(f32[4,128,1024]{2,1,0:T(8,128)} %get-tuple-element.37), calls=%async_computation | async-start | bytes 4194304 | tf_op jit(solution)/shard_map/all_to_all | solution.py:494
  26.9 63.8 %copy-start.3 = (s32[3]{0:T(128)}, s32[3]{0:T(128)S(1)}, u32[]{:S(2)}) copy-start(s32[3]{0:T(128)S(1)} %pad_add_fusion.place_ref) | copy-start | bytes 40
  28.2 0.7 copy-start.1
  50.6 0.7 copy-start.2
  96.5 12.0 %copy-start.4 = (s32[3]{0:T(128)S(1)}, s32[3]{0:T(128)}, u32[]{:S(2)}) copy-start(s32[3]{0:T(128)} %copy-done.3) | copy-start | bytes 40
  96.5 12.0 %all-to-all-start.1 = ((f32[4,264,128]{2,1,0:T(8,128)}), f32[4,264,128]{2,1,0:T(8,128)S(1)}, u32[]{:S(2)}, u32[]{:S(2)}) async-start(f32[4,264,128]{2,1,0:T(8,128)} %get-tuple-element.43), calls=%async_computation.1 | async-start | bytes 1081344 | tf_op jit(solution)/shard_map/all_to_all | solution.py:494
  108.5 1.2 copy-start
  147.0 36.6 %all-to-all-start.4 = ((f32[8,128,128]{2,1,0:T(8,128)}), f32[8,128,128]{2,1,0:T(8,128)S(1)}, u32[]{:S(2)}, u32[]{:S(2)}) async-start(f32[8,128,128]{2,1,0:T(8,128)} %get-tuple-element.49), calls=%async_computation.4 | async-start | bytes 1048576 | tf_op jit(solution)/shard_map/all_to_all | solution.py:494

commit v5 on v4

--- a/solution.py
+++ b/solution.py
@@ -14,19 +14,17 @@
 PARTS = 4
 KEPT_ROWS = (
     ("q", ROWS), ("k", REFL), ("v", REFL), ("w", REFL), ("u", REFL), ("qt", ROWS), ("pu", ROWS),
-    ("cols", REFL), ("z", REFL), ("yg", REFL),
+    ("cols", REFL),
 )
-KEPT, KEPT_SIZE = {}, 0
+KEPT, KEPT_PLACE, KEPT_SIZE = {}, {}, 0
 for _name, _rows in KEPT_ROWS:
     KEPT[_name] = slice(KEPT_SIZE, KEPT_SIZE + _rows)
+    KEPT_PLACE[_name] = pl.ds(KEPT_SIZE, _rows)
     KEPT_SIZE += _rows
 EPS = 1e-06
 EXTRA = 8
 LARGE_BYTES = 63 * 1024 * 1024
 SMALL_BYTES = 16 * 1024 * 1024
-FINISH_BYTES = LARGE_BYTES
-
-SIDE_BYTES = LARGE_BYTES
 
 
 def halves(a):
@@ -75,8 +73,8 @@
 
 def prepare_kernel(
     bias_ref, wb_ref, frames_any, wk_any, wq_any, wv_any, cot_any,
-    send_ref, kept_any, wide_any,
-    frames_ref, wk_ref, wq_ref, wv_ref, cot_ref, kept_ref, wide_ref, in_sems, out_sems,
+    send_any, kept_any, inner_any,
+    frames_ref, wk_ref, wq_ref, wv_ref, cot_ref, send_ref, kept_ref, inner_ref, in_sems, out_sems,
 ):
     arrive = fetch(
         (
@@ -91,8 +89,6 @@
 
     arrive[0].wait()
     frames = frames_ref[...]
-    wide_ref[...] = frames.astype(jnp.float32)
-    out_copies = fetch([(wide_ref, wide_any.at[i]) for i in range(PARTS)], out_sems)
     logits = dot(frames, wb_ref[...], 1, 1)
     arrive[1].wait()
     k_raw = dot(frames, wk_ref[...])
@@ -134,40 +130,74 @@
         ],
         axis=0,
     )
+    inner_ref[:REFL] = inverse
+    scores = jnp.where(seen_mask(), mm(q, k, 1, 1), 0.0)
+    inner_ref[REFL:] = scores
+    out_copies = fetch([(inner_ref, inner_any)], out_sems)
     wu = mm(inverse, jnp.concatenate([beta * k, beta * v], axis=1))
     w, u = wu[:, :DH], wu[:, DH:]
     keep("w", w)
     keep("u", u)
     kwu = mm(k, wu, 0, 0)
-    scores = jnp.where(seen_mask(), mm(q, k, 1, 1), 0.0)
     pwu = mm(scores, wu)
     qt = q - pwu[:, :DH]
     keep("qt", qt)
     keep("pu", pwu[:, DH:])
+    out_copies.append(pltpu.make_async_copy(kept_ref, kept_any, out_sems.at[1]))
+    out_copies[-1].start()
     cot = cot_ref[...].astype(jnp.float32)
     send_ref[0] = eye_like() - kwu[:, :DH]
     send_ref[1] = kwu[:, DH:]
     send_ref[2] = mm(cot, qt, 0, 0)
-    late = KEPT["z"].start
-    out_copies.append(
-        pltpu.make_async_copy(
-            kept_ref.at[pl.ds(0, late)], kept_any.at[pl.ds(0, late)], out_sems.at[PARTS]
-        )
-    )
-    out_copies[-1].start()
-    pg = mm(scores, cot, 0, 0)
-    zy = mm(inverse, jnp.concatenate([k, pg], axis=1), 0, 0)
-    keep("z", zy[:, :DH])
-    keep("yg", zy[:, DH:])
-    late_rows = pl.ds(late, KEPT_SIZE - late)
-    out_copies.append(
-        pltpu.make_async_copy(
-            kept_ref.at[late_rows], kept_any.at[late_rows], out_sems.at[PARTS + 1]
-        )
-    )
+    for i in range(PARTS):
+        out_copies.append(pltpu.make_async_copy(send_ref, send_any.at[i], out_sems.at[2 + i]))
+        out_copies[-1].start()
+    for copy in out_copies:
+        copy.wait()
+
+
+def rest_kernel(
+    inner_any, kept_any, cot_any, frames_any, late_any, wide_any,
+    inner_ref, k_ref, cot_ref, frames_ref, late_ref, wide_ref, in_sems, out_sems,
+):
+    arrive = fetch(
+        (
+            (frames_any, frames_ref), (inner_any, inner_ref), (kept_any.at[KEPT_PLACE["k"]], k_ref),
+            (cot_any, cot_ref),
+        ),
+        in_sems,
+    )
+    arrive[0].wait()
+    wide_ref[...] = frames_ref[...].astype(jnp.float32)
+    out_copies = fetch([(wide_ref, wide_any.at[i]) for i in range(PARTS)], out_sems)
+    for copy in arrive[1:]:
+        copy.wait()
+    cot = cot_ref[...].astype(jnp.float32)
+    pg = mm(inner_ref[REFL:], cot, 0, 0)
+    zy = mm(inner_ref[:REFL], jnp.concatenate([k_ref[...], pg], axis=1), 0, 0)
+    late_ref[:REFL] = zy[:, :DH]
+    late_ref[REFL:] = zy[:, DH:]
+    out_copies.append(pltpu.make_async_copy(late_ref, late_any, out_sems.at[PARTS]))
     out_copies[-1].start()
     for copy in out_copies:
         copy.wait()
+
+
+def rest(inner, kept, cotangent, frames):
+    late, wide = f32(2 * REFL, DH), f32(PARTS, ROWS, 1024)
+    return pl.pallas_call(
+        rest_kernel,
+        out_shape=(late, wide),
+        in_specs=[HBM] * 4,
+        out_specs=(HBM, HBM),
+        scratch_shapes=[
+            held(a) for a in (inner, f32(REFL, DH), cotangent, frames, late, f32(ROWS, 1024))
+        ]
+        + [pltpu.SemaphoreType.DMA((4,)), pltpu.SemaphoreType.DMA((PARTS + 1,))],
+        compiler_params=pltpu.CompilerParams(vmem_limit_bytes=LARGE_BYTES),
+        cost_estimate=pl.CostEstimate(flops=170_000_000, bytes_accessed=6_000_000, transcendentals=0),
+        name="rest",
+    )(inner, kept, cotangent, frames)
 
 
 def eye_like():
@@ -234,15 +264,15 @@
 
 
 def finish_kernel(
-    place_ref, far_any, near_any, own_any, kept_any, cot_any, frames_any,
+    place_ref, far_any, near_any, own_any, kept_any, late_any, cot_any, frames_any,
     out_ref, pieces_any, tiles_any,
-    far_ref, near_ref, own_ref, kept_ref, cot_ref, frames_ref, pieces_ref, tiles_ref,
+    far_ref, near_ref, own_ref, kept_ref, late_ref, cot_ref, frames_ref, pieces_ref, tiles_ref,
     in_sems, out_sems,
 ):
     arrive = fetch(
         (
             (far_any, far_ref), (near_any, near_ref), (own_any, own_ref), (kept_any, kept_ref),
-            (cot_any, cot_ref), (frames_any, frames_ref),
+            (late_any, late_ref), (cot_any, cot_ref), (frames_any, frames_ref),
         ),
         in_sems,
     )
@@ -251,7 +281,7 @@
     count = PARTS
 
     def far(group, which):
-        return jnp.concatenate([far_ref[i, group, which] for i in range(PARTS)], axis=0)
+        return jnp.concatenate([far_ref[group, i, which] for i in range(PARTS)], axis=0)
 
     entering = jnp.where(me > 0, far(0, 1), 0.0)
     for i in range(1, count - 1):
@@ -259,7 +289,7 @@
     leaving = jnp.where(me < count - 1, far(count - 1, 2), 0.0)
     for i in range(count - 2, 0, -1):
         leaving = jnp.where(me < i, mm(leaving, far(i, 0)) + far(i, 2), leaving)
-    for copy in arrive[1:5]:
+    for copy in arrive[1:6]:
         copy.wait()
     for around_ref in (near_ref, own_ref):
         entering = mm(around_ref[0], entering) + around_ref[1]
@@ -270,7 +300,7 @@
     beta, rk, rq = cols[:, 0:1], cols[:, 1:2], cols[:ROWS, 2:3]
     out_ref[...] = (mm(kept_ref[KEPT["qt"], :], entering) + kept_ref[KEPT["pu"], :]).astype(jnp.bfloat16)
     fresh = kept_ref[KEPT["u"], :] - mm(kept_ref[KEPT["w"], :], entering)
-    y = kept_ref[KEPT["yg"], :] + mm(kept_ref[KEPT["z"], :], leaving, 1, 1)
+    y = late_ref[REFL:] + mm(late_ref[:REFL], leaving, 1, 1)
     gram = mm(k, k, 1, 1)
     row, col = place((REFL, REFL), 0), place((REFL, REFL), 1)
     d_system = jnp.where(row > col, -mm(y, fresh, 1, 1), 0.0)
@@ -309,7 +339,7 @@
     tiles_ref[:, 5 * DH :] = padded.astype(jnp.bfloat16)
     tiles_copy = pltpu.make_async_copy(tiles_ref, tiles_any, out_sems.at[0])
     tiles_copy.start()
-    arrive[5].wait()
+    arrive[6].wait()
     wide = jnp.float32
     tiles = (g_query, g_keys[:, :DH], g_keys[:, DH:], g_values[:, :DH])
     shared = g_values[:, DH:].astype(wide)
@@ -346,13 +376,13 @@
 
 
 def prepare(bias, w_beta, *large):
-    kept, wide = f32(KEPT_SIZE, DH), f32(PARTS, ROWS, 1024)
+    send, kept, inner = f32(3, DH, DH), f32(KEPT_SIZE, DH), f32(REFL + ROWS, REFL)
     return pl.pallas_call(
         prepare_kernel,
-        out_shape=(f32(3, DH, DH), kept, wide),
+        out_shape=(f32(PARTS, 3, DH, DH), kept, inner),
         in_specs=[SMEM, VMEM] + [HBM] * 5,
-        out_specs=(VMEM, HBM, HBM),
-        scratch_shapes=[held(a) for a in (*large, kept, f32(ROWS, 1024))]
+        out_specs=(HBM, HBM, HBM),
+        scratch_shapes=[held(a) for a in (*large, send, kept, inner)]
         + [pltpu.SemaphoreType.DMA((5,)), pltpu.SemaphoreType.DMA((PARTS + 2,))],
         compiler_params=pltpu.CompilerParams(vmem_limit_bytes=LARGE_BYTES),
         name="prepare",
@@ -365,11 +395,11 @@
     return pl.pallas_call(
         finish_kernel,
         out_shape=(jax.ShapeDtypeStruct((ROWS, DH), jnp.bfloat16), pieces, tiles),
-        in_specs=[SMEM] + [HBM] * 6,
+        in_specs=[SMEM] + [HBM] * 7,
         out_specs=(VMEM, HBM, HBM),
         scratch_shapes=[held(a) for a in (*large, pieces, tiles)]
-        + [pltpu.SemaphoreType.DMA((6,)), pltpu.SemaphoreType.DMA((2,))],
-        compiler_params=pltpu.CompilerParams(vmem_limit_bytes=FINISH_BYTES),
+        + [pltpu.SemaphoreType.DMA((7,)), pltpu.SemaphoreType.DMA((2,))],
+        compiler_params=pltpu.CompilerParams(vmem_limit_bytes=LARGE_BYTES),
         name="finish",
     )(place, *large)
 
@@ -414,7 +444,7 @@
         out_specs=(HBM, HBM),
         scratch_shapes=[held(a) for a in (tiles, *large, part, narrow)]
         + [pltpu.SemaphoreType.DMA((5,)), pltpu.SemaphoreType.DMA((2,))],
-        compiler_params=pltpu.CompilerParams(vmem_limit_bytes=SIDE_BYTES),
+        compiler_params=pltpu.CompilerParams(vmem_limit_bytes=LARGE_BYTES),
         cost_estimate=pl.CostEstimate(flops=170_000_000, bytes_accessed=6_000_000, transcendentals=0),
         name="side",
     )(tiles, w_beta, *large)
@@ -449,7 +479,9 @@
     )(place, pieces, frames)
 
 
-def lay_kernel(whole_ref, query_any, keys_any, values_any, beta_ref, bias_ref, sems):
+def lay_kernel(
+    whole_ref, query_any, keys_any, values_any, beta_any, bias_any, beta_ref, bias_ref, sems
+):
     left, right = pl.ds(0, DH), pl.ds(DH, DH)
     full = pl.ds(0, 1024)
     pairs = [
@@ -468,6 +500,9 @@
         [row[2 * half : 2 * half + 2] for row in rows for half in range(2)], axis=1
     )
     bias_ref[...] = rows[0][4:5, :2]
+    for i, (a, b) in enumerate(((beta_ref, beta_any), (bias_ref, bias_any))):
+        copies.append(pltpu.make_async_copy(a, b, sems.at[8 + i]))
+        copies[-1].start()
     for copy in copies:
         copy.wait()
 
@@ -479,8 +514,8 @@
             f32(1024, DH), f32(1024, 2 * DH), f32(1024, 2 * DH), f32(2, 1024), f32(1, 2),
         ),
         in_specs=[VMEM],
-        out_specs=(HBM, HBM, HBM, VMEM, VMEM),
-        scratch_shapes=[pltpu.SemaphoreType.DMA((8,))],
+        out_specs=(HBM,) * 5,
+        scratch_shapes=[held(f32(2, 1024)), held(f32(1, 2)), pltpu.SemaphoreType.DMA((10,))],
         compiler_params=pltpu.CompilerParams(vmem_limit_bytes=SMALL_BYTES),
         name="lay",
     )(whole)
@@ -497,16 +532,19 @@
 def local(frames, w_query, w_keys, w_values, w_beta, beta_bias, cotangent):
     place = jnp.stack([lax.axis_index("x"), lax.axis_index("zl"), lax.axis_index("zh")])
     beta_turned = w_beta.T
-    own, kept, wide_frames = prepare(
+    own, kept, inner = prepare(
         beta_bias, beta_turned, frames, w_keys, w_query, w_values, cotangent
     )
-    row, wide_frames = lax.optimization_barrier((lax.all_gather(own, "x"), wide_frames))
+    late, wide_frames = rest(inner, kept, cotangent, frames)
+    row, wide_frames, late = lax.optimization_barrier((trade(own, "x"), wide_frames, late))
     group_frames = trade(wide_frames, "x")
     total, own_around = group_scan(row, place, 0, DH)
     total, near_around = group_scan(lax.all_gather(total, "zl"), place, 1, DH // PARTS)
-    far = lax.all_gather(lax.all_gather(total, "zh"), "x")
+    far = lax.all_gather(total, ("zh", "x")).reshape(PARTS, PARTS, 3, DH // PARTS, DH)
     far, group_frames = lax.optimization_barrier((far, group_frames))
-    outputs, pieces, tiles = finish(place, far, near_around, own_around, kept, cotangent, frames)
+    outputs, pieces, tiles = finish(
+        place, far, near_around, own_around, kept, late, cotangent, frames
+    )
     partial, group_frames = side(tiles, beta_turned, w_query, w_keys, w_values, group_frames)
     sums = weigh(place, trade(pieces, "x"), group_frames)
     part = jnp.sum(trade(sums, "zl"), axis=0)

time: 216 us -> 252 us (1.17)
  blocking collectives: 170 us -> 192 us
  waiting for transfers between devices: 4.05 us -> 13.8 us
  starting transfers between devices: 13 us -> 16.9 us
    all_to_all x2, blocking collectives: 36 us -> 47.1 us  [trade(): return lax.all_to_all(a, axis, 0, 0, tiled=True)]
    all_gather x3 -> x1, blocking collectives: 53.4 us -> 63.8 us  [local(): lax.all_gather(total, ('zh', 'x')).reshape(PARTS, PARTS, 3, DH // PARTS, DH)]
    all_to_all x3 -> x4, waiting for transfers between devices: 4.05 us -> 13.8 us  [trade(): return lax.all_to_all(a, axis, 0, 0, tiled=True)]
    all_to_all x3 -> x4, starting transfers between devices: 13 us -> 16.9 us  [trade(): return lax.all_to_all(a, axis, 0, 0, tiled=True)]
    pallas_call x1 -> x2, Pallas kernels: 7.88 us -> 9.31 us  [the longest x1 6.86 us: prepare(): pl.pallas_call(prepare_kernel, out_shape=(f32(PARTS, 3, DH, DH), kept, in...]
  transfers between devices with their start and end apart: 3 -> 4, of which waited for: 1 -> 2; matrix products, arithmetic and copies ran while one was open for 0% -> 0% of each run, Pallas kernels for 3% -> 4%
where the time goes in v5:
time: 252 us; the launch traced here: 251 us
  blocking collectives  192 us (76%)
  Pallas kernels  24.3 us (10%)
  starting transfers between devices  16.9 us (7%)
  waiting for transfers between devices  13.8 us (5%)
  local copies, waits for them, and re-layouts  2.83 us (1%)
    all_gather x1, blocking collectives, local(): lax.all_gather(total, ('zh', 'x')).reshape(PARTS, PARTS, 3, DH // PARTS, DH)  63.8 us
    all_to_all x2, blocking collectives, trade(): return lax.all_to_all(a, axis, 0, 0, tiled=True)  47.1 us
    all_gather x1, blocking collectives, local(): part = lax.all_gather(part, ('zh', 'zl')).reshape(1280, DH)  31.5 us
    all_to_all x1, blocking collectives, spread(): lax.all_to_all(jnp.broadcast_to(a[None], (PARTS, *a.shape)), axis, 0, 0,...  28.6 us
    all_gather x1, blocking collectives, local(): lax.all_gather(total, 'zl')  20.7 us
    all_to_all x4, starting transfers between devices, trade(): return lax.all_to_all(a, axis, 0, 0, tiled=True)  16.9 us
    all_to_all x4, waiting for transfers between devices, trade(): return lax.all_to_all(a, axis, 0, 0, tiled=True)  13.8 us
    pallas_call x1, Pallas kernels, prepare(): pl.pallas_call(prepare_kernel, out_shape=(f32(PARTS, 3, DH, DH), kept, in...  6.86 us
  transfers between devices with their start and end apart: 4, of which 2 were waited for; matrix products, arithmetic and copies ran while one was open for 0% of the time, Pallas kernels for 4%

profile of v5, /device:TPU:24, one launch (start us, length us, event | category | flops | bytes accessed | tf_op | source)
XLA Modules:
  0.0 251.2 jit_solution(13853756584310190174)
XLA Ops:
  0.6 6.9 %prepare.1 = (f32[4,3,128,128]{3,2,1,0:T(8,128)}, f32[1664,128]{1,0:T(8,128)}, f32[384,256]{1,0:T(8,128)}) custom-call(f32[2]{0:T(128)} %bias_ref.1, bf16[2,1024]{1,0:T(2,128)(2,1)} %bitcast.12, bf16[128,1024]{1,0:T(8,128)(2,1)} %frames_any.5, bf16[1024,256]{1,0:T(8,128)(2,1)} %wk_any.3, bf16[1024,128]{1,0:T(8,128)(2,1)} %wq_any.3, ...), custom_call_target="tpu_custom_call" | custom-call | tf_op jit(solution)/shard_map/prepare/pallas_call | solution.py:380
  7.5 4.3 %all-to-all-start = ((f32[4,3,128,128]{3,2,1,0:T(8,128)}), f32[4,3,128,128]{3,2,1,0:T(8,128)S(1)}, u32[]{:S(2)}, u32[]{:S(2)}) async-start(f32[4,3,128,128]{3,2,1,0:T(8,128)} %get-tuple-element.35), calls=%async_computation | async-start | bytes 1572864 | tf_op jit(solution)/shard_map/all_to_all | solution.py:529
  11.8 2.5 rest.1
  14.3 9.8 %all-to-all-done.parts_ref = f32[4,3,128,128]{3,2,1,0:T(8,128)S(1)} async-done(((f32[4,3,128,128]{3,2,1,0:T(8,128)}), f32[4,3,128,128]{3,2,1,0:T(8,128)S(1)}, u32[]{:S(2)}, u32[]{:S(2)}) %all-to-all-start) | async-done | bytes 786464 | tf_op jit(solution)/shard_map/all_to_all | solution.py:529
  24.1 4.4 %all-to-all-start.1 = ((f32[4,128,1024]{2,1,0:T(8,128)}), f32[4,128,1024]{2,1,0:T(8,128)}, u32[]{:S(2)}, u32[]{:S(2)}) async-start(f32[4,128,1024]{2,1,0:T(8,128)} %get-tuple-element.43), calls=%async_computation.1 | async-start | bytes 4194304 | tf_op jit(solution)/shard_map/all_to_all | solution.py:529
  28.6 0.1 pad_add_fusion.place_ref
  28.6 1.3 group_scan.2
  29.9 0.0 copy-start.1
  29.9 0.7 copy-done.1
  30.6 20.7 %all-gather = f32[12,128,128]{2,1,0:T(8,128)S(1)} all-gather(f32[3,128,128]{2,1,0:T(8,128)S(1)} %get-tuple-element.41), channel_id=2, replica_groups=mesh['zh'=4,'zl'=4,'x'=4,'y'=4,'core'=2] {'zl'}, dimensions={0}, use_global_device_ids=true | all-gather | bytes 983040 | tf_op jit(solution)/shard_map/all_gather | solution.py:542
  51.3 1.3 group_scan.3
  52.6 0.0 copy-start.2
  52.6 0.7 copy-done.2
  53.3 63.8 %all-gather.1 = f32[48,32,128]{2,1,0:T(8,128)} all-gather(f32[3,32,128]{2,1,0:T(8,128)S(1)} %get-tuple-element.42), channel_id=3, replica_groups=mesh['zh'=4,'zl'=4,'x'=4,'y'=4,'core'=2] {'zh','x'}, dimensions={0}, use_global_device_ids=true | all-gather | bytes 835584 | tf_op jit(solution)/shard_map/all_gather | solution.py:543
  117.1 0.0 all-to-all-done.1.frames_any
  117.1 0.0 copy-done.3
  117.1 5.6 %finish.1 = (bf16[128,128]{1,0:T(8,128)(2,1)}, f32[4,264,128]{2,1,0:T(8,128)}, bf16[128,768]{1,0:T(8,128)(2,1)}) custom-call(s32[3]{0:T(128)} %copy-done.3, f32[4,4,3,32,128]{4,3,2,1,0:T(8,128)} %bitcast.10, f32[4,128,128]{2,1,0:T(8,128)} %copy-done.2, f32[4,128,128]{2,1,0:T(8,128)} %copy-done.1, f32[1664,128]{1,0:T(8,128)} %get-tuple-element.37.kept_any, ...), custom_call_target="tpu_custom_call" | custom-call | tf_op jit(solution)/shard_map/finish/pallas_call | solution.py:395
  122.8 0.0 copy-start.4
  122.8 3.5 %all-to-all-start.2 = ((f32[4,264,128]{2,1,0:T(8,128)}), f32[4,264,128]{2,1,0:T(8,128)S(1)}, u32[]{:S(2)}, u32[]{:S(2)}) async-start(f32[4,264,128]{2,1,0:T(8,128)} %get-tuple-element.49), calls=%async_computation.2 | async-start | bytes 1081344 | tf_op jit(solution)/shard_map/all_to_all | solution.py:529
  126.3 4.1 %side.1 = (f32[8,128,128]{2,1,0:T(8,128)}, bf16[4,128,1024]{2,1,0:T(8,128)(2,1)}) custom-call(bf16[128,768]{1,0:T(8,128)(2,1)} %get-tuple-element.50.tiles_any, bf16[2,1024]{1,0:T(2,128)(2,1)} %bitcast.13, bf16[1024,128]{1,0:T(8,128)(2,1)} %wq_any.3, bf16[1024,256]{1,0:T(8,128)(2,1)} %wk_any.3, bf16[1024,256]{1,0:T(8,128)(2,1)} %wv_any.3, ...), custom_call_target="tpu_custom_call" | custom-call | flops 170000000 | bytes 6000000 | tf_op jit(solution)/shard_map/side/pallas_call | solution.py:440
  130.4 4.0 %all-to-all-done.2.pieces_ref = f32[4,264,128]{2,1,0:T(8,128)S(1)} async-done(((f32[4,264,128]{2,1,0:T(8,128)}), f32[4,264,128]{2,1,0:T(8,128)S(1)}, u32[]{:S(2)}, u32[]{:S(2)}) %all-to-all-start.2) | async-done | bytes 540704 | tf_op jit(solution)/shard_map/all_to_all | solution.py:529
  134.4 1.2 copy-done
  135.7 1.1 weigh.1
  136.7 17.9 %all_to_all.35 = f32[4,328,128]{2,1,0:T(8,128)S(1)} all-to-all(f32[4,328,128]{2,1,0:T(8,128)S(1)} %weigh.1), channel_id=1, replica_groups=mesh['zh'=4,'zl'=4,'x'=4,'y'=4,'core'=2] {'zl'}, dimensions={0} | all-to-all | bytes 1343488 | tf_op jit(solution)/shard_map/all_to_all | solution.py:529
  154.8 29.2 %all_to_all.36 = f32[4,88,128]{2,1,0:T(8,128)S(1)} all-to-all(f32[4,88,128]{2,1,0:T(8,128)S(1)} %pad_maximum_fusion.1), channel_id=1, replica_groups=mesh['zh'=4,'zl'=4,'x'=4,'y'=4,'core'=2] {'zh'}, dimensions={0} | all-to-all | bytes 360448 | tf_op jit(solution)/shard_map/all_to_all | solution.py:529
  184.0 4.7 %all-to-all-start.5 = ((f32[8,128,128]{2,1,0:T(8,128)}), f32[8,128,128]{2,1,0:T(8,128)S(1)}, u32[]{:S(2)}, u32[]{:S(2)}) async-start(f32[8,128,128]{2,1,0:T(8,128)} %get-tuple-element.55), calls=%async_computation.5 | async-start | bytes 1048576 | tf_op jit(solution)/shard_map/all_to_all | solution.py:529
  188.7 31.5 %all-gather.2 = f32[1280,128]{1,0:T(8,128)S(1)} all-gather(f32[80,128]{1,0:T(8,128)S(1)} %slice.18), channel_id=4, replica_groups=mesh['zh'=4,'zl'=4,'x'=4,'y'=4,'core'=2] {'zh','zl'}, dimensions={0}, use_global_device_ids=true | all-gather | bytes 696320 | tf_op jit(solution)/shard_map/all_gather | solution.py:559
  220.2 0.0 all-to-all-done.5
  220.2 0.6 reduce_sum.29
  220.8 0.2 broadcast_in_dim.5
  221.0 28.6 %all_to_all.37.whole_ref = f32[4,1288,128]{2,1,0:T(8,128)S(1)} all-to-all(f32[4,1288,128]{2,1,0:T(8,128)S(1)} %broadcast_in_dim.5), channel_id=1, replica_groups=mesh['zh'=4,'zl'=4,'x'=4,'y'=4,'core'=2] {'x'}, dimensions={0} | all-to-all | bytes 5275648 | tf_op jit(solution)/shard_map/all_to_all | solution.py:525
  249.6 1.6 lay.1
  (12 shorter events, 0.1 us)
Async XLA Ops:
  7.5 16.6 %all-to-all-start = ((f32[4,3,128,128]{3,2,1,0:T(8,128)}), f32[4,3,128,128]{3,2,1,0:T(8,128)S(1)}, u32[]{:S(2)}, u32[]{:S(2)}) async-start(f32[4,3,128,128]{3,2,1,0:T(8,128)} %get-tuple-element.35), calls=%async_computation | async-start | bytes 1572864 | tf_op jit(solution)/shard_map/all_to_all | solution.py:529
  24.1 93.0 %all-to-all-start.1 = ((f32[4,128,1024]{2,1,0:T(8,128)}), f32[4,128,1024]{2,1,0:T(8,128)}, u32[]{:S(2)}, u32[]{:S(2)}) async-start(f32[4,128,1024]{2,1,0:T(8,128)} %get-tuple-element.43), calls=%async_computation.1 | async-start | bytes 4194304 | tf_op jit(solution)/shard_map/all_to_all | solution.py:529
  28.6 88.5 %copy-start.3 = (s32[3]{0:T(128)}, s32[3]{0:T(128)S(1)}, u32[]{:S(2)}) copy-start(s32[3]{0:T(128)S(1)} %pad_add_fusion.place_ref) | copy-start | bytes 40
  29.9 0.7 copy-start.1
  52.6 0.7 copy-start.2
  122.8 11.6 %copy-start.4 = (s32[3]{0:T(128)S(1)}, s32[3]{0:T(128)}, u32[]{:S(2)}) copy-start(s32[3]{0:T(128)} %copy-done.3) | copy-start | bytes 40
  122.8 11.6 %all-to-all-start.2 = ((f32[4,264,128]{2,1,0:T(8,128)}), f32[4,264,128]{2,1,0:T(8,128)S(1)}, u32[]{:S(2)}, u32[]{:S(2)}) async-start(f32[4,264,128]{2,1,0:T(8,128)} %get-tuple-element.49), calls=%async_computation.2 | async-start | bytes 1081344 | tf_op jit(solution)/shard_map/all_to_all | solution.py:529
  134.4 1.2 copy-start
  184.0 36.2 %all-to-all-start.5 = ((f32[8,128,128]{2,1,0:T(8,128)}), f32[8,128,128]{2,1,0:T(8,128)S(1)}, u32[]{:S(2)}, u32[]{:S(2)}) async-start(f32[8,128,128]{2,1,0:T(8,128)} %get-tuple-element.55), calls=%async_computation.5 | async-start | bytes 1048576 | tf_op jit(solution)/shard_map/all_to_all | solution.py:529

commit v6 on v5

--- a/solution.py
+++ b/solution.py
@@ -277,23 +277,24 @@
         in_sems,
     )
     me = place_ref[2]
-    arrive[0].wait()
-    count = PARTS
+    for copy in arrive[:6]:
+        copy.wait()
+    inward = mm(own_ref[0], jnp.concatenate([near_ref[0], near_ref[1]], axis=1))
+    inward_map, inward_shift = inward[:, :DH], inward[:, DH:] + own_ref[1]
+    outward = mm(jnp.concatenate([near_ref[2], near_ref[3]], axis=0), own_ref[2])
+    outward_map, outward_shift = outward[:DH], outward[DH:] + own_ref[3]
 
     def far(group, which):
-        return jnp.concatenate([far_ref[group, i, which] for i in range(PARTS)], axis=0)
+        return jnp.concatenate([far_ref[i, group, which] for i in range(PARTS)], axis=0)
 
     entering = jnp.where(me > 0, far(0, 1), 0.0)
-    for i in range(1, count - 1):
+    leaving = jnp.where(me < PARTS - 1, far(PARTS - 1, 2), 0.0)
+    for i in range(1, PARTS - 1):
+        j = PARTS - 1 - i
         entering = jnp.where(me > i, mm(far(i, 0), entering) + far(i, 1), entering)
-    leaving = jnp.where(me < count - 1, far(count - 1, 2), 0.0)
-    for i in range(count - 2, 0, -1):
-        leaving = jnp.where(me < i, mm(leaving, far(i, 0)) + far(i, 2), leaving)
-    for copy in arrive[1:6]:
-        copy.wait()
-    for around_ref in (near_ref, own_ref):
-        entering = mm(around_ref[0], entering) + around_ref[1]
-        leaving = mm(leaving, around_ref[2]) + around_ref[3]
+        leaving = jnp.where(me < j, mm(leaving, far(j, 0)) + far(j, 2), leaving)
+    entering = mm(inward_map, entering) + inward_shift
+    leaving = mm(leaving, outward_map) + outward_shift
     q, k, v = kept_ref[KEPT["q"], :], kept_ref[KEPT["k"], :], kept_ref[KEPT["v"], :]
     cot = cot_ref[...].astype(jnp.float32)
     cols = kept_ref[KEPT["cols"], :]
@@ -480,7 +481,8 @@
 
 
 def lay_kernel(
-    whole_ref, query_any, keys_any, values_any, beta_any, bias_any, beta_ref, bias_ref, sems
+    whole_ref, heads_ref, query_any, keys_any, values_any, beta_any, bias_any, frames_any,
+    beta_ref, bias_ref, sum_ref, sems,
 ):
     left, right = pl.ds(0, DH), pl.ds(DH, DH)
     full = pl.ds(0, 1024)
@@ -500,25 +502,33 @@
         [row[2 * half : 2 * half + 2] for row in rows for half in range(2)], axis=1
     )
     bias_ref[...] = rows[0][4:5, :2]
-    for i, (a, b) in enumerate(((beta_ref, beta_any), (bias_ref, bias_any))):
+    total = heads_ref[0]
+    for i in range(1, heads_ref.shape[0]):
+        total = total + heads_ref[i]
+    sum_ref[...] = total.astype(jnp.bfloat16)
+    small = ((beta_ref, beta_any), (bias_ref, bias_any), (sum_ref, frames_any))
+    for i, (a, b) in enumerate(small):
         copies.append(pltpu.make_async_copy(a, b, sems.at[8 + i]))
         copies[-1].start()
     for copy in copies:
         copy.wait()
 
 
-def lay(whole):
+def lay(whole, heads):
+    frames = jax.ShapeDtypeStruct((ROWS, DH), jnp.bfloat16)
     return pl.pallas_call(
         lay_kernel,
         out_shape=(
-            f32(1024, DH), f32(1024, 2 * DH), f32(1024, 2 * DH), f32(2, 1024), f32(1, 2),
+            f32(1024, DH), f32(1024, 2 * DH), f32(1024, 2 * DH), f32(2, 1024), f32(1, 2), frames,
         ),
-        in_specs=[VMEM],
-        out_specs=(HBM,) * 5,
-        scratch_shapes=[held(f32(2, 1024)), held(f32(1, 2)), pltpu.SemaphoreType.DMA((10,))],
+        in_specs=[VMEM, VMEM],
+        out_specs=(HBM,) * 6,
+        scratch_shapes=[
+            held(f32(2, 1024)), held(f32(1, 2)), held(frames), pltpu.SemaphoreType.DMA((11,)),
+        ],
         compiler_params=pltpu.CompilerParams(vmem_limit_bytes=SMALL_BYTES),
         name="lay",
-    )(whole)
+    )(whole, heads)
 
 
 def spread(a, axis):
@@ -540,7 +550,7 @@
     group_frames = trade(wide_frames, "x")
     total, own_around = group_scan(row, place, 0, DH)
     total, near_around = group_scan(lax.all_gather(total, "zl"), place, 1, DH // PARTS)
-    far = lax.all_gather(total, ("zh", "x")).reshape(PARTS, PARTS, 3, DH // PARTS, DH)
+    far = lax.all_gather(lax.all_gather(total, "zh"), "x")
     far, group_frames = lax.optimization_barrier((far, group_frames))
     outputs, pieces, tiles = finish(
         place, far, near_around, own_around, kept, late, cotangent, frames
@@ -557,10 +567,11 @@
     part, partial = lax.optimization_barrier((part, partial))
     partial = trade(partial, ("y", "core"))
     part = lax.all_gather(part, ("zh", "zl")).reshape(1280, DH)
-    grad_frames = jnp.sum(partial, axis=0).astype(jnp.bfloat16)
-    part, grad_frames = lax.optimization_barrier((part, grad_frames))
+    part, partial = lax.optimization_barrier((part, partial))
     whole = jnp.concatenate([part, extra], axis=0)
-    grad_query, grad_keys, grad_values, beta_rows, bias_row = lay(spread(whole, "x"))
+    grad_query, grad_keys, grad_values, beta_rows, bias_row, grad_frames = lay(
+        spread(whole, "x"), partial
+    )
     grad_beta = beta_rows.T
     grad_bias = bias_row.reshape(2)
     return (outputs, grad_frames, grad_query, grad_keys, grad_values, grad_beta, grad_bias)

time: 252 us -> 217 us (0.86)
  blocking collectives: 192 us -> 156 us
    all_gather x1 -> x2, blocking collectives: 63.8 us -> 39 us  [local(): far = lax.all_gather(lax.all_gather(total, 'zh'), 'x')]
    all_to_all x2, blocking collectives: 47.1 us -> 36.4 us  [trade(): return lax.all_to_all(a, axis, 0, 0, tiled=True)]
where the time goes in v6:
time: 217 us; the launch traced here: 216 us
  blocking collectives  156 us (72%)
  Pallas kernels  24.6 us (11%)
  starting transfers between devices  17.2 us (8%)
  waiting for transfers between devices  13.9 us (6%)
  local copies, waits for them, and re-layouts  2.85 us (1%)
    all_gather x2, blocking collectives, local(): far = lax.all_gather(lax.all_gather(total, 'zh'), 'x')  39 us
    all_to_all x2, blocking collectives, trade(): return lax.all_to_all(a, axis, 0, 0, tiled=True)  36.4 us
    all_gather x1, blocking collectives, local(): part = lax.all_gather(part, ('zh', 'zl')).reshape(1280, DH)  31.9 us
    all_to_all x1, blocking collectives, spread(): lax.all_to_all(jnp.broadcast_to(a[None], (PARTS, *a.shape)), axis, 0, 0,...  28.4 us
    all_gather x1, blocking collectives, local(): lax.all_gather(total, 'zl')  20.7 us
    all_to_all x4, starting transfers between devices, trade(): return lax.all_to_all(a, axis, 0, 0, tiled=True)  17.2 us
    all_to_all x4, waiting for transfers between devices, trade(): return lax.all_to_all(a, axis, 0, 0, tiled=True)  13.9 us
    pallas_call x1, Pallas kernels, prepare(): pl.pallas_call(prepare_kernel, out_shape=(f32(PARTS, 3, DH, DH), kept, in...  6.86 us
  transfers between devices with their start and end apart: 4, of which 2 were waited for; matrix products, arithmetic and copies ran while one was open for 0% of the time, Pallas kernels for 4%

profile of v6, /device:TPU:24, one launch (start us, length us, event | category | flops | bytes accessed | tf_op | source)
XLA Modules:
  0.0 215.8 jit_solution(17623636428360734578)
XLA Ops:
  0.6 6.9 %prepare.1 = (f32[4,3,128,128]{3,2,1,0:T(8,128)}, f32[1664,128]{1,0:T(8,128)}, f32[384,256]{1,0:T(8,128)}) custom-call(f32[2]{0:T(128)} %bias_ref.1, bf16[2,1024]{1,0:T(2,128)(2,1)} %bitcast.14, bf16[128,1024]{1,0:T(8,128)(2,1)} %frames_any.5, bf16[1024,256]{1,0:T(8,128)(2,1)} %wk_any.3, bf16[1024,128]{1,0:T(8,128)(2,1)} %wq_any.3, ...), custom_call_target="tpu_custom_call" | custom-call | tf_op jit(solution)/shard_map/prepare/pallas_call | solution.py:381
  7.5 4.3 %all-to-all-start = ((f32[4,3,128,128]{3,2,1,0:T(8,128)}), f32[4,3,128,128]{3,2,1,0:T(8,128)S(1)}, u32[]{:S(2)}, u32[]{:S(2)}) async-start(f32[4,3,128,128]{3,2,1,0:T(8,128)} %get-tuple-element.36), calls=%async_computation | async-start | bytes 1572864 | tf_op jit(solution)/shard_map/all_to_all | solution.py:539
  11.8 2.5 %rest.1 = (f32[512,128]{1,0:T(8,128)}, f32[4,128,1024]{2,1,0:T(8,128)}) custom-call(f32[384,256]{1,0:T(8,128)} %get-tuple-element.37.inner_any, f32[1664,128]{1,0:T(8,128)} %get-tuple-element.38.kept_any, bf16[128,128]{1,0:T(8,128)(2,1)} %cot_any.5, bf16[128,1024]{1,0:T(8,128)(2,1)} %frames_any.5), custom_call_target="tpu_custom_call" | custom-call | flops 170000000 | bytes 6000000 | tf_op jit(solution)/shard_map/rest/pallas_call | solution.py:188
  14.3 9.8 %all-to-all-done.parts_ref = f32[4,3,128,128]{3,2,1,0:T(8,128)S(1)} async-done(((f32[4,3,128,128]{3,2,1,0:T(8,128)}), f32[4,3,128,128]{3,2,1,0:T(8,128)S(1)}, u32[]{:S(2)}, u32[]{:S(2)}) %all-to-all-start) | async-done | bytes 786464 | tf_op jit(solution)/shard_map/all_to_all | solution.py:539
  24.1 4.4 %all-to-all-start.1 = ((f32[4,128,1024]{2,1,0:T(8,128)}), f32[4,128,1024]{2,1,0:T(8,128)}, u32[]{:S(2)}, u32[]{:S(2)}) async-start(f32[4,128,1024]{2,1,0:T(8,128)} %get-tuple-element.44), calls=%async_computation.1 | async-start | bytes 4194304 | tf_op jit(solution)/shard_map/all_to_all | solution.py:539
  28.6 0.1 pad_add_fusion.place_ref
  28.6 1.3 group_scan.2
  29.9 0.0 copy-start.1
  29.9 0.7 copy-done.1
  30.7 20.7 %all-gather = f32[12,128,128]{2,1,0:T(8,128)S(1)} all-gather(f32[3,128,128]{2,1,0:T(8,128)S(1)} %get-tuple-element.42), channel_id=2, replica_groups=mesh['zh'=4,'zl'=4,'x'=4,'y'=4,'core'=2] {'zl'}, dimensions={0}, use_global_device_ids=true | all-gather | bytes 983040 | tf_op jit(solution)/shard_map/all_gather | solution.py:552
  51.3 1.3 group_scan.3
  52.6 0.0 copy-start.2
  52.7 0.7 copy-done.2
  53.3 24.6 %all-gather.1 = f32[12,32,128]{2,1,0:T(8,128)S(1)} all-gather(f32[3,32,128]{2,1,0:T(8,128)S(1)} %get-tuple-element.43), channel_id=3, replica_groups=mesh['zh'=4,'zl'=4,'x'=4,'y'=4,'core'=2] {'zh'}, dimensions={0}, use_global_device_ids=true | all-gather | bytes 245760 | tf_op jit(solution)/shard_map/all_gather | solution.py:553
  78.0 14.3 %all-gather.2 = f32[16,3,32,128]{3,2,1,0:T(8,128)} all-gather(f32[4,3,32,128]{3,2,1,0:T(8,128)S(1)} %bitcast.12), channel_id=4, replica_groups=mesh['zh'=4,'zl'=4,'x'=4,'y'=4,'core'=2] {'x'}, dimensions={0}, use_global_device_ids=true | all-gather | bytes 983040 | tf_op jit(solution)/shard_map/all_gather | solution.py:553
  92.3 0.0 all-to-all-done.1.frames_any
  92.3 0.0 copy-done.3
  92.4 5.9 %finish.1 = (bf16[128,128]{1,0:T(8,128)(2,1)}, f32[4,264,128]{2,1,0:T(8,128)}, bf16[128,768]{1,0:T(8,128)(2,1)}) custom-call(s32[3]{0:T(128)} %copy-done.3, f32[4,4,3,32,128]{4,3,2,1,0:T(8,128)} %bitcast.11, f32[4,128,128]{2,1,0:T(8,128)} %copy-done.2, f32[4,128,128]{2,1,0:T(8,128)} %copy-done.1, f32[1664,128]{1,0:T(8,128)} %get-tuple-element.38.kept_any, ...), custom_call_target="tpu_custom_call" | custom-call | tf_op jit(solution)/shard_map/finish/pallas_call | solution.py:396
  98.3 0.0 copy-start.4
  98.3 3.7 %all-to-all-start.2 = ((f32[4,264,128]{2,1,0:T(8,128)}), f32[4,264,128]{2,1,0:T(8,128)S(1)}, u32[]{:S(2)}, u32[]{:S(2)}) async-start(f32[4,264,128]{2,1,0:T(8,128)} %get-tuple-element.50), calls=%async_computation.2 | async-start | bytes 1081344 | tf_op jit(solution)/shard_map/all_to_all | solution.py:539
  102.0 4.1 %side.1 = (f32[8,128,128]{2,1,0:T(8,128)}, bf16[4,128,1024]{2,1,0:T(8,128)(2,1)}) custom-call(bf16[128,768]{1,0:T(8,128)(2,1)} %get-tuple-element.51.tiles_any, bf16[2,1024]{1,0:T(2,128)(2,1)} %bitcast.15, bf16[1024,128]{1,0:T(8,128)(2,1)} %wq_any.3, bf16[1024,256]{1,0:T(8,128)(2,1)} %wk_any.3, bf16[1024,256]{1,0:T(8,128)(2,1)} %wv_any.3, ...), custom_call_target="tpu_custom_call" | custom-call | flops 170000000 | bytes 6000000 | tf_op jit(solution)/shard_map/side/pallas_call | solution.py:441
  106.1 4.0 %all-to-all-done.2.pieces_ref = f32[4,264,128]{2,1,0:T(8,128)S(1)} async-done(((f32[4,264,128]{2,1,0:T(8,128)}), f32[4,264,128]{2,1,0:T(8,128)S(1)}, u32[]{:S(2)}, u32[]{:S(2)}) %all-to-all-start.2) | async-done | bytes 540704 | tf_op jit(solution)/shard_map/all_to_all | solution.py:539
  110.2 1.2 copy-done
  111.4 1.1 weigh.1
  112.5 17.2 %all_to_all.35 = f32[4,328,128]{2,1,0:T(8,128)S(1)} all-to-all(f32[4,328,128]{2,1,0:T(8,128)S(1)} %weigh.1), channel_id=1, replica_groups=mesh['zh'=4,'zl'=4,'x'=4,'y'=4,'core'=2] {'zl'}, dimensions={0} | all-to-all | bytes 1343488 | tf_op jit(solution)/shard_map/all_to_all | solution.py:539
  129.8 19.2 %all_to_all.36 = f32[4,88,128]{2,1,0:T(8,128)S(1)} all-to-all(f32[4,88,128]{2,1,0:T(8,128)S(1)} %pad_maximum_fusion.1), channel_id=1, replica_groups=mesh['zh'=4,'zl'=4,'x'=4,'y'=4,'core'=2] {'zh'}, dimensions={0} | all-to-all | bytes 360448 | tf_op jit(solution)/shard_map/all_to_all | solution.py:539
  149.1 4.7 %all-to-all-start.5 = ((f32[8,128,128]{2,1,0:T(8,128)}), f32[8,128,128]{2,1,0:T(8,128)S(1)}, u32[]{:S(2)}, u32[]{:S(2)}) async-start(f32[8,128,128]{2,1,0:T(8,128)} %get-tuple-element.56), calls=%async_computation.5 | async-start | bytes 1048576 | tf_op jit(solution)/shard_map/all_to_all | solution.py:539
  153.8 31.9 %all-gather.3 = f32[1280,128]{1,0:T(8,128)S(1)} all-gather(f32[80,128]{1,0:T(8,128)S(1)} %slice.18), channel_id=5, replica_groups=mesh['zh'=4,'zl'=4,'x'=4,'y'=4,'core'=2] {'zh','zl'}, dimensions={0}, use_global_device_ids=true | all-gather | bytes 696320 | tf_op jit(solution)/shard_map/all_gather | solution.py:569
  185.7 0.0 all-to-all-done.5.heads_ref
  185.7 0.2 broadcast_in_dim.5
  185.9 28.4 %all_to_all.37.whole_ref = f32[4,1288,128]{2,1,0:T(8,128)S(1)} all-to-all(f32[4,1288,128]{2,1,0:T(8,128)S(1)} %broadcast_in_dim.5), channel_id=1, replica_groups=mesh['zh'=4,'zl'=4,'x'=4,'y'=4,'core'=2] {'x'}, dimensions={0} | all-to-all | bytes 5275648 | tf_op jit(solution)/shard_map/all_to_all | solution.py:535
  214.3 1.6 lay.1
  (12 shorter events, 0.1 us)
Async XLA Ops:
  7.5 16.6 %all-to-all-start = ((f32[4,3,128,128]{3,2,1,0:T(8,128)}), f32[4,3,128,128]{3,2,1,0:T(8,128)S(1)}, u32[]{:S(2)}, u32[]{:S(2)}) async-start(f32[4,3,128,128]{3,2,1,0:T(8,128)} %get-tuple-element.36), calls=%async_computation | async-start | bytes 1572864 | tf_op jit(solution)/shard_map/all_to_all | solution.py:539
  24.1 68.3 %all-to-all-start.1 = ((f32[4,128,1024]{2,1,0:T(8,128)}), f32[4,128,1024]{2,1,0:T(8,128)}, u32[]{:S(2)}, u32[]{:S(2)}) async-start(f32[4,128,1024]{2,1,0:T(8,128)} %get-tuple-element.44), calls=%async_computation.1 | async-start | bytes 4194304 | tf_op jit(solution)/shard_map/all_to_all | solution.py:539
  28.6 63.7 %copy-start.3 = (s32[3]{0:T(128)}, s32[3]{0:T(128)S(1)}, u32[]{:S(2)}) copy-start(s32[3]{0:T(128)S(1)} %pad_add_fusion.place_ref) | copy-start | bytes 40
  29.9 0.7 copy-start.1
  52.6 0.7 copy-start.2
  98.3 11.9 %copy-start.4 = (s32[3]{0:T(128)S(1)}, s32[3]{0:T(128)}, u32[]{:S(2)}) copy-start(s32[3]{0:T(128)} %copy-done.3) | copy-start | bytes 40
  98.3 11.9 %all-to-all-start.2 = ((f32[4,264,128]{2,1,0:T(8,128)}), f32[4,264,128]{2,1,0:T(8,128)S(1)}, u32[]{:S(2)}, u32[]{:S(2)}) async-start(f32[4,264,128]{2,1,0:T(8,128)} %get-tuple-element.50), calls=%async_computation.2 | async-start | bytes 1081344 | tf_op jit(solution)/shard_map/all_to_all | solution.py:539
  110.2 1.2 copy-start
  149.1 36.6 %all-to-all-start.5 = ((f32[8,128,128]{2,1,0:T(8,128)}), f32[8,128,128]{2,1,0:T(8,128)S(1)}, u32[]{:S(2)}, u32[]{:S(2)}) async-start(f32[8,128,128]{2,1,0:T(8,128)} %get-tuple-element.56), calls=%async_computation.5 | async-start | bytes 1048576 | tf_op jit(solution)/shard_map/all_to_all | solution.py:539

commit v7 on v6

--- a/solution.py
+++ b/solution.py
@@ -13,13 +13,12 @@
 REFL = 256
 PARTS = 4
 KEPT_ROWS = (
-    ("q", ROWS), ("k", REFL), ("v", REFL), ("w", REFL), ("u", REFL), ("qt", ROWS), ("pu", ROWS),
-    ("cols", REFL),
+    ("q", ROWS), ("k", REFL), ("v", REFL), ("w", REFL), ("u", REFL), ("z", REFL), ("yg", REFL),
+    ("cols", REFL), ("cot", ROWS), ("qt", ROWS), ("pu", ROWS), ("own", 4 * DH), ("near", 4 * DH),
 )
-KEPT, KEPT_PLACE, KEPT_SIZE = {}, {}, 0
+KEPT, KEPT_SIZE = {}, 0
 for _name, _rows in KEPT_ROWS:
     KEPT[_name] = slice(KEPT_SIZE, KEPT_SIZE + _rows)
-    KEPT_PLACE[_name] = pl.ds(KEPT_SIZE, _rows)
     KEPT_SIZE += _rows
 EPS = 1e-06
 EXTRA = 8
@@ -73,8 +72,8 @@
 
 def prepare_kernel(
     bias_ref, wb_ref, frames_any, wk_any, wq_any, wv_any, cot_any,
-    send_any, kept_any, inner_any,
-    frames_ref, wk_ref, wq_ref, wv_ref, cot_ref, send_ref, kept_ref, inner_ref, in_sems, out_sems,
+    send_any, kept_any, wide_any,
+    frames_ref, wk_ref, wq_ref, wv_ref, cot_ref, send_ref, kept_ref, wide_ref, in_sems, out_sems,
 ):
     arrive = fetch(
         (
@@ -89,6 +88,8 @@
 
     arrive[0].wait()
     frames = frames_ref[...]
+    wide_ref[...] = frames.astype(jnp.float32)
+    out_copies = fetch([(wide_ref, wide_any.at[i]) for i in range(PARTS)], out_sems)
     logits = dot(frames, wb_ref[...], 1, 1)
     arrive[1].wait()
     k_raw = dot(frames, wk_ref[...])
@@ -130,74 +131,37 @@
         ],
         axis=0,
     )
-    inner_ref[:REFL] = inverse
-    scores = jnp.where(seen_mask(), mm(q, k, 1, 1), 0.0)
-    inner_ref[REFL:] = scores
-    out_copies = fetch([(inner_ref, inner_any)], out_sems)
     wu = mm(inverse, jnp.concatenate([beta * k, beta * v], axis=1))
     w, u = wu[:, :DH], wu[:, DH:]
     keep("w", w)
     keep("u", u)
+    cot = cot_ref[...].astype(jnp.float32)
+    keep("cot", cot)
+    scores = jnp.where(seen_mask(), mm(q, k, 1, 1), 0.0)
+    pg = mm(scores, cot, 0, 0)
+    zy = mm(inverse, jnp.concatenate([k, pg], axis=1), 0, 0)
+    keep("z", zy[:, :DH])
+    keep("yg", zy[:, DH:])
+    first, second = pl.ds(0, KEPT["qt"].start), pl.ds(KEPT["qt"].start, 2 * ROWS)
+    out_copies.append(
+        pltpu.make_async_copy(kept_ref.at[first], kept_any.at[first], out_sems.at[PARTS])
+    )
+    out_copies[-1].start()
     kwu = mm(k, wu, 0, 0)
     pwu = mm(scores, wu)
     qt = q - pwu[:, :DH]
     keep("qt", qt)
     keep("pu", pwu[:, DH:])
-    out_copies.append(pltpu.make_async_copy(kept_ref, kept_any, out_sems.at[1]))
-    out_copies[-1].start()
-    cot = cot_ref[...].astype(jnp.float32)
     send_ref[0] = eye_like() - kwu[:, :DH]
     send_ref[1] = kwu[:, DH:]
     send_ref[2] = mm(cot, qt, 0, 0)
-    for i in range(PARTS):
-        out_copies.append(pltpu.make_async_copy(send_ref, send_any.at[i], out_sems.at[2 + i]))
+    for i, (a, b) in enumerate(
+        ((send_ref, send_any), (kept_ref.at[second], kept_any.at[second]))
+    ):
+        out_copies.append(pltpu.make_async_copy(a, b, out_sems.at[PARTS + 1 + i]))
         out_copies[-1].start()
     for copy in out_copies:
         copy.wait()
-
-
-def rest_kernel(
-    inner_any, kept_any, cot_any, frames_any, late_any, wide_any,
-    inner_ref, k_ref, cot_ref, frames_ref, late_ref, wide_ref, in_sems, out_sems,
-):
-    arrive = fetch(
-        (
-            (frames_any, frames_ref), (inner_any, inner_ref), (kept_any.at[KEPT_PLACE["k"]], k_ref),
-            (cot_any, cot_ref),
-        ),
-        in_sems,
-    )
-    arrive[0].wait()
-    wide_ref[...] = frames_ref[...].astype(jnp.float32)
-    out_copies = fetch([(wide_ref, wide_any.at[i]) for i in range(PARTS)], out_sems)
-    for copy in arrive[1:]:
-        copy.wait()
-    cot = cot_ref[...].astype(jnp.float32)
-    pg = mm(inner_ref[REFL:], cot, 0, 0)
-    zy = mm(inner_ref[:REFL], jnp.concatenate([k_ref[...], pg], axis=1), 0, 0)
-    late_ref[:REFL] = zy[:, :DH]
-    late_ref[REFL:] = zy[:, DH:]
-    out_copies.append(pltpu.make_async_copy(late_ref, late_any, out_sems.at[PARTS]))
-    out_copies[-1].start()
-    for copy in out_copies:
-        copy.wait()
-
-
-def rest(inner, kept, cotangent, frames):
-    late, wide = f32(2 * REFL, DH), f32(PARTS, ROWS, 1024)
-    return pl.pallas_call(
-        rest_kernel,
-        out_shape=(late, wide),
-        in_specs=[HBM] * 4,
-        out_specs=(HBM, HBM),
-        scratch_shapes=[
-            held(a) for a in (inner, f32(REFL, DH), cotangent, frames, late, f32(ROWS, 1024))
-        ]
-        + [pltpu.SemaphoreType.DMA((4,)), pltpu.SemaphoreType.DMA((PARTS + 1,))],
-        compiler_params=pltpu.CompilerParams(vmem_limit_bytes=LARGE_BYTES),
-        cost_estimate=pl.CostEstimate(flops=170_000_000, bytes_accessed=6_000_000, transcendentals=0),
-        name="rest",
-    )(inner, kept, cotangent, frames)
 
 
 def eye_like():
@@ -227,12 +191,16 @@
     return whole, (before[:, :DH], before[:, DH:], after[:DH], after[DH:])
 
 
-def group_kernel(place_ref, parts_ref, total_ref, around_any, whole_ref, around_ref, sem, *, axis):
+def group_kernel(
+    place_ref, parts_ref, kept_in, total_ref, kept_any, whole_ref, around_ref, sem, *, axis, name
+):
+    del kept_in
     parts = [tuple(parts_ref[i, j] for j in range(3)) for i in range(PARTS)]
     whole, around = compose_group(place_ref[axis], parts)
     for i, value in enumerate(around):
-        around_ref[i] = value
-    copy = pltpu.make_async_copy(around_ref, around_any, sem)
+        around_ref[DH * i : DH * i + DH] = value
+    rows = pl.ds(KEPT[name].start, 4 * DH)
+    copy = pltpu.make_async_copy(around_ref, kept_any.at[rows], sem)
     copy.start()
     if total_ref.shape[1] == DH:
         for i, value in enumerate(whole):
@@ -247,38 +215,27 @@
     copy.wait()
 
 
-def group_scan(parts, place, axis, rows):
-    return pl.pallas_call(
-        functools.partial(group_kernel, axis=axis),
-        out_shape=(f32(3, rows, DH), f32(4, DH, DH)),
-        in_specs=[SMEM, VMEM],
+def group_scan(parts, kept, place, axis, name, rows):
+    return pl.pallas_call(
+        functools.partial(group_kernel, axis=axis, name=name),
+        out_shape=(f32(3, rows, DH), kept),
+        in_specs=[SMEM, VMEM, HBM],
         out_specs=(VMEM, HBM),
         scratch_shapes=[
             pltpu.VMEM((3, DH, DH), jnp.float32),
-            pltpu.VMEM((4, DH, DH), jnp.float32),
+            pltpu.VMEM((4 * DH, DH), jnp.float32),
             pltpu.SemaphoreType.DMA,
         ],
+        input_output_aliases={2: 1},
         compiler_params=pltpu.CompilerParams(vmem_limit_bytes=SMALL_BYTES),
         name="group_scan",
-    )(place, parts)
-
-
-def finish_kernel(
-    place_ref, far_any, near_any, own_any, kept_any, late_any, cot_any, frames_any,
-    out_ref, pieces_any, tiles_any,
-    far_ref, near_ref, own_ref, kept_ref, late_ref, cot_ref, frames_ref, pieces_ref, tiles_ref,
-    in_sems, out_sems,
-):
-    arrive = fetch(
-        (
-            (far_any, far_ref), (near_any, near_ref), (own_any, own_ref), (kept_any, kept_ref),
-            (late_any, late_ref), (cot_any, cot_ref), (frames_any, frames_ref),
-        ),
-        in_sems,
-    )
+    )(place, parts, kept)
+
+
+def finish_kernel(place_ref, far_ref, kept_ref, out_ref, pieces_ref, tiles_ref):
     me = place_ref[2]
-    for copy in arrive[:6]:
-        copy.wait()
+    own_ref = kept_ref[KEPT["own"], :].reshape(4, DH, DH)
+    near_ref = kept_ref[KEPT["near"], :].reshape(4, DH, DH)
     inward = mm(own_ref[0], jnp.concatenate([near_ref[0], near_ref[1]], axis=1))
     inward_map, inward_shift = inward[:, :DH], inward[:, DH:] + own_ref[1]
     outward = mm(jnp.concatenate([near_ref[2], near_ref[3]], axis=0), own_ref[2])
@@ -296,12 +253,12 @@
     entering = mm(inward_map, entering) + inward_shift
     leaving = mm(leaving, outward_map) + outward_shift
     q, k, v = kept_ref[KEPT["q"], :], kept_ref[KEPT["k"], :], kept_ref[KEPT["v"], :]
-    cot = cot_ref[...].astype(jnp.float32)
+    cot = kept_ref[KEPT["cot"], :]
     cols = kept_ref[KEPT["cols"], :]
     beta, rk, rq = cols[:, 0:1], cols[:, 1:2], cols[:ROWS, 2:3]
     out_ref[...] = (mm(kept_ref[KEPT["qt"], :], entering) + kept_ref[KEPT["pu"], :]).astype(jnp.bfloat16)
     fresh = kept_ref[KEPT["u"], :] - mm(kept_ref[KEPT["w"], :], entering)
-    y = late_ref[REFL:] + mm(late_ref[:REFL], leaving, 1, 1)
+    y = kept_ref[KEPT["yg"], :] + mm(kept_ref[KEPT["z"], :], leaving, 1, 1)
     gram = mm(k, k, 1, 1)
     row, col = place((REFL, REFL), 0), place((REFL, REFL), 1)
     d_system = jnp.where(row > col, -mm(y, fresh, 1, 1), 0.0)
@@ -331,20 +288,16 @@
     v_first, v_second = unmix(by)
     g_keys = jnp.concatenate([k_first, k_second], axis=1).astype(jnp.bfloat16)
     g_values = jnp.concatenate([v_first, v_second], axis=1).astype(jnp.bfloat16)
-    g_logits = g_logits_f32.astype(jnp.bfloat16)
     tiles_ref[:, :DH] = g_query
     tiles_ref[:, DH : 3 * DH] = g_keys
     tiles_ref[:, 3 * DH : 5 * DH] = g_values
     lane = lax.broadcasted_iota(jnp.int32, (ROWS, DH), 1)
     padded = jnp.where(lane == 0, l_first, jnp.where(lane == 1, l_second, 0.0))
     tiles_ref[:, 5 * DH :] = padded.astype(jnp.bfloat16)
-    tiles_copy = pltpu.make_async_copy(tiles_ref, tiles_any, out_sems.at[0])
-    tiles_copy.start()
-    arrive[6].wait()
     wide = jnp.float32
     tiles = (g_query, g_keys[:, :DH], g_keys[:, DH:], g_values[:, :DH])
     shared = g_values[:, DH:].astype(wide)
-    beta_rows = dot(g_logits, frames_ref[...], 0, 0)
+    turned = padded.astype(jnp.bfloat16).astype(wide).T
     bias_row = jnp.sum(g_logits_f32, axis=0, keepdims=True)
     bias_lanes = jnp.where(
         lax.broadcasted_iota(jnp.int32, (1, DH), 1) == 0, bias_row[:, 0:1], bias_row[:, 1:2]
@@ -352,14 +305,9 @@
     for i in range(PARTS):
         pieces_ref[i, :ROWS] = tiles[i].astype(wide)
         pieces_ref[i, ROWS : 2 * ROWS] = shared
-        span = beta_rows[:, 256 * i : 256 * i + 256]
         pieces_ref[i, 2 * ROWS :] = jnp.concatenate(
-            [span[:, :DH], span[:, DH:], bias_lanes, jnp.zeros((EXTRA - 5, DH), wide)], axis=0
+            [turned[:2], bias_lanes, jnp.zeros((EXTRA - 3, DH), wide)], axis=0
         )
-    pieces_copy = pltpu.make_async_copy(pieces_ref, pieces_any, out_sems.at[1])
-    pieces_copy.start()
-    tiles_copy.wait()
-    pieces_copy.wait()
 
 
 def f32(*shape):
@@ -377,50 +325,36 @@
 
 
 def prepare(bias, w_beta, *large):
-    send, kept, inner = f32(3, DH, DH), f32(KEPT_SIZE, DH), f32(REFL + ROWS, REFL)
+    send, kept, wide = f32(3, DH, DH), f32(KEPT_SIZE, DH), f32(PARTS, ROWS, 1024)
     return pl.pallas_call(
         prepare_kernel,
-        out_shape=(f32(PARTS, 3, DH, DH), kept, inner),
+        out_shape=(send, kept, wide),
         in_specs=[SMEM, VMEM] + [HBM] * 5,
         out_specs=(HBM, HBM, HBM),
-        scratch_shapes=[held(a) for a in (*large, send, kept, inner)]
-        + [pltpu.SemaphoreType.DMA((5,)), pltpu.SemaphoreType.DMA((PARTS + 2,))],
+        scratch_shapes=[
+            held(a) for a in (*large, send, f32(KEPT["own"].start, DH), f32(ROWS, 1024))
+        ]
+        + [pltpu.SemaphoreType.DMA((5,)), pltpu.SemaphoreType.DMA((PARTS + 3,))],
         compiler_params=pltpu.CompilerParams(vmem_limit_bytes=LARGE_BYTES),
         name="prepare",
     )(bias, w_beta, *large)
 
 
-def finish(place, *large):
-    pieces = f32(PARTS, 2 * ROWS + EXTRA, DH)
-    tiles = jax.ShapeDtypeStruct((ROWS, 6 * DH), jnp.bfloat16)
+def finish(place, far, kept):
     return pl.pallas_call(
         finish_kernel,
-        out_shape=(jax.ShapeDtypeStruct((ROWS, DH), jnp.bfloat16), pieces, tiles),
-        in_specs=[SMEM] + [HBM] * 7,
-        out_specs=(VMEM, HBM, HBM),
-        scratch_shapes=[held(a) for a in (*large, pieces, tiles)]
-        + [pltpu.SemaphoreType.DMA((7,)), pltpu.SemaphoreType.DMA((2,))],
-        compiler_params=pltpu.CompilerParams(vmem_limit_bytes=LARGE_BYTES),
+        out_shape=(
+            jax.ShapeDtypeStruct((ROWS, DH), jnp.bfloat16),
+            f32(PARTS, 2 * ROWS + EXTRA, DH),
+            jax.ShapeDtypeStruct((ROWS, 6 * DH), jnp.bfloat16),
+        ),
+        in_specs=[SMEM, VMEM, VMEM],
+        compiler_params=pltpu.CompilerParams(vmem_limit_bytes=SMALL_BYTES),
         name="finish",
-    )(place, *large)
-
-
-def side_kernel(
-    tiles_any, wb_ref, wq_any, wk_any, wv_any, frames_any, part_any, narrow_any,
-    tiles_ref, wq_ref, wk_ref, wv_ref, frames_ref, part_ref, narrow_ref, in_sems, out_sems,
-):
-    arrive = fetch(
-        (
-            (frames_any, frames_ref), (tiles_any, tiles_ref), (wq_any, wq_ref), (wk_any, wk_ref),
-            (wv_any, wv_ref),
-        ),
-        in_sems,
-    )
-    arrive[0].wait()
-    narrow_ref[...] = frames_ref[...].astype(jnp.bfloat16)
-    out_copies = fetch([(narrow_ref, narrow_any)], out_sems)
-    for copy in arrive[1:]:
-        copy.wait()
+    )(place, far, kept)
+
+
+def side_kernel(tiles_ref, wb_ref, wq_ref, wk_ref, wv_ref, part_ref):
     part = (
         dot(tiles_ref[:, :DH], wq_ref[...], 1, 1)
         + dot(tiles_ref[:, DH : 3 * DH], wk_ref[...], 1, 1)
@@ -429,38 +363,49 @@
     )
     for i in range(8):
         part_ref[i] = part[:, DH * i : DH * i + DH]
-    out_copies.append(pltpu.make_async_copy(part_ref, part_any, out_sems.at[1]))
-    out_copies[1].start()
-    for copy in out_copies:
-        copy.wait()
-
-
-def side(tiles, w_beta, *large):
-    part = f32(8, ROWS, DH)
-    narrow = jax.ShapeDtypeStruct((PARTS, ROWS, 1024), jnp.bfloat16)
+
+
+def side(*args):
     return pl.pallas_call(
         side_kernel,
-        out_shape=(part, narrow),
-        in_specs=[HBM, VMEM] + [HBM] * 4,
-        out_specs=(HBM, HBM),
-        scratch_shapes=[held(a) for a in (tiles, *large, part, narrow)]
-        + [pltpu.SemaphoreType.DMA((5,)), pltpu.SemaphoreType.DMA((2,))],
-        compiler_params=pltpu.CompilerParams(vmem_limit_bytes=LARGE_BYTES),
-        cost_estimate=pl.CostEstimate(flops=170_000_000, bytes_accessed=6_000_000, transcendentals=0),
+        out_shape=f32(8, ROWS, DH),
+        compiler_params=pltpu.CompilerParams(vmem_limit_bytes=SMALL_BYTES),
+        cost_estimate=pl.CostEstimate(flops=170_000_000, bytes_accessed=3_000_000, transcendentals=0),
         name="side",
-    )(tiles, w_beta, *large)
+    )(*args)
+
+
+def narrow_kernel(frames_ref, narrow_ref):
+    narrow_ref[...] = frames_ref[...].astype(jnp.bfloat16)
+
+
+def narrow(frames):
+    return pl.pallas_call(
+        narrow_kernel,
+        out_shape=jax.ShapeDtypeStruct(frames.shape, jnp.bfloat16),
+        in_specs=[VMEM],
+        out_specs=VMEM,
+        compiler_params=pltpu.CompilerParams(vmem_limit_bytes=SMALL_BYTES),
+        cost_estimate=pl.CostEstimate(flops=1_000_000, bytes_accessed=3_000_000, transcendentals=0),
+        name="narrow",
+    )(frames)
 
 
 def weigh_kernel(place_ref, pieces_ref, frames_ref, sums_ref):
     quarter = pl.ds(pl.multiple_of(place_ref[0] * 256, 256), 256)
     total = jnp.zeros((1024, DH), jnp.float32)
     corner = jnp.zeros((256, DH), jnp.float32)
-    extra = jnp.zeros((EXTRA, DH), jnp.float32)
+    beta = jnp.zeros((2, 256), jnp.float32)
+    bias = jnp.zeros((1, DH), jnp.float32)
     for i in range(PARTS):
         piece = pieces_ref[i, : 2 * ROWS].astype(jnp.bfloat16)
-        extra = extra + pieces_ref[i, 2 * ROWS :]
+        rows = pieces_ref[i, 2 * ROWS :]
+        bias = bias + rows[2:3]
+        beta = beta + dot(rows[:2].astype(jnp.bfloat16), frames_ref[i, :, quarter])
         total = total + dot(frames_ref[i], piece[:ROWS], 0, 0)
         corner = corner + dot(frames_ref[i, :, quarter], piece[ROWS:], 0, 0)
+    extra = [beta[:, :DH], beta[:, DH:], bias, jnp.zeros((EXTRA - 5, DH), jnp.float32)]
+    extra = jnp.concatenate(extra, axis=0)
     total = jnp.concatenate([total, corner], axis=0)
     rows = total.shape[0] // (PARTS * PARTS)
     for i in range(PARTS):
@@ -542,21 +487,17 @@
 def local(frames, w_query, w_keys, w_values, w_beta, beta_bias, cotangent):
     place = jnp.stack([lax.axis_index("x"), lax.axis_index("zl"), lax.axis_index("zh")])
     beta_turned = w_beta.T
-    own, kept, inner = prepare(
+    own, kept, wide_frames = prepare(
         beta_bias, beta_turned, frames, w_keys, w_query, w_values, cotangent
     )
-    late, wide_frames = rest(inner, kept, cotangent, frames)
-    row, wide_frames, late = lax.optimization_barrier((trade(own, "x"), wide_frames, late))
+    row, wide_frames = lax.optimization_barrier((lax.all_gather(own, "x"), wide_frames))
     group_frames = trade(wide_frames, "x")
-    total, own_around = group_scan(row, place, 0, DH)
-    total, near_around = group_scan(lax.all_gather(total, "zl"), place, 1, DH // PARTS)
+    total, kept = group_scan(row, kept, place, 0, "own", DH)
+    total, kept = group_scan(lax.all_gather(total, "zl"), kept, place, 1, "near", DH // PARTS)
     far = lax.all_gather(lax.all_gather(total, "zh"), "x")
-    far, group_frames = lax.optimization_barrier((far, group_frames))
-    outputs, pieces, tiles = finish(
-        place, far, near_around, own_around, kept, late, cotangent, frames
-    )
-    partial, group_frames = side(tiles, beta_turned, w_query, w_keys, w_values, group_frames)
-    sums = weigh(place, trade(pieces, "x"), group_frames)
+    outputs, pieces, tiles = finish(place, far, kept)
+    partial = side(tiles, beta_turned, w_query, w_keys, w_values)
+    sums = weigh(place, trade(pieces, "x"), narrow(group_frames))
     part = jnp.sum(trade(sums, "zl"), axis=0)
     part, extra = part[:320], part[320:]
     part = jnp.concatenate(

time: 217 us -> 209 us (0.963)
  blocking collectives: 156 us -> 149 us
  Pallas kernels: 24.6 us -> 18.6 us
  waiting for transfers between devices: 13.9 us -> 18.5 us
  starting transfers between devices: 17.2 us -> 20.2 us
  local copies, waits for them, and re-layouts: 2.85 us -> 0.23 us
    all_to_all x2 -> x1, blocking collectives: 36.4 us -> 15.8 us  [trade(): return lax.all_to_all(a, axis, 0, 0, tiled=True)]
    all_gather x0 -> x1, blocking collectives: none -> 13.9 us  [local(): lax.all_gather(own, 'x')]
    all_to_all x4, waiting for transfers between devices: 13.9 us -> 18.5 us  [trade(): return lax.all_to_all(a, axis, 0, 0, tiled=True)]
    pallas_call x5, Pallas kernels: 16 us -> 12.6 us  [the longest x1 6.89 us: prepare(): pl.pallas_call(prepare_kernel, out_shape=(send, kept, wide), in_specs=[SM...]
    all_to_all x4, starting transfers between devices: 17.2 us -> 20.2 us  [trade(): return lax.all_to_all(a, axis, 0, 0, tiled=True)]
    unnamed x10, local copies, waits for them, and re-layouts: 2.65 us -> 0.03 us
    pallas_call x1, Pallas kernels: 5.92 us -> 3.31 us  [finish(): pl.pallas_call(finish_kernel, out_shape=(jax.ShapeDtypeStruct((ROWS, DH),...]
where the time goes in v7:
time: 209 us; the launch traced here: 208 us
  blocking collectives  149 us (71%)
  starting transfers between devices  20.2 us (10%)
  Pallas kernels  18.6 us (9%)
  waiting for transfers between devices  18.5 us (9%)
    all_gather x2, blocking collectives, local(): far = lax.all_gather(lax.all_gather(total, 'zh'), 'x')  39.1 us
    all_gather x1, blocking collectives, local(): part = lax.all_gather(part, ('zh', 'zl')).reshape(1280, DH)  31 us
    all_to_all x1, blocking collectives, spread(): lax.all_to_all(jnp.broadcast_to(a[None], (PARTS, *a.shape)), axis, 0, 0,...  28.6 us
    all_gather x1, blocking collectives, local(): lax.all_gather(total, 'zl')  20.3 us
    all_to_all x4, starting transfers between devices, trade(): return lax.all_to_all(a, axis, 0, 0, tiled=True)  20.2 us
    all_to_all x4, waiting for transfers between devices, trade(): return lax.all_to_all(a, axis, 0, 0, tiled=True)  18.5 us
    all_to_all x1, blocking collectives, trade(): return lax.all_to_all(a, axis, 0, 0, tiled=True)  15.8 us
    all_gather x1, blocking collectives, local(): lax.all_gather(own, 'x')  13.9 us
  transfers between devices with their start and end apart: 4, of which 2 were waited for; matrix products, arithmetic and copies ran while one was open for 0% of the time, Pallas kernels for 4%

profile of v7, /device:TPU:24, one launch (start us, length us, event | category | flops | bytes accessed | tf_op | source)
XLA Modules:
  0.0 208.0 jit_solution(5212422969961729968)
XLA Ops:
  0.6 6.9 %prepare.1 = (f32[3,128,128]{2,1,0:T(8,128)}, f32[3328,128]{1,0:T(8,128)}, f32[4,128,1024]{2,1,0:T(8,128)}) custom-call(f32[2]{0:T(128)} %bias_ref.1, bf16[2,1024]{1,0:T(2,128)(2,1)} %bitcast.14, bf16[128,1024]{1,0:T(8,128)(2,1)} %frames_any.1, bf16[1024,256]{1,0:T(8,128)(2,1)} %wk_ref.1, bf16[1024,128]{1,0:T(8,128)(2,1)} %wq_ref.1, ...), custom_call_target="tpu_custom_call" | custom-call | tf_op jit(solution)/shard_map/prepare/pallas_call | solution.py:329
  7.5 13.9 %all-gather = f32[12,128,128]{2,1,0:T(8,128)S(1)} all-gather(f32[3,128,128]{2,1,0:T(8,128)} %get-tuple-element.29), channel_id=2, replica_groups=mesh['zh'=4,'zl'=4,'x'=4,'y'=4,'core'=2] {'x'}, dimensions={0}, use_global_device_ids=true | all-gather | bytes 983040 | tf_op jit(solution)/shard_map/all_gather | solution.py:493
  21.4 4.6 %all-to-all-start.1 = ((f32[4,128,1024]{2,1,0:T(8,128)}), f32[4,128,1024]{2,1,0:T(8,128)}, u32[]{:S(2)}, u32[]{:S(2)}) async-start(f32[4,128,1024]{2,1,0:T(8,128)} %get-tuple-element.39), calls=%async_computation.1 | async-start | bytes 4194304 | tf_op jit(solution)/shard_map/all_to_all | solution.py:484
  26.0 0.1 pad_add_fusion.place_ref
  26.1 0.0 copy-done
  26.1 1.3 group_scan.2
  27.4 20.3 %all-gather.1 = f32[12,128,128]{2,1,0:T(8,128)S(1)} all-gather(f32[3,128,128]{2,1,0:T(8,128)S(1)} %get-tuple-element.33), channel_id=3, replica_groups=mesh['zh'=4,'zl'=4,'x'=4,'y'=4,'core'=2] {'zl'}, dimensions={0}, use_global_device_ids=true | all-gather | bytes 983040 | tf_op jit(solution)/shard_map/all_gather | solution.py:496
  47.7 1.3 group_scan.3
  49.0 25.3 %all-gather.2 = f32[12,32,128]{2,1,0:T(8,128)S(1)} all-gather(f32[3,32,128]{2,1,0:T(8,128)S(1)} %get-tuple-element.35), channel_id=4, replica_groups=mesh['zh'=4,'zl'=4,'x'=4,'y'=4,'core'=2] {'zh'}, dimensions={0}, use_global_device_ids=true | all-gather | bytes 245760 | tf_op jit(solution)/shard_map/all_gather | solution.py:497
  74.3 13.9 %all-gather.3 = f32[16,3,32,128]{3,2,1,0:T(8,128)S(1)} all-gather(f32[4,3,32,128]{3,2,1,0:T(8,128)S(1)} %bitcast.16), channel_id=5, replica_groups=mesh['zh'=4,'zl'=4,'x'=4,'y'=4,'core'=2] {'x'}, dimensions={0}, use_global_device_ids=true | all-gather | bytes 983040 | tf_op jit(solution)/shard_map/all_gather | solution.py:497
  88.1 3.3 %finish.1 = (bf16[128,128]{1,0:T(8,128)(2,1)}, f32[4,264,128]{2,1,0:T(8,128)}, bf16[128,768]{1,0:T(8,128)(2,1)S(1)}) custom-call(s32[3]{0:T(128)S(1)} %pad_add_fusion.place_ref, f32[4,4,3,32,128]{4,3,2,1,0:T(8,128)S(1)} %bitcast.12, f32[3328,128]{1,0:T(8,128)S(1)} %get-tuple-element.36.kept_ref), custom_call_target="tpu_custom_call" | custom-call | tf_op jit(solution)/shard_map/finish/pallas_call | solution.py:344
  91.5 0.0 all-to-all-done.1.frames_ref
  91.5 4.6 %all-to-all-start = ((f32[4,264,128]{2,1,0:T(8,128)}), f32[4,264,128]{2,1,0:T(8,128)S(1)}, u32[]{:S(2)}, u32[]{:S(2)}) async-start(f32[4,264,128]{2,1,0:T(8,128)} %get-tuple-element.38), calls=%async_computation | async-start | bytes 1081344 | tf_op jit(solution)/shard_map/all_to_all | solution.py:484
  96.1 1.7 narrow.1.frames_ref
  97.8 6.5 %all-to-all-done.pieces_ref = f32[4,264,128]{2,1,0:T(8,128)S(1)} async-done(((f32[4,264,128]{2,1,0:T(8,128)}), f32[4,264,128]{2,1,0:T(8,128)S(1)}, u32[]{:S(2)}, u32[]{:S(2)}) %all-to-all-start) | async-done | bytes 540704 | tf_op jit(solution)/shard_map/all_to_all | solution.py:484
  104.2 1.1 weigh.1
  105.4 0.0 copy-start.1
  105.4 0.0 copy-start.2
  105.4 0.0 copy-start.3
  105.4 0.0 copy-start.4
  105.4 15.8 %all_to_all.30 = f32[4,328,128]{2,1,0:T(8,128)S(1)} all-to-all(f32[4,328,128]{2,1,0:T(8,128)S(1)} %weigh.1), channel_id=1, replica_groups=mesh['zh'=4,'zl'=4,'x'=4,'y'=4,'core'=2] {'zl'}, dimensions={0} | all-to-all | bytes 1343488 | tf_op jit(solution)/shard_map/all_to_all | solution.py:484
  121.3 0.7 pad_maximum_fusion.1
  122.0 6.3 %all-to-all-start.3 = ((f32[4,88,128]{2,1,0:T(8,128)}), f32[4,88,128]{2,1,0:T(8,128)S(1)}, u32[]{:S(2)}, u32[]{:S(2)}) async-start(f32[4,88,128]{2,1,0:T(8,128)} %pad_maximum_fusion.1), calls=%async_computation.3 | async-start | bytes 360448 | tf_op jit(solution)/shard_map/all_to_all | solution.py:484
  128.3 0.0 copy-done.3
  128.3 1.4 side.1
  129.7 12.0 %all-to-all-done.3 = f32[4,88,128]{2,1,0:T(8,128)S(1)} async-done(((f32[4,88,128]{2,1,0:T(8,128)}), f32[4,88,128]{2,1,0:T(8,128)S(1)}, u32[]{:S(2)}, u32[]{:S(2)}) %all-to-all-start.3) | async-done | bytes 180256 | tf_op jit(solution)/shard_map/all_to_all | solution.py:484
  141.8 4.7 %all-to-all-start.4 = ((f32[8,128,128]{2,1,0:T(8,128)}), f32[8,128,128]{2,1,0:T(8,128)S(1)}, u32[]{:S(2)}, u32[]{:S(2)}) async-start(f32[8,128,128]{2,1,0:T(8,128)} %side.1), calls=%async_computation.4 | async-start | bytes 1048576 | tf_op jit(solution)/shard_map/all_to_all | solution.py:484
  146.5 31.0 %all-gather.4 = f32[1280,128]{1,0:T(8,128)S(1)} all-gather(f32[80,128]{1,0:T(8,128)S(1)} %slice.18), channel_id=6, replica_groups=mesh['zh'=4,'zl'=4,'x'=4,'y'=4,'core'=2] {'zh','zl'}, dimensions={0}, use_global_device_ids=true | all-gather | bytes 696320 | tf_op jit(solution)/shard_map/all_gather | solution.py:510
  177.5 0.0 all-to-all-done.4.heads_ref
  177.6 0.2 broadcast_in_dim.5
  177.8 28.6 %all_to_all.31.whole_ref = f32[4,1288,128]{2,1,0:T(8,128)S(1)} all-to-all(f32[4,1288,128]{2,1,0:T(8,128)S(1)} %broadcast_in_dim.5), channel_id=1, replica_groups=mesh['zh'=4,'zl'=4,'x'=4,'y'=4,'core'=2] {'x'}, dimensions={0} | all-to-all | bytes 5275648 | tf_op jit(solution)/shard_map/all_to_all | solution.py:480
  206.4 1.6 lay.1
  (12 shorter events, 0.1 us)
Async XLA Ops:
  21.4 4.7 %copy-start = (f32[3328,128]{1,0:T(8,128)S(1)}, f32[3328,128]{1,0:T(8,128)}, u32[]{:S(2)}) copy-start(f32[3328,128]{1,0:T(8,128)} %get-tuple-element.32.kept_in) | copy-start | bytes 5111812
  21.4 70.0 %all-to-all-start.1 = ((f32[4,128,1024]{2,1,0:T(8,128)}), f32[4,128,1024]{2,1,0:T(8,128)}, u32[]{:S(2)}, u32[]{:S(2)}) async-start(f32[4,128,1024]{2,1,0:T(8,128)} %get-tuple-element.39), calls=%async_computation.1 | async-start | bytes 4194304 | tf_op jit(solution)/shard_map/all_to_all | solution.py:484
  91.5 12.8 %all-to-all-start = ((f32[4,264,128]{2,1,0:T(8,128)}), f32[4,264,128]{2,1,0:T(8,128)S(1)}, u32[]{:S(2)}, u32[]{:S(2)}) async-start(f32[4,264,128]{2,1,0:T(8,128)} %get-tuple-element.38), calls=%async_computation | async-start | bytes 1081344 | tf_op jit(solution)/shard_map/all_to_all | solution.py:484
  105.4 22.9 %copy-start.1 = (bf16[1024,256]{1,0:T(8,128)(2,1)S(1)}, bf16[1024,256]{1,0:T(8,128)(2,1)}, u32[]{:S(2)}) copy-start(bf16[1024,256]{1,0:T(8,128)(2,1)} %wk_ref.1) | copy-start | bytes 1572868
  105.4 22.9 %copy-start.2 = (bf16[1024,256]{1,0:T(8,128)(2,1)S(1)}, bf16[1024,256]{1,0:T(8,128)(2,1)}, u32[]{:S(2)}) copy-start(bf16[1024,256]{1,0:T(8,128)(2,1)} %wv_ref.1) | copy-start | bytes 1572868
  105.4 22.9 %copy-start.3 = (bf16[1024,128]{1,0:T(8,128)(2,1)S(1)}, bf16[1024,128]{1,0:T(8,128)(2,1)}, u32[]{:S(2)}) copy-start(bf16[1024,128]{1,0:T(8,128)(2,1)} %wq_ref.1) | copy-start | bytes 786436
  105.4 22.9 %copy-start.4 = (bf16[1024,2]{0,1:T(2,128)(2,1)S(1)}, bf16[1024,2]{0,1:T(2,128)(2,1)}, u32[]{:S(2)}) copy-start(bf16[1024,2]{0,1:T(2,128)(2,1)} %param.11) | copy-start | bytes 12292
  122.0 19.8 %all-to-all-start.3 = ((f32[4,88,128]{2,1,0:T(8,128)}), f32[4,88,128]{2,1,0:T(8,128)S(1)}, u32[]{:S(2)}, u32[]{:S(2)}) async-start(f32[4,88,128]{2,1,0:T(8,128)} %pad_maximum_fusion.1), calls=%async_computation.3 | async-start | bytes 360448 | tf_op jit(solution)/shard_map/all_to_all | solution.py:484
  141.8 35.7 %all-to-all-start.4 = ((f32[8,128,128]{2,1,0:T(8,128)}), f32[8,128,128]{2,1,0:T(8,128)S(1)}, u32[]{:S(2)}, u32[]{:S(2)}) async-start(f32[8,128,128]{2,1,0:T(8,128)} %side.1), calls=%async_computation.4 | async-start | bytes 1048576 | tf_op jit(solution)/shard_map/all_to_all | solution.py:484

commit v8 on v7

--- a/solution.py
+++ b/solution.py
@@ -242,7 +242,8 @@
     outward_map, outward_shift = outward[:DH], outward[DH:] + own_ref[3]
 
     def far(group, which):
-        return jnp.concatenate([far_ref[i, group, which] for i in range(PARTS)], axis=0)
+        at = (-1, PARTS - 2, 2 * PARTS - 4)[which] + group
+        return jnp.concatenate([far_ref[i, at] for i in range(PARTS)], axis=0)
 
     entering = jnp.where(me > 0, far(0, 1), 0.0)
     leaving = jnp.where(me < PARTS - 1, far(PARTS - 1, 2), 0.0)
@@ -354,25 +355,31 @@
     )(place, far, kept)
 
 
-def side_kernel(tiles_ref, wb_ref, wq_ref, wk_ref, wv_ref, part_ref):
-    part = (
+def side_kernel(place_ref, tiles_ref, wb_ref, wq_ref, wk_ref, wv_ref, *refs):
+    out_refs, sum_ref = refs[:-1], refs[-1]
+    sum_ref[...] = (
         dot(tiles_ref[:, :DH], wq_ref[...], 1, 1)
         + dot(tiles_ref[:, DH : 3 * DH], wk_ref[...], 1, 1)
         + dot(tiles_ref[:, 3 * DH : 5 * DH], wv_ref[...], 1, 1)
         + dot(tiles_ref[:, 5 * DH : 5 * DH + 2], wb_ref[...])
     )
-    for i in range(8):
-        part_ref[i] = part[:, DH * i : DH * i + DH]
-
-
-def side(*args):
+    chip, core = place_ref[3], place_ref[4]
+    for i, out_ref in enumerate(out_refs):
+        pair = 2 * lax.rem(chip + i, PARTS)
+        for j, block in enumerate((pair + core, pair + 1 - core)):
+            out_ref[j] = sum_ref[:, pl.ds(pl.multiple_of(block * DH, DH), DH)]
+
+
+def side(place, *args):
     return pl.pallas_call(
         side_kernel,
-        out_shape=f32(8, ROWS, DH),
+        out_shape=(f32(2, ROWS, DH),) * PARTS,
+        in_specs=[SMEM] + [VMEM] * len(args),
+        scratch_shapes=[pltpu.VMEM((ROWS, 2 * PARTS * DH), jnp.float32)],
         compiler_params=pltpu.CompilerParams(vmem_limit_bytes=SMALL_BYTES),
         cost_estimate=pl.CostEstimate(flops=170_000_000, bytes_accessed=3_000_000, transcendentals=0),
         name="side",
-    )(*args)
+    )(place, *args)
 
 
 def narrow_kernel(frames_ref, narrow_ref):
@@ -425,10 +432,10 @@
     )(place, pieces, frames)
 
 
-def lay_kernel(
-    whole_ref, heads_ref, query_any, keys_any, values_any, beta_any, bias_any, frames_any,
-    beta_ref, bias_ref, sum_ref, sems,
-):
+def lay_kernel(whole_ref, *refs):
+    heads = refs[:2]
+    query_any, keys_any, values_any, beta_any, bias_any, frames_any = refs[2:8]
+    beta_ref, bias_ref, sum_ref, sems = refs[8:]
     left, right = pl.ds(0, DH), pl.ds(DH, DH)
     full = pl.ds(0, 1024)
     pairs = [
@@ -447,10 +454,7 @@
         [row[2 * half : 2 * half + 2] for row in rows for half in range(2)], axis=1
     )
     bias_ref[...] = rows[0][4:5, :2]
-    total = heads_ref[0]
-    for i in range(1, heads_ref.shape[0]):
-        total = total + heads_ref[i]
-    sum_ref[...] = total.astype(jnp.bfloat16)
+    sum_ref[...] = (heads[0][...] + heads[1][...]).astype(jnp.bfloat16)
     small = ((beta_ref, beta_any), (bias_ref, bias_any), (sum_ref, frames_any))
     for i, (a, b) in enumerate(small):
         copies.append(pltpu.make_async_copy(a, b, sems.at[8 + i]))
@@ -466,14 +470,14 @@
         out_shape=(
             f32(1024, DH), f32(1024, 2 * DH), f32(1024, 2 * DH), f32(2, 1024), f32(1, 2), frames,
         ),
-        in_specs=[VMEM, VMEM],
+        in_specs=[VMEM] * 3,
         out_specs=(HBM,) * 6,
         scratch_shapes=[
             held(f32(2, 1024)), held(f32(1, 2)), held(frames), pltpu.SemaphoreType.DMA((11,)),
         ],
         compiler_params=pltpu.CompilerParams(vmem_limit_bytes=SMALL_BYTES),
         name="lay",
-    )(whole, heads)
+    )(whole, *heads)
 
 
 def spread(a, axis):
@@ -484,8 +488,16 @@
     return lax.all_to_all(a, axis, 0, 0, tiled=True)
 
 
+def shift(a, axis, steps):
+    size = lax.axis_size(axis)
+    return lax.ppermute(a, axis, [(i, (i + steps) % size) for i in range(size)])
+
+
 def local(frames, w_query, w_keys, w_values, w_beta, beta_bias, cotangent):
-    place = jnp.stack([lax.axis_index("x"), lax.axis_index("zl"), lax.axis_index("zh")])
+    place = jnp.stack(
+        [lax.axis_index("x"), lax.axis_index("zl"), lax.axis_index("zh")]
+        + [lax.axis_index("y"), lax.axis_index("core")]
+    )
     beta_turned = w_beta.T
     own, kept, wide_frames = prepare(
         beta_bias, beta_turned, frames, w_keys, w_query, w_values, cotangent
@@ -494,19 +506,23 @@
     group_frames = trade(wide_frames, "x")
     total, kept = group_scan(row, kept, place, 0, "own", DH)
     total, kept = group_scan(lax.all_gather(total, "zl"), kept, place, 1, "near", DH // PARTS)
-    far = lax.all_gather(lax.all_gather(total, "zh"), "x")
+    far = lax.all_gather(total, "zh")
+    far = jnp.concatenate([far[1:-1, 0], far[:-1, 1], far[1:, 2]], axis=0)
+    far = lax.all_gather(far, "x")
     outputs, pieces, tiles = finish(place, far, kept)
-    partial = side(tiles, beta_turned, w_query, w_keys, w_values)
+    own, *others = side(place, tiles, beta_turned, w_query, w_keys, w_values)
+    for i, other in enumerate(others):
+        own = own + shift(other, "y", i + 1)
     sums = weigh(place, trade(pieces, "x"), narrow(group_frames))
     part = jnp.sum(trade(sums, "zl"), axis=0)
     part, extra = part[:320], part[320:]
     part = jnp.concatenate(
         [part.reshape(PARTS, 80, DH), jnp.broadcast_to(extra[None], (PARTS, EXTRA, DH))], axis=1
     )
+    part, own = lax.optimization_barrier((part, own))
+    partial = (own[0], shift(own[1], "core", 1))
     part = jnp.sum(trade(part, "zh"), axis=0)
     part, extra = part[:80], part[80:]
-    part, partial = lax.optimization_barrier((part, partial))
-    partial = trade(partial, ("y", "core"))
     part = lax.all_gather(part, ("zh", "zl")).reshape(1280, DH)
     part, partial = lax.optimization_barrier((part, partial))
     whole = jnp.concatenate([part, extra], axis=0)

time: 209 us -> 202 us (0.967)
  blocking collectives: 149 us -> 125 us
  starting transfers between devices: 20.2 us -> 29.3 us
  waiting for transfers between devices: 18.5 us -> 26 us
    all_to_all x1 -> x0, blocking collectives: 15.8 us -> none  [trade(): return lax.all_to_all(a, axis, 0, 0, tiled=True)]
    ppermute x0 -> x4, starting transfers between devices: none -> 10.5 us  [shift(): return lax.ppermute(a, axis, [(i, (i + steps) % size) for i in range(size)])]
    all_to_all x1, blocking collectives: 28.6 us -> 21.9 us  [spread(): lax.all_to_all(jnp.broadcast_to(a[None], (PARTS, *a.shape)), axis, 0, 0,...]
    ppermute x0 -> x4, waiting for transfers between devices: none -> 6.14 us  [shift(): return lax.ppermute(a, axis, [(i, (i + steps) % size) for i in range(size)])]
  transfers between devices with their start and end apart: 4 -> 8, of which waited for: 2 -> 4; matrix products, arithmetic and copies ran while one was open for 0% -> 0% of each run, Pallas kernels for 4% -> 4%
where the time goes in v8:
time: 202 us
  blocking collectives  125 us (62%)
  starting transfers between devices  29.3 us (15%)
  waiting for transfers between devices  26 us (13%)
  Pallas kernels  19.3 us (10%)
    all_gather x1, blocking collectives, local(): part = lax.all_gather(part, ('zh', 'zl')).reshape(1280, DH)  30.5 us
    all_gather x1, blocking collectives, local(): far = lax.all_gather(total, 'zh')  25.2 us
    all_to_all x1, blocking collectives, spread(): lax.all_to_all(jnp.broadcast_to(a[None], (PARTS, *a.shape)), axis, 0, 0,...  21.9 us
    all_gather x1, blocking collectives, local(): lax.all_gather(total, 'zl')  20.3 us
    all_to_all x4, waiting for transfers between devices, trade(): return lax.all_to_all(a, axis, 0, 0, tiled=True)  19.9 us
    all_to_all x4, starting transfers between devices, trade(): return lax.all_to_all(a, axis, 0, 0, tiled=True)  18.8 us
    all_gather x1, blocking collectives, local(): lax.all_gather(own, 'x')  13.9 us
    all_gather x1, blocking collectives, local(): far = lax.all_gather(far, 'x')  13.4 us
  transfers between devices with their start and end apart: 8, of which 4 were waited for; matrix products, arithmetic and copies ran while one was open for 0% of the time, Pallas kernels for 4%

profile of v8, /device:TPU:24, one launch (start us, length us, event | category | flops | bytes accessed | tf_op | source)
XLA Modules:
  0.0 201.8 jit_solution(7614963808623590814)
XLA Ops:
  0.6 6.9 %prepare.1 = (f32[3,128,128]{2,1,0:T(8,128)}, f32[3328,128]{1,0:T(8,128)}, f32[4,128,1024]{2,1,0:T(8,128)}) custom-call(f32[2]{0:T(128)} %bias_ref.1, bf16[2,1024]{1,0:T(2,128)(2,1)} %bitcast.32, bf16[128,1024]{1,0:T(8,128)(2,1)} %frames_any.1, bf16[1024,256]{1,0:T(8,128)(2,1)} %wk_ref.1, bf16[1024,128]{1,0:T(8,128)(2,1)} %wq_ref.1, ...), custom_call_target="tpu_custom_call" | custom-call | tf_op jit(solution)/shard_map/prepare/pallas_call | solution.py:330
  7.5 13.9 %all-gather = f32[12,128,128]{2,1,0:T(8,128)S(1)} all-gather(f32[3,128,128]{2,1,0:T(8,128)} %get-tuple-element.34), channel_id=2, replica_groups=mesh['zh'=4,'zl'=4,'x'=4,'y'=4,'core'=2] {'x'}, dimensions={0}, use_global_device_ids=true | all-gather | bytes 983040 | tf_op jit(solution)/shard_map/all_gather | solution.py:505
  21.4 4.6 %all-to-all-start.1 = ((f32[4,128,1024]{2,1,0:T(8,128)}), f32[4,128,1024]{2,1,0:T(8,128)}, u32[]{:S(2)}, u32[]{:S(2)}) async-start(f32[4,128,1024]{2,1,0:T(8,128)} %get-tuple-element.44), calls=%async_computation.1 | async-start | bytes 4194304 | tf_op jit(solution)/shard_map/all_to_all | solution.py:488
  26.0 0.1 stack.23.place_ref
  26.1 1.3 group_scan.2
  27.4 20.3 %all-gather.1 = f32[12,128,128]{2,1,0:T(8,128)S(1)} all-gather(f32[3,128,128]{2,1,0:T(8,128)S(1)} %get-tuple-element.38), channel_id=3, replica_groups=mesh['zh'=4,'zl'=4,'x'=4,'y'=4,'core'=2] {'zl'}, dimensions={0}, use_global_device_ids=true | all-gather | bytes 983040 | tf_op jit(solution)/shard_map/all_gather | solution.py:508
  47.7 1.3 group_scan.3
  49.0 25.2 %all-gather.2 = f32[12,32,128]{2,1,0:T(8,128)S(1)} all-gather(f32[3,32,128]{2,1,0:T(8,128)S(1)} %get-tuple-element.40), channel_id=4, replica_groups=mesh['zh'=4,'zl'=4,'x'=4,'y'=4,'core'=2] {'zh'}, dimensions={0}, use_global_device_ids=true | all-gather | bytes 245760 | tf_op jit(solution)/shard_map/all_gather | solution.py:509
  74.3 13.4 %all-gather.3 = f32[32,32,128]{2,1,0:T(8,128)S(1)} all-gather(f32[8,32,128]{2,1,0:T(8,128)S(1)} %pad_maximum_fusion.2), channel_id=5, replica_groups=mesh['zh'=4,'zl'=4,'x'=4,'y'=4,'core'=2] {'x'}, dimensions={0}, use_global_device_ids=true | all-gather | bytes 655360 | tf_op jit(solution)/shard_map/all_gather | solution.py:511
  87.7 3.3 %finish.1 = (bf16[128,128]{1,0:T(8,128)(2,1)}, f32[4,264,128]{2,1,0:T(8,128)}, bf16[128,768]{1,0:T(8,128)(2,1)S(1)}) custom-call(s32[5]{0:T(128)S(1)} %stack.23.place_ref, f32[4,8,32,128]{3,2,1,0:T(8,128)S(1)} %bitcast.31, f32[3328,128]{1,0:T(8,128)S(1)} %get-tuple-element.41.kept_ref), custom_call_target="tpu_custom_call" | custom-call | tf_op jit(solution)/shard_map/finish/pallas_call | solution.py:345
  91.0 4.1 %all-to-all-start = ((f32[4,264,128]{2,1,0:T(8,128)}), f32[4,264,128]{2,1,0:T(8,128)S(1)}, u32[]{:S(2)}, u32[]{:S(2)}) async-start(f32[4,264,128]{2,1,0:T(8,128)} %get-tuple-element.43), calls=%async_computation | async-start | bytes 1081344 | tf_op jit(solution)/shard_map/all_to_all | solution.py:488
  95.1 1.7 narrow.1.frames_ref
  96.8 0.0 copy-start.1
  96.8 0.0 copy-start.2
  96.8 0.0 copy-start.4
  96.8 6.4 %all-to-all-done.pieces_ref = f32[4,264,128]{2,1,0:T(8,128)S(1)} async-done(((f32[4,264,128]{2,1,0:T(8,128)}), f32[4,264,128]{2,1,0:T(8,128)S(1)}, u32[]{:S(2)}, u32[]{:S(2)}) %all-to-all-start) | async-done | bytes 540704 | tf_op jit(solution)/shard_map/all_to_all | solution.py:488
  103.3 2.0 weigh.1
  105.2 3.5 %all-to-all-start.2 = ((f32[4,328,128]{2,1,0:T(8,128)}), f32[4,328,128]{2,1,0:T(8,128)S(1)}, u32[]{:S(2)}, u32[]{:S(2)}) async-start(f32[4,328,128]{2,1,0:T(8,128)} %weigh.1), calls=%async_computation.2 | async-start | bytes 1343488 | tf_op jit(solution)/shard_map/all_to_all | solution.py:488
  108.8 1.2 side.1
  110.0 2.0 %collective-permute-start = (f32[2,128,128]{2,1,0:T(8,128)S(1)}, f32[2,128,128]{2,1,0:T(8,128)S(1)}, u32[]{:S(2)}, u32[]{:S(2)}) collective-permute-start(f32[2,128,128]{2,1,0:T(8,128)S(1)} %get-tuple-element.47), channel_id=1, source_target_pairs={{0,2},{2,4},{4,6},{6,0},{1,3},{3,5},{5,7},{7,1},{8,10},{10,12},{12... | collective-permute-start | bytes 393224 | tf_op jit(solution)/shard_map/ppermute | solution.py:493
  112.1 4.6 %collective-permute-start.1 = (f32[2,128,128]{2,1,0:T(8,128)S(1)}, f32[2,128,128]{2,1,0:T(8,128)S(1)}, u32[]{:S(2)}, u32[]{:S(2)}) collective-permute-start(f32[2,128,128]{2,1,0:T(8,128)S(1)} %get-tuple-element.48), channel_id=1, source_target_pairs={{0,4},{2,6},{4,0},{6,2},{1,5},{3,7},{5,1},{7,3},{8,12},{10,14},{12... | collective-permute-start | bytes 393224 | tf_op jit(solution)/shard_map/ppermute | solution.py:493
  116.6 1.9 collective-permute-start.2
  118.6 1.8 collective-permute-done.1
  120.4 4.3 %collective-permute-done.2 = f32[2,128,128]{2,1,0:T(8,128)S(1)} collective-permute-done((f32[2,128,128]{2,1,0:T(8,128)S(1)}, f32[2,128,128]{2,1,0:T(8,128)S(1)}, u32[]{:S(2)}, u32[]{:S(2)}) %collective-permute-start.2) | collective-permute-done | bytes 131104 | tf_op jit(solution)/shard_map/ppermute | solution.py:493
  124.8 0.7 pad_maximum_fusion.1
  125.5 6.6 %all-to-all-start.3 = ((f32[4,88,128]{2,1,0:T(8,128)}), f32[4,88,128]{2,1,0:T(8,128)S(1)}, u32[]{:S(2)}, u32[]{:S(2)}) async-start(f32[4,88,128]{2,1,0:T(8,128)} %pad_maximum_fusion.1), calls=%async_computation.3 | async-start | bytes 360448 | tf_op jit(solution)/shard_map/all_to_all | solution.py:488
  132.2 1.9 collective-permute-start.3
  134.1 13.5 %all-to-all-done.3 = f32[4,88,128]{2,1,0:T(8,128)S(1)} async-done(((f32[4,88,128]{2,1,0:T(8,128)}), f32[4,88,128]{2,1,0:T(8,128)S(1)}, u32[]{:S(2)}, u32[]{:S(2)}) %all-to-all-start.3) | async-done | bytes 180256 | tf_op jit(solution)/shard_map/all_to_all | solution.py:488
  147.6 30.5 %all-gather.4 = f32[1280,128]{1,0:T(8,128)S(1)} all-gather(f32[80,128]{1,0:T(8,128)S(1)} %slice.41), channel_id=6, replica_groups=mesh['zh'=4,'zl'=4,'x'=4,'y'=4,'core'=2] {'zh','zl'}, dimensions={0}, use_global_device_ids=true | all-gather | bytes 696320 | tf_op jit(solution)/shard_map/all_gather | solution.py:526
  178.2 0.2 broadcast_in_dim.5
  178.4 21.9 %all_to_all.25.whole_ref = f32[4,1288,128]{2,1,0:T(8,128)S(1)} all-to-all(f32[4,1288,128]{2,1,0:T(8,128)S(1)} %broadcast_in_dim.5), channel_id=1, replica_groups=mesh['zh'=4,'zl'=4,'x'=4,'y'=4,'core'=2] {'x'}, dimensions={0} | all-to-all | bytes 5275648 | tf_op jit(solution)/shard_map/all_to_all | solution.py:484
  200.2 1.6 lay.1
  (24 shorter events, 0.2 us)
Async XLA Ops:
  21.4 4.7 %copy-start = (f32[3328,128]{1,0:T(8,128)S(1)}, f32[3328,128]{1,0:T(8,128)}, u32[]{:S(2)}) copy-start(f32[3328,128]{1,0:T(8,128)} %get-tuple-element.37.kept_in) | copy-start | bytes 5111812
  21.4 69.6 %all-to-all-start.1 = ((f32[4,128,1024]{2,1,0:T(8,128)}), f32[4,128,1024]{2,1,0:T(8,128)}, u32[]{:S(2)}, u32[]{:S(2)}) async-start(f32[4,128,1024]{2,1,0:T(8,128)} %get-tuple-element.44), calls=%async_computation.1 | async-start | bytes 4194304 | tf_op jit(solution)/shard_map/all_to_all | solution.py:488
  91.0 12.3 %all-to-all-start = ((f32[4,264,128]{2,1,0:T(8,128)}), f32[4,264,128]{2,1,0:T(8,128)S(1)}, u32[]{:S(2)}, u32[]{:S(2)}) async-start(f32[4,264,128]{2,1,0:T(8,128)} %get-tuple-element.43), calls=%async_computation | async-start | bytes 1081344 | tf_op jit(solution)/shard_map/all_to_all | solution.py:488
  96.8 11.9 %copy-start.1 = (bf16[1024,256]{1,0:T(8,128)(2,1)S(1)}, bf16[1024,256]{1,0:T(8,128)(2,1)}, u32[]{:S(2)}) copy-start(bf16[1024,256]{1,0:T(8,128)(2,1)} %wk_ref.1) | copy-start | bytes 1572868
  96.8 11.9 %copy-start.2 = (bf16[1024,256]{1,0:T(8,128)(2,1)S(1)}, bf16[1024,256]{1,0:T(8,128)(2,1)}, u32[]{:S(2)}) copy-start(bf16[1024,256]{1,0:T(8,128)(2,1)} %wv_ref.1) | copy-start | bytes 1572868
  96.8 11.9 %copy-start.3 = (bf16[1024,128]{1,0:T(8,128)(2,1)S(1)}, bf16[1024,128]{1,0:T(8,128)(2,1)}, u32[]{:S(2)}) copy-start(bf16[1024,128]{1,0:T(8,128)(2,1)} %wq_ref.1) | copy-start | bytes 786436
  96.8 11.9 %copy-start.4 = (bf16[1024,2]{0,1:T(2,128)(2,1)S(1)}, bf16[1024,2]{0,1:T(2,128)(2,1)}, u32[]{:S(2)}) copy-start(bf16[1024,2]{0,1:T(2,128)(2,1)} %param.11) | copy-start | bytes 12292
  105.2 19.5 %all-to-all-start.2 = ((f32[4,328,128]{2,1,0:T(8,128)}), f32[4,328,128]{2,1,0:T(8,128)S(1)}, u32[]{:S(2)}, u32[]{:S(2)}) async-start(f32[4,328,128]{2,1,0:T(8,128)} %weigh.1), calls=%async_computation.2 | async-start | bytes 1343488 | tf_op jit(solution)/shard_map/all_to_all | solution.py:488
  110.0 8.6 %collective-permute-start = (f32[2,128,128]{2,1,0:T(8,128)S(1)}, f32[2,128,128]{2,1,0:T(8,128)S(1)}, u32[]{:S(2)}, u32[]{:S(2)}) collective-permute-start(f32[2,128,128]{2,1,0:T(8,128)S(1)} %get-tuple-element.47), channel_id=1, source_target_pairs={{0,2},{2,4},{4,6},{6,0},{1,3},{3,5},{5,7},{7,1},{8,10},{10,12},{12... | collective-permute-start | bytes 393224 | tf_op jit(solution)/shard_map/ppermute | solution.py:493
  112.1 8.4 %collective-permute-start.1 = (f32[2,128,128]{2,1,0:T(8,128)S(1)}, f32[2,128,128]{2,1,0:T(8,128)S(1)}, u32[]{:S(2)}, u32[]{:S(2)}) collective-permute-start(f32[2,128,128]{2,1,0:T(8,128)S(1)} %get-tuple-element.48), channel_id=1, source_target_pairs={{0,4},{2,6},{4,0},{6,2},{1,5},{3,7},{5,1},{7,3},{8,12},{10,14},{12... | collective-permute-start | bytes 393224 | tf_op jit(solution)/shard_map/ppermute | solution.py:493
  116.6 8.1 %collective-permute-start.2 = (f32[2,128,128]{2,1,0:T(8,128)S(1)}, f32[2,128,128]{2,1,0:T(8,128)S(1)}, u32[]{:S(2)}, u32[]{:S(2)}) collective-permute-start(f32[2,128,128]{2,1,0:T(8,128)S(1)} %get-tuple-element.49), channel_id=1, source_target_pairs={{0,6},{2,0},{4,2},{6,4},{1,7},{3,1},{5,3},{7,5},{8,14},{10,8},{12,... | collective-permute-start | bytes 393224 | tf_op jit(solution)/shard_map/ppermute | solution.py:493
  125.5 22.0 %all-to-all-start.3 = ((f32[4,88,128]{2,1,0:T(8,128)}), f32[4,88,128]{2,1,0:T(8,128)S(1)}, u32[]{:S(2)}, u32[]{:S(2)}) async-start(f32[4,88,128]{2,1,0:T(8,128)} %pad_maximum_fusion.1), calls=%async_computation.3 | async-start | bytes 360448 | tf_op jit(solution)/shard_map/all_to_all | solution.py:488
  132.2 45.9 %collective-permute-start.3 = (f32[128,128]{1,0:T(8,128)S(1)}, f32[128,128]{1,0:T(8,128)S(1)}, u32[]{:S(2)}, u32[]{:S(2)}) collective-permute-start(f32[128,128]{1,0:T(8,128)S(1)} %get-tuple-element.63), channel_id=1, source_target_pairs={{0,1},{1,0},{2,3},{3,2},{4,5},{5,4},{6,7},{7,6},{8,9},{9,8},{10,11... | collective-permute-start | bytes 196616 | tf_op jit(solution)/shard_map/ppermute | solution.py:493

commit v9 on v8

--- a/solution.py
+++ b/solution.py
@@ -510,17 +510,19 @@
     far = jnp.concatenate([far[1:-1, 0], far[:-1, 1], far[1:, 2]], axis=0)
     far = lax.all_gather(far, "x")
     outputs, pieces, tiles = finish(place, far, kept)
-    own, *others = side(place, tiles, beta_turned, w_query, w_keys, w_values)
-    for i, other in enumerate(others):
-        own = own + shift(other, "y", i + 1)
-    sums = weigh(place, trade(pieces, "x"), narrow(group_frames))
+    pieces, group_frames = trade(pieces, "x"), narrow(group_frames)
+    heads = side(place, tiles, beta_turned, w_query, w_keys, w_values)
+    pieces, group_frames, heads = lax.optimization_barrier((pieces, group_frames, heads))
+    sums = weigh(place, pieces, group_frames)
+    shared = heads[0]
+    for i in range(1, PARTS):
+        shared = shared + shift(heads[i], "y", i)
     part = jnp.sum(trade(sums, "zl"), axis=0)
     part, extra = part[:320], part[320:]
     part = jnp.concatenate(
         [part.reshape(PARTS, 80, DH), jnp.broadcast_to(extra[None], (PARTS, EXTRA, DH))], axis=1
     )
-    part, own = lax.optimization_barrier((part, own))
-    partial = (own[0], shift(own[1], "core", 1))
+    partial = (shared[0], shift(shared[1], "core", 1))
     part = jnp.sum(trade(part, "zh"), axis=0)
     part, extra = part[:80], part[80:]
     part = lax.all_gather(part, ("zh", "zl")).reshape(1280, DH)

time: 202 us -> 198 us (0.980)
  waiting for transfers between devices: 26 us -> 20.8 us
    ppermute x4, waiting for transfers between devices: 6.14 us -> 0.01 us  [shift(): return lax.ppermute(a, axis, [(i, (i + steps) % size) for i in range(size)])]
  transfers between devices with their start and end apart: 8 -> 8, of which waited for: 4 -> 3; matrix products, arithmetic and copies ran while one was open for 0% -> 0% of each run, Pallas kernels for 4% -> 4%
where the time goes in v9:
time: 198 us; the launch traced here: 197 us
  blocking collectives  126 us (64%)
  starting transfers between devices  27.6 us (14%)
  waiting for transfers between devices  20.8 us (11%)
  Pallas kernels  19.3 us (10%)
    all_gather x1, blocking collectives, local(): part = lax.all_gather(part, ('zh', 'zl')).reshape(1280, DH)  31.5 us
    all_gather x1, blocking collectives, local(): far = lax.all_gather(total, 'zh')  25.3 us
    all_to_all x1, blocking collectives, spread(): lax.all_to_all(jnp.broadcast_to(a[None], (PARTS, *a.shape)), axis, 0, 0,...  21.9 us
    all_to_all x4, waiting for transfers between devices, trade(): return lax.all_to_all(a, axis, 0, 0, tiled=True)  20.8 us
    all_gather x1, blocking collectives, local(): lax.all_gather(total, 'zl')  20.3 us
    all_to_all x4, starting transfers between devices, trade(): return lax.all_to_all(a, axis, 0, 0, tiled=True)  17.1 us
    all_gather x1, blocking collectives, local(): lax.all_gather(own, 'x')  13.9 us
    all_gather x1, blocking collectives, local(): far = lax.all_gather(far, 'x')  13.5 us
  transfers between devices with their start and end apart: 8, of which 3 were waited for; matrix products, arithmetic and copies ran while one was open for 0% of the time, Pallas kernels for 4%

profile of v9, /device:TPU:24, one launch (start us, length us, event | category | flops | bytes accessed | tf_op | source)
XLA Modules:
  0.0 197.3 jit_solution(4043843765212735083)
XLA Ops:
  0.6 6.9 %prepare.1 = (f32[3,128,128]{2,1,0:T(8,128)}, f32[3328,128]{1,0:T(8,128)}, f32[4,128,1024]{2,1,0:T(8,128)}) custom-call(f32[2]{0:T(128)} %bias_ref.1, bf16[2,1024]{1,0:T(2,128)(2,1)} %bitcast.32, bf16[128,1024]{1,0:T(8,128)(2,1)} %frames_any.1, bf16[1024,256]{1,0:T(8,128)(2,1)} %wk_ref.1, bf16[1024,128]{1,0:T(8,128)(2,1)} %wq_ref.1, ...), custom_call_target="tpu_custom_call" | custom-call | tf_op jit(solution)/shard_map/prepare/pallas_call | solution.py:330
  7.5 13.9 %all-gather = f32[12,128,128]{2,1,0:T(8,128)S(1)} all-gather(f32[3,128,128]{2,1,0:T(8,128)} %get-tuple-element.38), channel_id=2, replica_groups=mesh['zh'=4,'zl'=4,'x'=4,'y'=4,'core'=2] {'x'}, dimensions={0}, use_global_device_ids=true | all-gather | bytes 983040 | tf_op jit(solution)/shard_map/all_gather | solution.py:505
  21.4 4.6 %all-to-all-start.1 = ((f32[4,128,1024]{2,1,0:T(8,128)}), f32[4,128,1024]{2,1,0:T(8,128)}, u32[]{:S(2)}, u32[]{:S(2)}) async-start(f32[4,128,1024]{2,1,0:T(8,128)} %get-tuple-element.48), calls=%async_computation.1 | async-start | bytes 4194304 | tf_op jit(solution)/shard_map/all_to_all | solution.py:488
  26.0 0.1 stack.23.place_ref
  26.1 1.3 group_scan.2
  27.4 20.3 %all-gather.1 = f32[12,128,128]{2,1,0:T(8,128)S(1)} all-gather(f32[3,128,128]{2,1,0:T(8,128)S(1)} %get-tuple-element.42), channel_id=3, replica_groups=mesh['zh'=4,'zl'=4,'x'=4,'y'=4,'core'=2] {'zl'}, dimensions={0}, use_global_device_ids=true | all-gather | bytes 983040 | tf_op jit(solution)/shard_map/all_gather | solution.py:508
  47.7 1.3 group_scan.3
  49.0 25.3 %all-gather.2 = f32[12,32,128]{2,1,0:T(8,128)S(1)} all-gather(f32[3,32,128]{2,1,0:T(8,128)S(1)} %get-tuple-element.44), channel_id=4, replica_groups=mesh['zh'=4,'zl'=4,'x'=4,'y'=4,'core'=2] {'zh'}, dimensions={0}, use_global_device_ids=true | all-gather | bytes 245760 | tf_op jit(solution)/shard_map/all_gather | solution.py:509
  74.3 0.0 copy-start.1
  74.3 0.0 copy-start.2
  74.4 13.5 %all-gather.3 = f32[32,32,128]{2,1,0:T(8,128)S(1)} all-gather(f32[8,32,128]{2,1,0:T(8,128)S(1)} %pad_maximum_fusion.2), channel_id=5, replica_groups=mesh['zh'=4,'zl'=4,'x'=4,'y'=4,'core'=2] {'x'}, dimensions={0}, use_global_device_ids=true | all-gather | bytes 655360 | tf_op jit(solution)/shard_map/all_gather | solution.py:511
  87.9 3.3 %finish.1 = (bf16[128,128]{1,0:T(8,128)(2,1)}, f32[4,264,128]{2,1,0:T(8,128)}, bf16[128,768]{1,0:T(8,128)(2,1)S(1)}) custom-call(s32[5]{0:T(128)S(1)} %stack.23.place_ref, f32[4,8,32,128]{3,2,1,0:T(8,128)S(1)} %bitcast.31, f32[3328,128]{1,0:T(8,128)S(1)} %get-tuple-element.45.kept_ref), custom_call_target="tpu_custom_call" | custom-call | tf_op jit(solution)/shard_map/finish/pallas_call | solution.py:345
  91.2 4.2 %all-to-all-start = ((f32[4,264,128]{2,1,0:T(8,128)}), f32[4,264,128]{2,1,0:T(8,128)S(1)}, u32[]{:S(2)}, u32[]{:S(2)}) async-start(f32[4,264,128]{2,1,0:T(8,128)} %get-tuple-element.47), calls=%async_computation | async-start | bytes 1081344 | tf_op jit(solution)/shard_map/all_to_all | solution.py:488
  95.4 1.2 side.1
  96.6 0.6 copy-done.5
  97.3 0.7 copy-done.7
  98.0 1.7 narrow.1.frames_ref
  99.7 3.9 %all-to-all-done.pieces_ref = f32[4,264,128]{2,1,0:T(8,128)S(1)} async-done(((f32[4,264,128]{2,1,0:T(8,128)}), f32[4,264,128]{2,1,0:T(8,128)S(1)}, u32[]{:S(2)}, u32[]{:S(2)}) %all-to-all-start) | async-done | bytes 540704 | tf_op jit(solution)/shard_map/all_to_all | solution.py:488
  103.6 2.0 weigh.1
  105.5 3.5 %all-to-all-start.2 = ((f32[4,328,128]{2,1,0:T(8,128)}), f32[4,328,128]{2,1,0:T(8,128)S(1)}, u32[]{:S(2)}, u32[]{:S(2)}) async-start(f32[4,328,128]{2,1,0:T(8,128)} %weigh.1), calls=%async_computation.2 | async-start | bytes 1343488 | tf_op jit(solution)/shard_map/all_to_all | solution.py:488
  109.0 2.0 %collective-permute-start = (f32[2,128,128]{2,1,0:T(8,128)S(1)}, f32[2,128,128]{2,1,0:T(8,128)S(1)}, u32[]{:S(2)}, u32[]{:S(2)}) collective-permute-start(f32[2,128,128]{2,1,0:T(8,128)S(1)} %copy-done.8), channel_id=1, source_target_pairs={{0,2},{2,4},{4,6},{6,0},{1,3},{3,5},{5,7},{7,1},{8,10},{10,12},{12... | collective-permute-start | bytes 393224 | tf_op jit(solution)/shard_map/ppermute | solution.py:493
  111.1 4.6 %collective-permute-start.1 = (f32[2,128,128]{2,1,0:T(8,128)S(1)}, f32[2,128,128]{2,1,0:T(8,128)S(1)}, u32[]{:S(2)}, u32[]{:S(2)}) collective-permute-start(f32[2,128,128]{2,1,0:T(8,128)S(1)} %copy-done.6), channel_id=1, source_target_pairs={{0,4},{2,6},{4,0},{6,2},{1,5},{3,7},{5,1},{7,3},{8,12},{10,14},{12... | collective-permute-start | bytes 393224 | tf_op jit(solution)/shard_map/ppermute | solution.py:493
  115.7 1.9 collective-permute-start.2
  117.6 5.3 %all-to-all-done.2 = f32[4,328,128]{2,1,0:T(8,128)S(1)} async-done(((f32[4,328,128]{2,1,0:T(8,128)}), f32[4,328,128]{2,1,0:T(8,128)S(1)}, u32[]{:S(2)}, u32[]{:S(2)}) %all-to-all-start.2) | async-done | bytes 671776 | tf_op jit(solution)/shard_map/all_to_all | solution.py:488
  123.0 0.7 pad_maximum_fusion.1
  123.7 4.9 %all-to-all-start.3 = ((f32[4,88,128]{2,1,0:T(8,128)}), f32[4,88,128]{2,1,0:T(8,128)S(1)}, u32[]{:S(2)}, u32[]{:S(2)}) async-start(f32[4,88,128]{2,1,0:T(8,128)} %pad_maximum_fusion.1), calls=%async_computation.3 | async-start | bytes 360448 | tf_op jit(solution)/shard_map/all_to_all | solution.py:488
  128.6 1.9 collective-permute-start.3
  130.6 11.6 %all-to-all-done.3 = f32[4,88,128]{2,1,0:T(8,128)S(1)} async-done(((f32[4,88,128]{2,1,0:T(8,128)}), f32[4,88,128]{2,1,0:T(8,128)S(1)}, u32[]{:S(2)}, u32[]{:S(2)}) %all-to-all-start.3) | async-done | bytes 180256 | tf_op jit(solution)/shard_map/all_to_all | solution.py:488
  142.2 31.5 %all-gather.4 = f32[1280,128]{1,0:T(8,128)S(1)} all-gather(f32[80,128]{1,0:T(8,128)S(1)} %slice.41), channel_id=6, replica_groups=mesh['zh'=4,'zl'=4,'x'=4,'y'=4,'core'=2] {'zh','zl'}, dimensions={0}, use_global_device_ids=true | all-gather | bytes 696320 | tf_op jit(solution)/shard_map/all_gather | solution.py:528
  173.7 0.2 broadcast_in_dim.5
  173.9 21.9 %all_to_all.25.whole_ref = f32[4,1288,128]{2,1,0:T(8,128)S(1)} all-to-all(f32[4,1288,128]{2,1,0:T(8,128)S(1)} %broadcast_in_dim.5), channel_id=1, replica_groups=mesh['zh'=4,'zl'=4,'x'=4,'y'=4,'core'=2] {'x'}, dimensions={0} | all-to-all | bytes 5275648 | tf_op jit(solution)/shard_map/all_to_all | solution.py:484
  195.8 1.6 lay.1
  (32 shorter events, 0.2 us)
Async XLA Ops:
  21.4 4.7 %copy-start = (f32[3328,128]{1,0:T(8,128)S(1)}, f32[3328,128]{1,0:T(8,128)}, u32[]{:S(2)}) copy-start(f32[3328,128]{1,0:T(8,128)} %get-tuple-element.41.kept_in) | copy-start | bytes 5111812
  21.4 69.8 %all-to-all-start.1 = ((f32[4,128,1024]{2,1,0:T(8,128)}), f32[4,128,1024]{2,1,0:T(8,128)}, u32[]{:S(2)}, u32[]{:S(2)}) async-start(f32[4,128,1024]{2,1,0:T(8,128)} %get-tuple-element.48), calls=%async_computation.1 | async-start | bytes 4194304 | tf_op jit(solution)/shard_map/all_to_all | solution.py:488
  74.3 21.1 %copy-start.1 = (bf16[1024,256]{1,0:T(8,128)(2,1)S(1)}, bf16[1024,256]{1,0:T(8,128)(2,1)}, u32[]{:S(2)}) copy-start(bf16[1024,256]{1,0:T(8,128)(2,1)} %wk_ref.1) | copy-start | bytes 1572868
  74.3 21.1 %copy-start.2 = (bf16[1024,256]{1,0:T(8,128)(2,1)S(1)}, bf16[1024,256]{1,0:T(8,128)(2,1)}, u32[]{:S(2)}) copy-start(bf16[1024,256]{1,0:T(8,128)(2,1)} %wv_ref.1) | copy-start | bytes 1572868
  74.3 21.1 %copy-start.3 = (bf16[1024,128]{1,0:T(8,128)(2,1)S(1)}, bf16[1024,128]{1,0:T(8,128)(2,1)}, u32[]{:S(2)}) copy-start(bf16[1024,128]{1,0:T(8,128)(2,1)} %wq_ref.1) | copy-start | bytes 786436
  74.3 21.1 %copy-start.4 = (bf16[1024,2]{0,1:T(2,128)(2,1)S(1)}, bf16[1024,2]{0,1:T(2,128)(2,1)}, u32[]{:S(2)}) copy-start(bf16[1024,2]{0,1:T(2,128)(2,1)} %param.11) | copy-start | bytes 12292
  91.2 12.4 %all-to-all-start = ((f32[4,264,128]{2,1,0:T(8,128)}), f32[4,264,128]{2,1,0:T(8,128)S(1)}, u32[]{:S(2)}, u32[]{:S(2)}) async-start(f32[4,264,128]{2,1,0:T(8,128)} %get-tuple-element.47), calls=%async_computation | async-start | bytes 1081344 | tf_op jit(solution)/shard_map/all_to_all | solution.py:488
  96.6 0.7 copy-start.5
  97.3 0.7 copy-start.7
  99.6 9.4 %copy-start.8 = (f32[2,128,128]{2,1,0:T(8,128)S(1)}, f32[2,128,128]{2,1,0:T(8,128)}, u32[]{:S(2)}) copy-start(f32[2,128,128]{2,1,0:T(8,128)} %copy-done.7) | copy-start | bytes 393220
  99.7 11.4 %copy-start.6 = (f32[2,128,128]{2,1,0:T(8,128)S(1)}, f32[2,128,128]{2,1,0:T(8,128)}, u32[]{:S(2)}) copy-start(f32[2,128,128]{2,1,0:T(8,128)} %copy-done.5) | copy-start | bytes 393220
  105.5 17.4 %all-to-all-start.2 = ((f32[4,328,128]{2,1,0:T(8,128)}), f32[4,328,128]{2,1,0:T(8,128)S(1)}, u32[]{:S(2)}, u32[]{:S(2)}) async-start(f32[4,328,128]{2,1,0:T(8,128)} %weigh.1), calls=%async_computation.2 | async-start | bytes 1343488 | tf_op jit(solution)/shard_map/all_to_all | solution.py:488
  109.0 19.5 %collective-permute-start = (f32[2,128,128]{2,1,0:T(8,128)S(1)}, f32[2,128,128]{2,1,0:T(8,128)S(1)}, u32[]{:S(2)}, u32[]{:S(2)}) collective-permute-start(f32[2,128,128]{2,1,0:T(8,128)S(1)} %copy-done.8), channel_id=1, source_target_pairs={{0,2},{2,4},{4,6},{6,0},{1,3},{3,5},{5,7},{7,1},{8,10},{10,12},{12... | collective-permute-start | bytes 393224 | tf_op jit(solution)/shard_map/ppermute | solution.py:493
  111.1 17.5 %collective-permute-start.1 = (f32[2,128,128]{2,1,0:T(8,128)S(1)}, f32[2,128,128]{2,1,0:T(8,128)S(1)}, u32[]{:S(2)}, u32[]{:S(2)}) collective-permute-start(f32[2,128,128]{2,1,0:T(8,128)S(1)} %copy-done.6), channel_id=1, source_target_pairs={{0,4},{2,6},{4,0},{6,2},{1,5},{3,7},{5,1},{7,3},{8,12},{10,14},{12... | collective-permute-start | bytes 393224 | tf_op jit(solution)/shard_map/ppermute | solution.py:493
  115.7 12.9 %collective-permute-start.2 = (f32[2,128,128]{2,1,0:T(8,128)S(1)}, f32[2,128,128]{2,1,0:T(8,128)S(1)}, u32[]{:S(2)}, u32[]{:S(2)}) collective-permute-start(f32[2,128,128]{2,1,0:T(8,128)S(1)} %get-tuple-element.59), channel_id=1, source_target_pairs={{0,6},{2,0},{4,2},{6,4},{1,7},{3,1},{5,3},{7,5},{8,14},{10,8},{12,... | collective-permute-start | bytes 393224 | tf_op jit(solution)/shard_map/ppermute | solution.py:493
  123.7 18.5 %all-to-all-start.3 = ((f32[4,88,128]{2,1,0:T(8,128)}), f32[4,88,128]{2,1,0:T(8,128)S(1)}, u32[]{:S(2)}, u32[]{:S(2)}) async-start(f32[4,88,128]{2,1,0:T(8,128)} %pad_maximum_fusion.1), calls=%async_computation.3 | async-start | bytes 360448 | tf_op jit(solution)/shard_map/all_to_all | solution.py:488
  128.6 45.0 %collective-permute-start.3 = (f32[128,128]{1,0:T(8,128)S(1)}, f32[128,128]{1,0:T(8,128)S(1)}, u32[]{:S(2)}, u32[]{:S(2)}) collective-permute-start(f32[128,128]{1,0:T(8,128)S(1)} %get-tuple-element.71), channel_id=1, source_target_pairs={{0,1},{1,0},{2,3},{3,2},{4,5},{5,4},{6,7},{7,6},{8,9},{9,8},{10,11... | collective-permute-start | bytes 196616 | tf_op jit(solution)/shard_map/ppermute | solution.py:493

commit v10 on v9

--- a/solution.py
+++ b/solution.py
@@ -514,9 +514,9 @@
     heads = side(place, tiles, beta_turned, w_query, w_keys, w_values)
     pieces, group_frames, heads = lax.optimization_barrier((pieces, group_frames, heads))
     sums = weigh(place, pieces, group_frames)
-    shared = heads[0]
-    for i in range(1, PARTS):
-        shared = shared + shift(heads[i], "y", i)
+    shared = heads[0] + shift(heads[1], "y", 1) + shift(heads[2], "y", 2)
+    shared, last = lax.optimization_barrier((shared, heads[3]))
+    shared = shared + shift(last, "y", 3)
     part = jnp.sum(trade(sums, "zl"), axis=0)
     part, extra = part[:320], part[320:]
     part = jnp.concatenate(

time: 198 us -> 204 us (1.030)
  blocking collectives: 126 us -> 133 us
    all_to_all x4, waiting for transfers between devices: 20.8 us -> 14.5 us  [trade(): return lax.all_to_all(a, axis, 0, 0, tiled=True)]
    all_to_all x1, blocking collectives: 21.9 us -> 28.1 us  [spread(): lax.all_to_all(jnp.broadcast_to(a[None], (PARTS, *a.shape)), axis, 0, 0,...]
    ppermute x4, waiting for transfers between devices: 0.01 us -> 5.42 us  [shift(): return lax.ppermute(a, axis, [(i, (i + steps) % size) for i in range(size)])]
  transfers between devices with their start and end apart: 8 -> 8, of which waited for: 3 -> 4; matrix products, arithmetic and copies ran while one was open for 0% -> 0% of each run, Pallas kernels for 4% -> 4%
where the time goes in v10:
time: 204 us; the launch traced here: 203 us
  blocking collectives  133 us (65%)
  starting transfers between devices  28.3 us (14%)
  waiting for transfers between devices  19.9 us (10%)
  Pallas kernels  19.3 us (9%)
    all_gather x1, blocking collectives, local(): part = lax.all_gather(part, ('zh', 'zl')).reshape(1280, DH)  31.5 us
    all_to_all x1, blocking collectives, spread(): lax.all_to_all(jnp.broadcast_to(a[None], (PARTS, *a.shape)), axis, 0, 0,...  28.1 us
    all_gather x1, blocking collectives, local(): far = lax.all_gather(total, 'zh')  25.3 us
    all_gather x1, blocking collectives, local(): lax.all_gather(total, 'zl')  20.3 us
    all_to_all x4, starting transfers between devices, trade(): return lax.all_to_all(a, axis, 0, 0, tiled=True)  17.1 us
    all_to_all x4, waiting for transfers between devices, trade(): return lax.all_to_all(a, axis, 0, 0, tiled=True)  14.5 us
    all_gather x1, blocking collectives, local(): lax.all_gather(own, 'x')  13.9 us
    all_gather x1, blocking collectives, local(): far = lax.all_gather(far, 'x')  13.5 us
  transfers between devices with their start and end apart: 8, of which 4 were waited for; matrix products, arithmetic and copies ran while one was open for 0% of the time, Pallas kernels for 4%

profile of v10, /device:TPU:24, one launch (start us, length us, event | category | flops | bytes accessed | tf_op | source)
XLA Modules:
  0.0 203.5 jit_solution(5496561353635335162)
XLA Ops:
  0.6 6.9 %prepare.1 = (f32[3,128,128]{2,1,0:T(8,128)}, f32[3328,128]{1,0:T(8,128)}, f32[4,128,1024]{2,1,0:T(8,128)}) custom-call(f32[2]{0:T(128)} %bias_ref.1, bf16[2,1024]{1,0:T(2,128)(2,1)} %bitcast.32, bf16[128,1024]{1,0:T(8,128)(2,1)} %frames_any.1, bf16[1024,256]{1,0:T(8,128)(2,1)} %wk_ref.1, bf16[1024,128]{1,0:T(8,128)(2,1)} %wq_ref.1, ...), custom_call_target="tpu_custom_call" | custom-call | tf_op jit(solution)/shard_map/prepare/pallas_call | solution.py:330
  7.5 13.9 %all-gather = f32[12,128,128]{2,1,0:T(8,128)S(1)} all-gather(f32[3,128,128]{2,1,0:T(8,128)} %get-tuple-element.40), channel_id=2, replica_groups=mesh['zh'=4,'zl'=4,'x'=4,'y'=4,'core'=2] {'x'}, dimensions={0}, use_global_device_ids=true | all-gather | bytes 983040 | tf_op jit(solution)/shard_map/all_gather | solution.py:505
  21.4 4.6 %all-to-all-start.1 = ((f32[4,128,1024]{2,1,0:T(8,128)}), f32[4,128,1024]{2,1,0:T(8,128)}, u32[]{:S(2)}, u32[]{:S(2)}) async-start(f32[4,128,1024]{2,1,0:T(8,128)} %get-tuple-element.50), calls=%async_computation.1 | async-start | bytes 4194304 | tf_op jit(solution)/shard_map/all_to_all | solution.py:488
  26.0 0.1 stack.23.place_ref
  26.1 1.3 group_scan.2
  27.4 20.3 %all-gather.1 = f32[12,128,128]{2,1,0:T(8,128)S(1)} all-gather(f32[3,128,128]{2,1,0:T(8,128)S(1)} %get-tuple-element.44), channel_id=3, replica_groups=mesh['zh'=4,'zl'=4,'x'=4,'y'=4,'core'=2] {'zl'}, dimensions={0}, use_global_device_ids=true | all-gather | bytes 983040 | tf_op jit(solution)/shard_map/all_gather | solution.py:508
  47.7 1.3 group_scan.3
  49.0 25.3 %all-gather.2 = f32[12,32,128]{2,1,0:T(8,128)S(1)} all-gather(f32[3,32,128]{2,1,0:T(8,128)S(1)} %get-tuple-element.46), channel_id=4, replica_groups=mesh['zh'=4,'zl'=4,'x'=4,'y'=4,'core'=2] {'zh'}, dimensions={0}, use_global_device_ids=true | all-gather | bytes 245760 | tf_op jit(solution)/shard_map/all_gather | solution.py:509
  74.3 0.0 copy-start.3
  74.4 13.5 %all-gather.3 = f32[32,32,128]{2,1,0:T(8,128)S(1)} all-gather(f32[8,32,128]{2,1,0:T(8,128)S(1)} %pad_maximum_fusion.2), channel_id=5, replica_groups=mesh['zh'=4,'zl'=4,'x'=4,'y'=4,'core'=2] {'x'}, dimensions={0}, use_global_device_ids=true | all-gather | bytes 655360 | tf_op jit(solution)/shard_map/all_gather | solution.py:511
  87.9 3.3 %finish.1 = (bf16[128,128]{1,0:T(8,128)(2,1)}, f32[4,264,128]{2,1,0:T(8,128)}, bf16[128,768]{1,0:T(8,128)(2,1)S(1)}) custom-call(s32[5]{0:T(128)S(1)} %stack.23.place_ref, f32[4,8,32,128]{3,2,1,0:T(8,128)S(1)} %bitcast.31, f32[3328,128]{1,0:T(8,128)S(1)} %get-tuple-element.47.kept_ref), custom_call_target="tpu_custom_call" | custom-call | tf_op jit(solution)/shard_map/finish/pallas_call | solution.py:345
  91.2 4.2 %all-to-all-start = ((f32[4,264,128]{2,1,0:T(8,128)}), f32[4,264,128]{2,1,0:T(8,128)S(1)}, u32[]{:S(2)}, u32[]{:S(2)}) async-start(f32[4,264,128]{2,1,0:T(8,128)} %get-tuple-element.49), calls=%async_computation | async-start | bytes 1081344 | tf_op jit(solution)/shard_map/all_to_all | solution.py:488
  95.4 1.2 side.1
  96.6 0.6 copy-done.5
  97.3 0.7 copy-done.7
  98.0 1.7 narrow.1.frames_ref
  99.7 3.9 %all-to-all-done.pieces_ref = f32[4,264,128]{2,1,0:T(8,128)S(1)} async-done(((f32[4,264,128]{2,1,0:T(8,128)}), f32[4,264,128]{2,1,0:T(8,128)S(1)}, u32[]{:S(2)}, u32[]{:S(2)}) %all-to-all-start) | async-done | bytes 540704 | tf_op jit(solution)/shard_map/all_to_all | solution.py:488
  103.6 2.0 weigh.1
  105.5 3.5 %all-to-all-start.2 = ((f32[4,328,128]{2,1,0:T(8,128)}), f32[4,328,128]{2,1,0:T(8,128)S(1)}, u32[]{:S(2)}, u32[]{:S(2)}) async-start(f32[4,328,128]{2,1,0:T(8,128)} %weigh.1), calls=%async_computation.2 | async-start | bytes 1343488 | tf_op jit(solution)/shard_map/all_to_all | solution.py:488
  109.0 2.0 collective-permute-start
  111.1 4.6 %collective-permute-start.1 = (f32[2,128,128]{2,1,0:T(8,128)S(1)}, f32[2,128,128]{2,1,0:T(8,128)S(1)}, u32[]{:S(2)}, u32[]{:S(2)}) collective-permute-start(f32[2,128,128]{2,1,0:T(8,128)S(1)} %copy-done.6), channel_id=1, source_target_pairs={{0,4},{2,6},{4,0},{6,2},{1,5},{3,7},{5,1},{7,3},{8,12},{10,14},{12... | collective-permute-start | bytes 393224 | tf_op jit(solution)/shard_map/ppermute | solution.py:493
  115.7 7.2 %all-to-all-done.2 = f32[4,328,128]{2,1,0:T(8,128)S(1)} async-done(((f32[4,328,128]{2,1,0:T(8,128)}), f32[4,328,128]{2,1,0:T(8,128)S(1)}, u32[]{:S(2)}, u32[]{:S(2)}) %all-to-all-start.2) | async-done | bytes 671776 | tf_op jit(solution)/shard_map/all_to_all | solution.py:488
  123.0 0.7 pad_maximum_fusion.1
  123.7 4.9 %all-to-all-start.3 = ((f32[4,88,128]{2,1,0:T(8,128)}), f32[4,88,128]{2,1,0:T(8,128)S(1)}, u32[]{:S(2)}, u32[]{:S(2)}) async-start(f32[4,88,128]{2,1,0:T(8,128)} %pad_maximum_fusion.1), calls=%async_computation.3 | async-start | bytes 360448 | tf_op jit(solution)/shard_map/all_to_all | solution.py:488
  128.6 2.7 %collective-permute-start.2 = (f32[2,128,128]{2,1,0:T(8,128)S(1)}, f32[2,128,128]{2,1,0:T(8,128)S(1)}, u32[]{:S(2)}, u32[]{:S(2)}) collective-permute-start(f32[2,128,128]{2,1,0:T(8,128)S(1)} %get-tuple-element.63), channel_id=1, source_target_pairs={{0,6},{2,0},{4,2},{6,4},{1,7},{3,1},{5,3},{7,5},{8,14},{10,8},{12,... | collective-permute-start | bytes 393224 | tf_op jit(solution)/shard_map/ppermute | solution.py:493
  131.2 5.4 %collective-permute-done.2 = f32[2,128,128]{2,1,0:T(8,128)S(1)} collective-permute-done((f32[2,128,128]{2,1,0:T(8,128)S(1)}, f32[2,128,128]{2,1,0:T(8,128)S(1)}, u32[]{:S(2)}, u32[]{:S(2)}) %collective-permute-start.2) | collective-permute-done | bytes 131104 | tf_op jit(solution)/shard_map/ppermute | solution.py:493
  136.7 1.9 collective-permute-start.3
  138.6 3.4 %all-to-all-done.3 = f32[4,88,128]{2,1,0:T(8,128)S(1)} async-done(((f32[4,88,128]{2,1,0:T(8,128)}), f32[4,88,128]{2,1,0:T(8,128)S(1)}, u32[]{:S(2)}, u32[]{:S(2)}) %all-to-all-start.3) | async-done | bytes 180256 | tf_op jit(solution)/shard_map/all_to_all | solution.py:488
  142.0 31.5 %all-gather.4 = f32[1280,128]{1,0:T(8,128)S(1)} all-gather(f32[80,128]{1,0:T(8,128)S(1)} %slice.41), channel_id=6, replica_groups=mesh['zh'=4,'zl'=4,'x'=4,'y'=4,'core'=2] {'zh','zl'}, dimensions={0}, use_global_device_ids=true | all-gather | bytes 696320 | tf_op jit(solution)/shard_map/all_gather | solution.py:528
  173.6 0.2 broadcast_in_dim.5
  173.8 28.1 %all_to_all.25.whole_ref = f32[4,1288,128]{2,1,0:T(8,128)S(1)} all-to-all(f32[4,1288,128]{2,1,0:T(8,128)S(1)} %broadcast_in_dim.5), channel_id=1, replica_groups=mesh['zh'=4,'zl'=4,'x'=4,'y'=4,'core'=2] {'x'}, dimensions={0} | all-to-all | bytes 5275648 | tf_op jit(solution)/shard_map/all_to_all | solution.py:484
  201.9 1.6 lay.1
  (33 shorter events, 0.2 us)
Async XLA Ops:
  21.4 4.7 %copy-start = (f32[3328,128]{1,0:T(8,128)S(1)}, f32[3328,128]{1,0:T(8,128)}, u32[]{:S(2)}) copy-start(f32[3328,128]{1,0:T(8,128)} %get-tuple-element.43.kept_in) | copy-start | bytes 5111812
  21.4 69.8 %all-to-all-start.1 = ((f32[4,128,1024]{2,1,0:T(8,128)}), f32[4,128,1024]{2,1,0:T(8,128)}, u32[]{:S(2)}, u32[]{:S(2)}) async-start(f32[4,128,1024]{2,1,0:T(8,128)} %get-tuple-element.50), calls=%async_computation.1 | async-start | bytes 4194304 | tf_op jit(solution)/shard_map/all_to_all | solution.py:488
  74.3 21.1 %copy-start.1 = (bf16[1024,256]{1,0:T(8,128)(2,1)S(1)}, bf16[1024,256]{1,0:T(8,128)(2,1)}, u32[]{:S(2)}) copy-start(bf16[1024,256]{1,0:T(8,128)(2,1)} %wk_ref.1) | copy-start | bytes 1572868
  74.3 21.1 %copy-start.2 = (bf16[1024,256]{1,0:T(8,128)(2,1)S(1)}, bf16[1024,256]{1,0:T(8,128)(2,1)}, u32[]{:S(2)}) copy-start(bf16[1024,256]{1,0:T(8,128)(2,1)} %wv_ref.1) | copy-start | bytes 1572868
  74.3 21.1 %copy-start.3 = (bf16[1024,128]{1,0:T(8,128)(2,1)S(1)}, bf16[1024,128]{1,0:T(8,128)(2,1)}, u32[]{:S(2)}) copy-start(bf16[1024,128]{1,0:T(8,128)(2,1)} %wq_ref.1) | copy-start | bytes 786436
  74.3 21.1 %copy-start.4 = (bf16[1024,2]{0,1:T(2,128)(2,1)S(1)}, bf16[1024,2]{0,1:T(2,128)(2,1)}, u32[]{:S(2)}) copy-start(bf16[1024,2]{0,1:T(2,128)(2,1)} %param.11) | copy-start | bytes 12292
  91.2 12.4 %all-to-all-start = ((f32[4,264,128]{2,1,0:T(8,128)}), f32[4,264,128]{2,1,0:T(8,128)S(1)}, u32[]{:S(2)}, u32[]{:S(2)}) async-start(f32[4,264,128]{2,1,0:T(8,128)} %get-tuple-element.49), calls=%async_computation | async-start | bytes 1081344 | tf_op jit(solution)/shard_map/all_to_all | solution.py:488
  96.6 0.7 copy-start.5
  97.3 0.7 copy-start.7
  99.6 9.4 %copy-start.8 = (f32[2,128,128]{2,1,0:T(8,128)S(1)}, f32[2,128,128]{2,1,0:T(8,128)}, u32[]{:S(2)}) copy-start(f32[2,128,128]{2,1,0:T(8,128)} %copy-done.7) | copy-start | bytes 393220
  99.7 11.4 %copy-start.6 = (f32[2,128,128]{2,1,0:T(8,128)S(1)}, f32[2,128,128]{2,1,0:T(8,128)}, u32[]{:S(2)}) copy-start(f32[2,128,128]{2,1,0:T(8,128)} %copy-done.5) | copy-start | bytes 393220
  105.5 17.4 %all-to-all-start.2 = ((f32[4,328,128]{2,1,0:T(8,128)}), f32[4,328,128]{2,1,0:T(8,128)S(1)}, u32[]{:S(2)}, u32[]{:S(2)}) async-start(f32[4,328,128]{2,1,0:T(8,128)} %weigh.1), calls=%async_computation.2 | async-start | bytes 1343488 | tf_op jit(solution)/shard_map/all_to_all | solution.py:488
  109.0 19.5 %collective-permute-start = (f32[2,128,128]{2,1,0:T(8,128)S(1)}, f32[2,128,128]{2,1,0:T(8,128)S(1)}, u32[]{:S(2)}, u32[]{:S(2)}) collective-permute-start(f32[2,128,128]{2,1,0:T(8,128)S(1)} %copy-done.8), channel_id=1, source_target_pairs={{0,2},{2,4},{4,6},{6,0},{1,3},{3,5},{5,7},{7,1},{8,10},{10,12},{12... | collective-permute-start | bytes 393224 | tf_op jit(solution)/shard_map/ppermute | solution.py:493
  111.1 17.5 %collective-permute-start.1 = (f32[2,128,128]{2,1,0:T(8,128)S(1)}, f32[2,128,128]{2,1,0:T(8,128)S(1)}, u32[]{:S(2)}, u32[]{:S(2)}) collective-permute-start(f32[2,128,128]{2,1,0:T(8,128)S(1)} %copy-done.6), channel_id=1, source_target_pairs={{0,4},{2,6},{4,0},{6,2},{1,5},{3,7},{5,1},{7,3},{8,12},{10,14},{12... | collective-permute-start | bytes 393224 | tf_op jit(solution)/shard_map/ppermute | solution.py:493
  123.7 18.3 %all-to-all-start.3 = ((f32[4,88,128]{2,1,0:T(8,128)}), f32[4,88,128]{2,1,0:T(8,128)S(1)}, u32[]{:S(2)}, u32[]{:S(2)}) async-start(f32[4,88,128]{2,1,0:T(8,128)} %pad_maximum_fusion.1), calls=%async_computation.3 | async-start | bytes 360448 | tf_op jit(solution)/shard_map/all_to_all | solution.py:488
  128.6 8.1 %collective-permute-start.2 = (f32[2,128,128]{2,1,0:T(8,128)S(1)}, f32[2,128,128]{2,1,0:T(8,128)S(1)}, u32[]{:S(2)}, u32[]{:S(2)}) collective-permute-start(f32[2,128,128]{2,1,0:T(8,128)S(1)} %get-tuple-element.63), channel_id=1, source_target_pairs={{0,6},{2,0},{4,2},{6,4},{1,7},{3,1},{5,3},{7,5},{8,14},{10,8},{12,... | collective-permute-start | bytes 393224 | tf_op jit(solution)/shard_map/ppermute | solution.py:493
  136.7 36.8 %collective-permute-start.3 = (f32[128,128]{1,0:T(8,128)S(1)}, f32[128,128]{1,0:T(8,128)S(1)}, u32[]{:S(2)}, u32[]{:S(2)}) collective-permute-start(f32[128,128]{1,0:T(8,128)S(1)} %get-tuple-element.75), channel_id=1, source_target_pairs={{0,1},{1,0},{2,3},{3,2},{4,5},{5,4},{6,7},{7,6},{8,9},{9,8},{10,11... | collective-permute-start | bytes 196616 | tf_op jit(solution)/shard_map/ppermute | solution.py:493
